TPU v7x, 32 devices: a whole 2x2x4 slice. The times are simulated.
32 devices in a mesh: dp: 8 (over z, x), tensor: 4 (over y, core).
Axes of the slice: x: 2, y: 2, z: 4, core: 2. Of those that a mesh axis runs over, the one named last changes fastest.
Arguments:
- frames: bfloat16 [16, 1024, 1024], P('dp', 'tensor'), may hold values from -6 to 6
- lengths: int32 [16], P('dp'), may hold values from 128 to 1024, as said below
- codebook: int32 [16], P('dp'), may hold values from 0 to 6
- ln_gain: float32 [2, 1024], replicated, may hold values from 0.5 to 1.5
- ln_bias: float32 [2, 1024], replicated, may hold values from -1.8 to 1.8
- ada_scale: float32 [7, 2, 1024], replicated, may hold values from 0.25 to 1.75
- ada_shift: float32 [7, 2, 1024], replicated, may hold values from -1.8 to 1.8
- w_qkv: bfloat16 [2, 1024, 3, 1024], P(None, None, None, 'tensor'), may hold values from -0.1875 to 0.1875
- w_out: bfloat16 [2, 1024, 1024], P(None, 'tensor'), may hold values from -0.75 to 0.75
- w_up: bfloat16 [2, 1024, 4096], P(None, None, 'tensor'), may hold values from -0.1875 to 0.1875
- w_down: bfloat16 [2, 4096, 1024], P(None, 'tensor'), may hold values from -0.09375 to 0.09375
- out_grad: bfloat16 [16, 1024, 1024], P('dp', 'tensor'), may hold values from -6 to 6
Outputs:
- hidden_out: bfloat16 [16, 1024, 1024], P('dp', 'tensor')
- frames_grad: float32 [16, 1024, 1024], P('dp', 'tensor')
- grad_ln_gain: float32 [2, 1024], replicated
- grad_ln_bias: float32 [2, 1024], replicated
- grad_ada_scale: float32 [7, 2, 1024], replicated
- grad_ada_shift: float32 [7, 2, 1024], replicated
- grad_w_qkv: float32 [2, 1024, 3, 1024], P(None, None, None, 'tensor')
- grad_w_out: float32 [2, 1024, 1024], P(None, 'tensor')
- grad_w_up: float32 [2, 1024, 4096], P(None, None, 'tensor')
- grad_w_down: float32 [2, 4096, 1024], P(None, 'tensor')
Inputs may be any that keep to these rules, and one draw needn't show every extreme that they name: `lengths`: in every run of 2 consecutive utterances that starts at a multiple of 2, one utterance has length 1024.
All inputs are finite; a program needn't handle non-finite values.
Results may differ from a plain program's by a relative error of at most 0.02.
Values may be sent and summed in bfloat16 or wider, within the bound.
A program may use at most 320 MiB of HBM per device.

v0:
```python
import jax
import jax.numpy as jnp
from jax import lax
from jax.sharding import PartitionSpec as P

HEAD_DIM = 64


def normalize(states):
    average = jnp.mean(states, axis=-1, keepdims=True)
    centred = states - average
    variance = jnp.mean(centred * centred, axis=-1, keepdims=True)
    inverse = lax.rsqrt(variance + 1e-05)
    return (centred * inverse, inverse)


def norm_backward(normed, inverse, grad_normed):
    mean_grad = jnp.mean(grad_normed, axis=-1, keepdims=True)
    mean_proj = jnp.mean(grad_normed * normed, axis=-1, keepdims=True)
    return inverse * (grad_normed - mean_grad - normed * mean_proj)


def gelu_slope(hidden):
    normal_cdf = 0.5 * (1.0 + jax.scipy.special.erf(hidden * 0.7071067811865476))
    density = jnp.exp(-0.5 * hidden * hidden) * 0.3989422804014327
    return normal_cdf + hidden * density


def contract_rows(left, right):
    return lax.dot_general(
        left, right, (((0,), (0,)), ((), ())), preferred_element_type=jnp.float32
    )


def contract_cols(left, right):
    return lax.dot_general(
        left, right, (((1,), (1,)), ((), ())), preferred_element_type=jnp.float32
    )


def gather_rows(entering, weight):

    def project(piece_rows, first_row):
        return (piece_rows, jnp.dot(piece_rows, weight, preferred_element_type=jnp.float32))

    return project(lax.all_gather(entering, "tensor", axis=0, tiled=True), jnp.int32(0))


def scatter_rows(operand, weight, row_count):

    def partial_sum(first_row, row_span):
        return jnp.dot(operand, weight, preferred_element_type=jnp.float32)

    return lax.psum_scatter(
        partial_sum(jnp.int32(0), row_count * lax.axis_size("tensor")).astype(jnp.bfloat16),
        "tensor",
        scatter_dimension=0,
        tiled=True,
    ).astype(jnp.float32)


def gather_grads(grad_rows, weight):

    def project(piece_rows, first_row):
        return (piece_rows, contract_cols(piece_rows, weight))

    return project(lax.all_gather(grad_rows, "tensor", axis=0, tiled=True), jnp.int32(0))


def scatter_grads(operand, weight, row_count):

    def partial_sum(first_row, row_span):
        return contract_cols(operand, weight)

    return lax.psum_scatter(
        partial_sum(jnp.int32(0), row_count * lax.axis_size("tensor")).astype(jnp.bfloat16),
        "tensor",
        scatter_dimension=0,
        tiled=True,
    ).astype(jnp.float32)


def masked_scores(query_rows, keys, first_row, key_valid, causal, scaling):
    scores = (
        jnp.einsum("qhe,khe->hqk", query_rows, keys, preferred_element_type=jnp.float32) * scaling
    )
    allowed = key_valid[None, None, :]
    if causal:
        query_pos = first_row + jnp.arange(query_rows.shape[0])
        key_pos = jnp.arange(keys.shape[0])
        allowed = allowed & (key_pos[None, None, :] <= query_pos[None, :, None])
    return jnp.where(allowed, scores, -1e30)


def attention_forward(queries, keys, values, key_valid, causal, scaling):
    length = queries.shape[0]
    block_rows = min(512, length)
    outputs = []
    logsums = []
    for block_index in range(length // block_rows):
        first_row = block_index * block_rows
        scores = masked_scores(
            queries[first_row : first_row + block_rows], keys, first_row, key_valid, causal, scaling
        )
        row_max = jnp.max(scores, axis=-1, keepdims=True)
        logsum = row_max + jnp.log(jnp.sum(jnp.exp(scores - row_max), axis=-1, keepdims=True))
        weights = jnp.exp(scores - logsum).astype(jnp.bfloat16)
        mixed_rows = jnp.einsum("hqk,khe->qhe", weights, values, preferred_element_type=jnp.float32)
        outputs.append(mixed_rows.reshape(block_rows, -1).astype(jnp.bfloat16))
        logsums.append(logsum[:, :, 0])
    return (jnp.concatenate(outputs, axis=0), jnp.concatenate(logsums, axis=1))


def attention_backward(queries, keys, values, logsums, grad_mixed, key_valid, causal, scaling):
    length = queries.shape[0]
    block_rows = min(512, length)
    grad_heads = grad_mixed.reshape(queries.shape)
    grad_keys = jnp.zeros(keys.shape, jnp.float32)
    grad_values = jnp.zeros(values.shape, jnp.float32)
    query_grads = []
    for block_index in range(length // block_rows):
        first_row = block_index * block_rows
        query_rows = queries[first_row : first_row + block_rows]
        grad_rows = grad_heads[first_row : first_row + block_rows]
        scores = masked_scores(query_rows, keys, first_row, key_valid, causal, scaling)
        row_probs = jnp.exp(scores - logsums[:, first_row : first_row + block_rows, None])
        grad_probs = jnp.einsum(
            "qhe,khe->hqk", grad_rows, values, preferred_element_type=jnp.float32
        )
        grad_values = grad_values + jnp.einsum(
            "hqk,qhe->khe",
            row_probs.astype(jnp.bfloat16),
            grad_rows,
            preferred_element_type=jnp.float32,
        )
        grad_scores = row_probs * (
            grad_probs - jnp.sum(row_probs * grad_probs, axis=-1, keepdims=True)
        )
        grad_scores = grad_scores.astype(jnp.bfloat16)
        query_grads.append(
            jnp.einsum("hqk,khe->qhe", grad_scores, keys, preferred_element_type=jnp.float32)
            * scaling
        )
        grad_keys = (
            grad_keys
            + jnp.einsum(
                "hqk,qhe->khe", grad_scores, query_rows, preferred_element_type=jnp.float32
            )
            * scaling
        )
    grad_queries = jnp.concatenate(query_grads, axis=0)
    stacked = jnp.stack([grad_queries, grad_keys, grad_values], axis=1).astype(jnp.bfloat16)
    return stacked.reshape(length, -1)


def layer_forward(
    states,
    layer_gains,
    layer_shifts,
    qkv_weight,
    out_weight,
    up_weight,
    down_weight,
    key_valid,
    causal,
    scaling,
):
    row_count = states.shape[0]
    normed_att, inverse_att = normalize(states)
    entering = (normed_att * layer_gains[0] + layer_shifts[0]).astype(jnp.bfloat16)
    qkv_flat = qkv_weight.reshape(qkv_weight.shape[0], -1)
    gathered_att, projected = gather_rows(entering, qkv_flat)
    length = gathered_att.shape[0]
    split_heads = projected.astype(jnp.bfloat16).reshape(length, 3, -1, HEAD_DIM)
    attended, logsums = attention_forward(
        split_heads[:, 0], split_heads[:, 1], split_heads[:, 2], key_valid, causal, scaling
    )
    middle = states + scatter_rows(attended, out_weight, row_count)
    normed_ffn, inverse_ffn = normalize(middle)
    entering_ffn = (normed_ffn * layer_gains[1] + layer_shifts[1]).astype(jnp.bfloat16)
    gathered_ffn, hidden = gather_rows(entering_ffn, up_weight)
    active = jax.nn.gelu(hidden, approximate=False).astype(jnp.bfloat16)
    result = middle + scatter_rows(active, down_weight, row_count)
    return (
        result,
        (
            normed_att,
            inverse_att,
            gathered_att,
            split_heads,
            attended,
            logsums,
            normed_ffn,
            inverse_ffn,
            gathered_ffn,
            hidden,
            active,
        ),
    )


def layer_backward(
    grad_states,
    saved_layer,
    layer_gains,
    qkv_weight,
    out_weight,
    up_weight,
    down_weight,
    key_valid,
    causal,
    scaling,
):
    (
        normed_att,
        inverse_att,
        gathered_att,
        split_heads,
        attended,
        logsums,
        normed_ffn,
        inverse_ffn,
        gathered_ffn,
        hidden,
        active,
    ) = saved_layer
    row_count = normed_att.shape[0]
    gathered_grad, grad_active = gather_grads(grad_states.astype(jnp.bfloat16), down_weight)
    grad_down = contract_rows(active, gathered_grad)
    grad_hidden = (grad_active * gelu_slope(hidden)).astype(jnp.bfloat16)
    grad_up = contract_rows(gathered_ffn, grad_hidden)
    grad_entering = scatter_grads(grad_hidden, up_weight, row_count)
    gain_ffn = jnp.sum(grad_entering * normed_ffn, axis=0)
    shift_ffn = jnp.sum(grad_entering, axis=0)
    grad_middle = grad_states + norm_backward(
        normed_ffn, inverse_ffn, grad_entering * layer_gains[1]
    )
    gathered_grad, grad_attended = gather_grads(grad_middle.astype(jnp.bfloat16), out_weight)
    grad_out = contract_rows(attended, gathered_grad)
    grad_projected = attention_backward(
        split_heads[:, 0],
        split_heads[:, 1],
        split_heads[:, 2],
        logsums,
        grad_attended.astype(jnp.bfloat16),
        key_valid,
        causal,
        scaling,
    )
    qkv_flat = qkv_weight.reshape(qkv_weight.shape[0], -1)
    grad_qkv = contract_rows(gathered_att, grad_projected).reshape(qkv_weight.shape)
    grad_entering = scatter_grads(grad_projected, qkv_flat, row_count)
    gain_att = jnp.sum(grad_entering * normed_att, axis=0)
    shift_att = jnp.sum(grad_entering, axis=0)
    grad_input = grad_middle + norm_backward(
        normed_att, inverse_att, grad_entering * layer_gains[0]
    )
    return (
        grad_input,
        (grad_qkv, grad_out, grad_up, grad_down),
        jnp.stack([gain_att, gain_ffn]),
        jnp.stack([shift_att, shift_ffn]),
    )


def per_device(
    frames,
    lengths,
    codebook,
    ln_gain,
    ln_bias,
    ada_scale,
    ada_shift,
    w_qkv,
    w_out,
    w_up,
    w_down,
    out_grad,
):
    micro_count = frames.shape[0]
    row_count = frames.shape[1]
    length = row_count * lax.axis_size("tensor")
    scaling = HEAD_DIM ** (-0.5)
    key_pos = jnp.arange(length)
    section_ids = jnp.arange(ada_scale.shape[0])
    qkv_sums = [jnp.zeros(w_qkv.shape[1:], jnp.float32) for layer_index in range(2)]
    out_sums = [jnp.zeros(w_out.shape[1:], jnp.float32) for layer_index in range(2)]
    up_sums = [jnp.zeros(w_up.shape[1:], jnp.float32) for layer_index in range(2)]
    down_sums = [jnp.zeros(w_down.shape[1:], jnp.float32) for layer_index in range(2)]
    gain_sum = jnp.zeros(ln_gain.shape, jnp.float32)
    bias_sum = jnp.zeros(ln_bias.shape, jnp.float32)
    scale_sum = jnp.zeros(ada_scale.shape, jnp.float32)
    shift_sum = jnp.zeros(ada_shift.shape, jnp.float32)
    outputs = []
    frame_grads = []
    for step_index in range(micro_count):
        key_valid = key_pos < lengths[step_index]
        section_match = (section_ids == codebook[step_index])[:, None, None]
        layer_gains = (ln_gain, jnp.sum(jnp.where(section_match, ada_scale, 0.0), axis=0))
        layer_shifts = (ln_bias, jnp.sum(jnp.where(section_match, ada_shift, 0.0), axis=0))
        states = frames[step_index].astype(jnp.float32)
        kept_layers = []
        for layer_index in range(2):
            states, saved_layer = layer_forward(
                states,
                layer_gains[layer_index],
                layer_shifts[layer_index],
                w_qkv[layer_index],
                w_out[layer_index],
                w_up[layer_index],
                w_down[layer_index],
                key_valid,
                layer_index == 0,
                scaling,
            )
            kept_layers.append(saved_layer)
        outputs.append(states.astype(jnp.bfloat16))
        grad_states = out_grad[step_index].astype(jnp.float32)
        for layer_index in (1, 0):
            grad_states, weight_grads, gain_grad, shift_grad = layer_backward(
                grad_states,
                kept_layers[layer_index],
                layer_gains[layer_index],
                w_qkv[layer_index],
                w_out[layer_index],
                w_up[layer_index],
                w_down[layer_index],
                key_valid,
                layer_index == 0,
                scaling,
            )
            qkv_sums[layer_index] = qkv_sums[layer_index] + weight_grads[0]
            out_sums[layer_index] = out_sums[layer_index] + weight_grads[1]
            up_sums[layer_index] = up_sums[layer_index] + weight_grads[2]
            down_sums[layer_index] = down_sums[layer_index] + weight_grads[3]
            if layer_index == 1:
                scale_sum = scale_sum + jnp.where(section_match, gain_grad[None], 0.0)
                shift_sum = shift_sum + jnp.where(section_match, shift_grad[None], 0.0)
            else:
                gain_sum = gain_sum + gain_grad
                bias_sum = bias_sum + shift_grad
        frame_grads.append(grad_states)
    norm_total = (
        lax.psum(gain_sum.astype(jnp.bfloat16), "tensor").astype(jnp.float32),
        lax.psum(bias_sum.astype(jnp.bfloat16), "tensor").astype(jnp.float32),
        lax.psum(scale_sum.astype(jnp.bfloat16), "tensor").astype(jnp.float32),
        lax.psum(shift_sum.astype(jnp.bfloat16), "tensor").astype(jnp.float32),
    )
    qkv_share, out_share, up_share, down_share, gain_share, bias_share, scale_share, shift_share = (
        lax.psum_scatter(jnp.stack(qkv_sums), "dp", scatter_dimension=1, tiled=True),
        lax.psum_scatter(jnp.stack(out_sums), "dp", scatter_dimension=2, tiled=True),
        lax.psum_scatter(jnp.stack(up_sums), "dp", scatter_dimension=1, tiled=True),
        lax.psum_scatter(jnp.stack(down_sums), "dp", scatter_dimension=2, tiled=True),
        lax.psum_scatter(norm_total[0], "dp", scatter_dimension=1, tiled=True),
        lax.psum_scatter(norm_total[1], "dp", scatter_dimension=1, tiled=True),
        lax.psum_scatter(norm_total[2], "dp", scatter_dimension=2, tiled=True),
        lax.psum_scatter(norm_total[3], "dp", scatter_dimension=2, tiled=True),
    )
    gathered_grads = (
        lax.all_gather(qkv_share.astype(jnp.bfloat16), "dp", axis=1, tiled=True).astype(
            qkv_share.dtype
        ),
        lax.all_gather(out_share.astype(jnp.bfloat16), "dp", axis=2, tiled=True).astype(
            out_share.dtype
        ),
        lax.all_gather(up_share.astype(jnp.bfloat16), "dp", axis=1, tiled=True).astype(
            up_share.dtype
        ),
        lax.all_gather(down_share.astype(jnp.bfloat16), "dp", axis=2, tiled=True).astype(
            down_share.dtype
        ),
        lax.all_gather(gain_share.astype(jnp.bfloat16), "dp", axis=1, tiled=True).astype(
            gain_share.dtype
        ),
        lax.all_gather(bias_share.astype(jnp.bfloat16), "dp", axis=1, tiled=True).astype(
            bias_share.dtype
        ),
        lax.all_gather(scale_share.astype(jnp.bfloat16), "dp", axis=2, tiled=True).astype(
            scale_share.dtype
        ),
        lax.all_gather(shift_share.astype(jnp.bfloat16), "dp", axis=2, tiled=True).astype(
            shift_share.dtype
        ),
    )
    return (
        jnp.stack(outputs),
        jnp.stack(frame_grads),
        gathered_grads[4],
        gathered_grads[5],
        gathered_grads[6],
        gathered_grads[7],
        gathered_grads[0],
        gathered_grads[1],
        gathered_grads[2],
        gathered_grads[3],
    )


def solution(mesh):
    placed = (
        P("dp", "tensor", None),
        P("dp"),
        P("dp"),
        P(),
        P(),
        P(),
        P(),
        P(None, None, None, "tensor"),
        P(None, "tensor", None),
        P(None, None, "tensor"),
        P(None, "tensor", None),
        P("dp", "tensor", None),
    )
    return jax.shard_map(
        per_device,
        mesh=mesh,
        in_specs=placed,
        out_specs=(
            P("dp", "tensor", None),
            P("dp", "tensor", None),
            P(),
            P(),
            P(),
            P(),
            P(None, None, None, "tensor"),
            P(None, "tensor", None),
            P(None, None, "tensor"),
            P(None, "tensor", None),
        ),
        check_vma=False,
    )
```

profile of v0, /device:TPU:0, one launch (start us, length us, event | category | flops | bytes accessed | tf_op | source)
XLA Modules:
  0.0 2127.8 jit_solution(2120660243886795529)
XLA Ops:
  60.9 31.5 %reduce-scatter.33.cloned.1.call-done = bf16[256,1024]{1,0:T(8,128)(2,1)} async-done(((bf16[1024,1024]{1,0:T(8,128)(2,1)}), bf16[256,1024]{1,0:T(8,128)(2,1)}) %reduce-scatter.33.cloned.1.call-update) | async-done | bytes 524304 | tf_op jit(solution)/shard_map/reduce_scatter | solution.py:54
  94.9 22.7 %all-gather.31.cloned.1.call-done = bf16[1024,1024]{1,0:T(8,128)(2,1)} async-done(((bf16[256,1024]{1,0:T(8,128)(2,1)}), bf16[1024,1024]{1,0:T(8,128)(2,1)}) %all-gather.31.cloned.1.call-update) | async-done | bytes 2097168 | tf_op jit(solution)/shard_map/all_gather | solution.py:46
  139.9 31.5 %reduce-scatter.41.cloned.1.call-done = bf16[256,1024]{1,0:T(8,128)(2,1)} async-done(((bf16[1024,1024]{1,0:T(8,128)(2,1)}), bf16[256,1024]{1,0:T(8,128)(2,1)}) %reduce-scatter.41.cloned.1.call-update) | async-done | bytes 524304 | tf_op jit(solution)/shard_map/reduce_scatter | solution.py:54
  177.5 22.1 %all-gather.33.cloned.1.call-done = bf16[1024,1024]{1,0:T(8,128)(2,1)} async-done(((bf16[256,1024]{1,0:T(8,128)(2,1)}), bf16[1024,1024]{1,0:T(8,128)(2,1)}) %all-gather.33.cloned.1.call-update) | async-done | bytes 2097168 | tf_op jit(solution)/shard_map/all_gather | solution.py:46
  258.7 34.7 %reduce-scatter.35.cloned.1.call-done = bf16[256,1024]{1,0:T(8,128)(2,1)} async-done(((bf16[1024,1024]{1,0:T(8,128)(2,1)}), bf16[256,1024]{1,0:T(8,128)(2,1)}) %reduce-scatter.35.cloned.1.call-update) | async-done | bytes 524304 | tf_op jit(solution)/shard_map/reduce_scatter | solution.py:54
  383.8 29.7 %reduce-scatter.37.cloned.1.call-done = bf16[256,1024]{1,0:T(8,128)(2,1)} async-done(((bf16[1024,1024]{1,0:T(8,128)(2,1)}), bf16[256,1024]{1,0:T(8,128)(2,1)}) %reduce-scatter.37.cloned.1.call-update) | async-done | bytes 524304 | tf_op jit(solution)/shard_map/reduce_scatter | solution.py:54
  416.9 20.8 all-gather.37.cloned.1.call-done
  546.9 32.4 %reduce-scatter.49.cloned.1.call-done = bf16[256,1024]{1,0:T(8,128)(2,1)} async-done(((bf16[1024,1024]{1,0:T(8,128)(2,1)}), bf16[256,1024]{1,0:T(8,128)(2,1)}) %reduce-scatter.49.cloned.1.call-update) | async-done | bytes 524304 | tf_op jit(solution)/shard_map/reduce_scatter | solution.py:75
  581.5 31.8 %reduce-scatter.47.cloned.1.call-done = bf16[256,1024]{1,0:T(8,128)(2,1)} async-done(((bf16[1024,1024]{1,0:T(8,128)(2,1)}), bf16[256,1024]{1,0:T(8,128)(2,1)}) %reduce-scatter.47.cloned.1.call-update) | async-done | bytes 524304 | tf_op jit(solution)/shard_map/reduce_scatter | solution.py:54
  613.3 34.0 %reduce-scatter.39.cloned.1.call-done = bf16[256,1024]{1,0:T(8,128)(2,1)} async-done(((bf16[1024,1024]{1,0:T(8,128)(2,1)}), bf16[256,1024]{1,0:T(8,128)(2,1)}) %reduce-scatter.39.cloned.1.call-update) | async-done | bytes 524304 | tf_op jit(solution)/shard_map/reduce_scatter | solution.py:54
  651.7 22.0 %all-gather.39.cloned.1.call-done = bf16[1024,1024]{1,0:T(8,128)(2,1)} async-done(((bf16[256,1024]{1,0:T(8,128)(2,1)}), bf16[1024,1024]{1,0:T(8,128)(2,1)}) %all-gather.39.cloned.1.call-update) | async-done | bytes 2097168 | tf_op jit(solution)/shard_map/all_gather | solution.py:67
  773.9 26.8 %reduce-scatter.59.cloned.1.call-done = bf16[256,1024]{1,0:T(8,128)(2,1)} async-done(((bf16[1024,1024]{1,0:T(8,128)(2,1)}), bf16[256,1024]{1,0:T(8,128)(2,1)}) %reduce-scatter.59.cloned.1.call-update) | async-done | bytes 524304 | tf_op jit(solution)/shard_map/reduce_scatter | solution.py:75
  805.1 20.5 all-gather.41.cloned.1.call-done
  861.6 22.9 %reduce-scatter.53.cloned.1.call-done = bf16[256,1024]{1,0:T(8,128)(2,1)} async-done(((bf16[1024,1024]{1,0:T(8,128)(2,1)}), bf16[256,1024]{1,0:T(8,128)(2,1)}) %reduce-scatter.53.cloned.1.call-update) | async-done | bytes 524304 | tf_op jit(solution)/shard_map/reduce_scatter | solution.py:75
  884.5 34.7 %reduce-scatter.61.cloned.1.call-done = bf16[256,1024]{1,0:T(8,128)(2,1)} async-done(((bf16[1024,1024]{1,0:T(8,128)(2,1)}), bf16[256,1024]{1,0:T(8,128)(2,1)}) %reduce-scatter.61.cloned.1.call-update) | async-done | bytes 524304 | tf_op jit(solution)/shard_map/reduce_scatter | solution.py:75
  926.6 21.9 %all-gather.49.cloned.1.call-done = bf16[1024,1024]{1,0:T(8,128)(2,1)} async-done(((bf16[256,1024]{1,0:T(8,128)(2,1)}), bf16[1024,1024]{1,0:T(8,128)(2,1)}) %all-gather.49.cloned.1.call-update) | async-done | bytes 2097168 | tf_op jit(solution)/shard_map/all_gather | solution.py:67
  1044.4 25.1 %reduce-scatter.55.cloned.1.call-done = bf16[256,1024]{1,0:T(8,128)(2,1)} async-done(((bf16[1024,1024]{1,0:T(8,128)(2,1)}), bf16[256,1024]{1,0:T(8,128)(2,1)}) %reduce-scatter.55.cloned.1.call-update) | async-done | bytes 524304 | tf_op jit(solution)/shard_map/reduce_scatter | solution.py:75
  1140.8 36.2 %reduce-scatter.67.cloned.1.call-done = f32[2,256,128]{2,1,0:T(8,128)} async-done(((f32[2,256,1024]{2,1,0:T(8,128)}), f32[2,256,128]{2,1,0:T(8,128)}) %reduce-scatter.67.cloned.1.call-update) | async-done | bytes 262160 | tf_op jit(solution)/shard_map/reduce_scatter | solution.py:351
  1178.7 151.1 %reduce-scatter.69.cloned.1.call-done = f32[2,128,1024]{2,1,0:T(8,128)} async-done(((f32[2,1024,1024]{2,1,0:T(8,128)}), f32[2,128,1024]{2,1,0:T(8,128)}) %reduce-scatter.69.cloned.1.call-update) | async-done | bytes 1048592 | tf_op jit(solution)/shard_map/reduce_scatter | solution.py:352
  1332.0 150.4 %reduce-scatter.71.cloned.1.call-done = f32[2,1024,128]{2,1,0:T(8,128)} async-done(((f32[2,1024,1024]{2,1,0:T(8,128)}), f32[2,1024,128]{2,1,0:T(8,128)}) %reduce-scatter.71.cloned.1.call-update) | async-done | bytes 1048592 | tf_op jit(solution)/shard_map/reduce_scatter | solution.py:353
  1484.5 119.6 %reduce-scatter.65.cloned.1.call-done = f32[2,128,3,256]{3,1,2,0:T(8,128)} async-done(((f32[2,1024,3,256]{3,1,2,0:T(8,128)}), f32[2,128,3,256]{3,1,2,0:T(8,128)}) %reduce-scatter.65.cloned.1.call-update) | async-done | bytes 786448 | tf_op jit(solution)/shard_map/reduce_scatter | solution.py:350
  1611.8 57.7 %reduce-scatter.73.cloned.1.call-done = f32[128,2]{1,0:T(8,128)} async-done(((f32[1024,2]{1,0:T(8,128)}), f32[128,2]{1,0:T(8,128)}) %reduce-scatter.73.cloned.1.call-update) | async-done | bytes 1040
  1689.6 44.2 %reduce-scatter.75.cloned.1.call-done = f32[128,2]{1,0:T(8,128)} async-done(((f32[1024,2]{1,0:T(8,128)}), f32[128,2]{1,0:T(8,128)}) %reduce-scatter.75.cloned.1.call-update) | async-done | bytes 1040
  1734.6 18.7 all_gather.89
  1753.9 44.5 %reduce-scatter.77.cloned.1.call-done = f32[128,14]{1,0:T(8,128)} async-done(((f32[1024,14]{1,0:T(8,128)}), f32[128,14]{1,0:T(8,128)}) %reduce-scatter.77.cloned.1.call-update) | async-done | bytes 7184
  1799.6 18.7 all_gather.90
  1819.0 43.7 %reduce-scatter.79.cloned.1.call-done = f32[128,14]{1,0:T(8,128)} async-done(((f32[1024,14]{1,0:T(8,128)}), f32[128,14]{1,0:T(8,128)}) %reduce-scatter.79.cloned.1.call-update) | async-done | bytes 7184
  1863.9 18.9 all_gather.91
  1883.4 20.2 all-gather.53.cloned.1.call-done
  1906.4 72.3 %all-gather.55.cloned.1.call-done = bf16[2,1024,1024]{2,1,0:T(8,128)(2,1)} async-done(((bf16[2,128,1024]{2,1,0:T(8,128)(2,1)}), bf16[2,1024,1024]{2,1,0:T(8,128)(2,1)}) %all-gather.55.cloned.1.call-update) | async-done | bytes 4194320 | tf_op jit(solution)/shard_map/all_gather | solution.py:366
  1985.4 68.9 %all-gather.57.cloned.1.call-done = bf16[2,1024,1024]{2,1,0:T(8,128)(2,1)} async-done(((bf16[2,1024,128]{2,1,0:T(8,128)(2,1)}), bf16[2,1024,1024]{2,1,0:T(8,128)(2,1)}) %all-gather.57.cloned.1.call-update) | async-done | bytes 4194320 | tf_op jit(solution)/shard_map/all_gather | solution.py:369
  2060.9 54.9 %all-gather.51.cloned.1.call-done = bf16[2,1024,3,256]{3,1,2,0:T(8,128)(2,1)} async-done(((bf16[2,128,3,256]{3,1,2,0:T(8,128)(2,1)}), bf16[2,1024,3,256]{3,1,2,0:T(8,128)(2,1)}) %all-gather.51.cloned.1.call-update) | async-done | bytes 3145744 | tf_op jit(solution)/shard_map/all_gather | solution.py:360
  (733 shorter events, 725.3 us)
Async XLA Ops:
  13.8 78.6 %reduce-scatter.33.cloned.1.call-start = ((), (), s32[]{:S(2)}) async-start(), calls=%async_computation.25 | async-start | bytes 2621440 | tf_op jit(solution)/shard_map/reduce_scatter | solution.py:54
  94.9 76.5 %reduce-scatter.41.cloned.1.call-start = ((), (), s32[]{:S(2)}) async-start(), calls=%async_computation.33 | async-start | bytes 2621440 | tf_op jit(solution)/shard_map/reduce_scatter | solution.py:54
  177.4 81.3 %reduce-scatter.43.cloned.1.call-start = ((), (), s32[]{:S(2)}) async-start(), calls=%async_computation.35 | async-start | bytes 2621440 | tf_op jit(solution)/shard_map/reduce_scatter | solution.py:54
  243.6 76.1 %all-gather.35.cloned.1.call-start = ((), (), s32[]{:S(2)}) async-start(), calls=%async_computation.36 | async-start | bytes 2621440 | tf_op jit(solution)/shard_map/all_gather | solution.py:46
  301.3 77.6 %reduce-scatter.45.cloned.1.call-start = ((), (), s32[]{:S(2)}) async-start(), calls=%async_computation.37 | async-start | bytes 2621440 | tf_op jit(solution)/shard_map/reduce_scatter | solution.py:54
  381.5 80.2 %all-gather.61.cloned.1.call-start = ((), (), s32[]{:S(2)}) async-start(), calls=%async_computation.63 | async-start | bytes 2621440 | tf_op jit(solution)/shard_map/all_gather | solution.py:67
  383.8 102.5 %all-gather.29.cloned.1.call-start = ((), (), s32[]{:S(2)}) async-start(), calls=%async_computation.30 | async-start | bytes 2621440 | tf_op jit(solution)/shard_map/all_gather | solution.py:46
  416.1 94.9 %all-gather.59.cloned.1.call-start = ((), (), s32[]{:S(2)}) async-start(), calls=%async_computation.62 | async-start | bytes 2621440 | tf_op jit(solution)/shard_map/all_gather | solution.py:67
  416.6 128.1 %reduce-scatter.57.cloned.1.call-start = ((), (), s32[]{:S(2)}) async-start(), calls=%async_computation.47 | async-start | bytes 2621440 | tf_op jit(solution)/shard_map/reduce_scatter | solution.py:75
  473.1 106.2 %reduce-scatter.49.cloned.1.call-start = ((), (), s32[]{:S(2)}) async-start(), calls=%async_computation.40 | async-start | bytes 2621440 | tf_op jit(solution)/shard_map/reduce_scatter | solution.py:75
  522.3 91.0 %reduce-scatter.47.cloned.1.call-start = ((), (), s32[]{:S(2)}) async-start(), calls=%async_computation.39 | async-start | bytes 2621440 | tf_op jit(solution)/shard_map/reduce_scatter | solution.py:54
  528.4 118.9 %reduce-scatter.39.cloned.1.call-start = ((), (), s32[]{:S(2)}) async-start(), calls=%async_computation.31 | async-start | bytes 2621440 | tf_op jit(solution)/shard_map/reduce_scatter | solution.py:54
  534.7 139.0 %all-gather.39.cloned.1.call-start = ((), (), s32[]{:S(2)}) async-start(), calls=%async_computation.41 | async-start | bytes 2621440 | tf_op jit(solution)/shard_map/all_gather | solution.py:67
  651.7 117.4 %reduce-scatter.51.cloned.1.call-start = ((), (), s32[]{:S(2)}) async-start(), calls=%async_computation.42 | async-start | bytes 2621440 | tf_op jit(solution)/shard_map/reduce_scatter | solution.py:75
  773.9 76.3 %all-gather.47.cloned.1.call-start = ((), (), s32[]{:S(2)}) async-start(), calls=%async_computation.50 | async-start | bytes 2621440 | tf_op jit(solution)/shard_map/all_gather | solution.py:67
  805.0 79.5 %reduce-scatter.53.cloned.1.call-start = ((), (), s32[]{:S(2)}) async-start(), calls=%async_computation.44 | async-start | bytes 2621440 | tf_op jit(solution)/shard_map/reduce_scatter | solution.py:75
  836.9 82.4 %reduce-scatter.61.cloned.1.call-start = ((), (), s32[]{:S(2)}) async-start(), calls=%async_computation.51 | async-start | bytes 2621440 | tf_op jit(solution)/shard_map/reduce_scatter | solution.py:75
  861.6 86.9 %all-gather.49.cloned.1.call-start = ((), (), s32[]{:S(2)}) async-start(), calls=%async_computation.52 | async-start | bytes 2621440 | tf_op jit(solution)/shard_map/all_gather | solution.py:67
  926.3 118.0 %reduce-scatter.63.cloned.1.call-start = ((), (), s32[]{:S(2)}) async-start(), calls=%async_computation.53 | async-start | bytes 2621440 | tf_op jit(solution)/shard_map/reduce_scatter | solution.py:75
  1037.3 86.1 %all-reduce.3.cloned.1.call-start = ((), (), s32[]{:S(2)}) async-start(), calls=%async_computation.68 | async-start | bytes 131072 | tf_op jit(solution)/shard_map/psum | solution.py:344
  1073.0 104.1 %reduce-scatter.67.cloned.1.call-start = ((), (), s32[]{:S(2)}) async-start(), calls=%async_computation.56 | async-start | bytes 2359296 | tf_op jit(solution)/shard_map/reduce_scatter | solution.py:351
  1074.5 255.4 %reduce-scatter.69.cloned.1.call-start = ((), (), s32[]{:S(2)}) async-start(), calls=%async_computation.58 | async-start | bytes 9437184 | tf_op jit(solution)/shard_map/reduce_scatter | solution.py:352
  1091.3 391.0 %reduce-scatter.71.cloned.1.call-start = ((), (), s32[]{:S(2)}) async-start(), calls=%async_computation.60 | async-start | bytes 9437184 | tf_op jit(solution)/shard_map/reduce_scatter | solution.py:353
  1108.8 495.4 %reduce-scatter.65.cloned.1.call-start = ((), (), s32[]{:S(2)}) async-start(), calls=%async_computation.54 | async-start | bytes 7077888 | tf_op jit(solution)/shard_map/reduce_scatter | solution.py:350
  1123.3 546.2 %reduce-scatter.73.cloned.1.call-start = ((), (), s32[]{:S(2)}) async-start(), calls=%async_computation.64 | async-start | bytes 589824
  1125.1 608.6 %reduce-scatter.75.cloned.1.call-start = ((), (), s32[]{:S(2)}) async-start(), calls=%async_computation.65 | async-start | bytes 589824
  1126.8 671.6 %reduce-scatter.77.cloned.1.call-start = ((), (), s32[]{:S(2)}) async-start(), calls=%async_computation.66 | async-start | bytes 589824
  1134.2 728.5 %reduce-scatter.79.cloned.1.call-start = ((), (), s32[]{:S(2)}) async-start(), calls=%async_computation.67 | async-start | bytes 589824
  1140.8 762.8 %all-gather.53.cloned.1.call-start = ((), (), s32[]{:S(2)}) async-start(), calls=%async_computation.57 | async-start | bytes 1179648 | tf_op jit(solution)/shard_map/all_gather | solution.py:363
  1178.7 800.1 %all-gather.55.cloned.1.call-start = ((), (), s32[]{:S(2)}) async-start(), calls=%async_computation.59 | async-start | bytes 4718592 | tf_op jit(solution)/shard_map/all_gather | solution.py:366
  1332.0 722.3 %all-gather.57.cloned.1.call-start = ((), (), s32[]{:S(2)}) async-start(), calls=%async_computation.61 | async-start | bytes 4718592 | tf_op jit(solution)/shard_map/all_gather | solution.py:369
  1484.5 631.4 %all-gather.51.cloned.1.call-start = ((), (), s32[]{:S(2)}) async-start(), calls=%async_computation.55 | async-start | bytes 3538944 | tf_op jit(solution)/shard_map/all_gather | solution.py:360
  (201 other events, 4984.3 us)
Sparse Core Ops, SparseCore 0:
  13.9 25.2 all-gather.22
  60.9 31.4 reduce-scatter.32
  139.9 31.4 reduce-scatter.40
  227.3 31.4 reduce-scatter.42
  262.0 31.4 reduce-scatter.34
  347.4 31.4 reduce-scatter.44
  382.0 31.4 reduce-scatter.36
  513.3 31.4 reduce-scatter.56
  547.9 31.3 reduce-scatter.48
  581.8 31.4 reduce-scatter.46
  615.8 31.3 reduce-scatter.38
  730.2 31.4 reduce-scatter.50
  769.0 31.7 reduce-scatter.58
  853.1 31.4 reduce-scatter.52
  887.8 31.3 reduce-scatter.60
  925.9 22.6 all-gather.48
  950.5 22.6 all-gather.42
  996.3 32.0 reduce-scatter.62
  1037.4 32.0 reduce-scatter.54
  1073.1 31.3 all-reduce.2
  1109.0 67.9 reduce-scatter.66
  1181.7 148.1 reduce-scatter.68
  1333.9 148.4 reduce-scatter.70
  1486.8 117.2 reduce-scatter.64
  1608.5 61.0 reduce-scatter.72
  1672.8 60.9 reduce-scatter.74
  1737.5 60.9 reduce-scatter.76
  1801.7 60.8 reduce-scatter.78
  1864.9 38.6 all-gather.52
  1906.4 72.2 all-gather.54
  1981.0 73.2 all-gather.56
  2057.2 58.6 all-gather.50
  (13 shorter events, 292.9 us)
where the time goes:
time: 2140 us; the launch traced here: 2130 us
  waiting for transfers between devices  1460 us (68%)
  matrix products  347 us (16%)
  other arithmetic  156 us (7%)
  blocking collectives  74.7 us (3%)
  local copies, waits for them, and re-layouts  65.7 us (3%)
    reduce_scatter x8, waiting for transfers between devices, scatter_rows(): lax.psum_scatter(partial_sum(jnp.int32(0), row_count * lax.axis_size('ten...  221 us
    unnamed x49, waiting for transfers between devices  193 us
    reduce_scatter x8, waiting for transfers between devices, scatter_grads(): lax.psum_scatter(partial_sum(jnp.int32(0), row_count * lax.axis_size('ten...  152 us
    reduce_scatter x1, waiting for transfers between devices, per_device(): lax.psum_scatter(jnp.stack(up_sums), 'dp', scatter_dimension=1, tiled=True)  151 us
    reduce_scatter x1, waiting for transfers between devices, per_device(): lax.psum_scatter(jnp.stack(down_sums), 'dp', scatter_dimension=2, tiled=T...  150 us
    all_gather x8, waiting for transfers between devices, gather_rows(): lax.all_gather(entering, 'tensor', axis=0, tiled=True)  125 us
    reduce_scatter x1, waiting for transfers between devices, per_device(): lax.psum_scatter(jnp.stack(qkv_sums), 'dp', scatter_dimension=1, tiled=True)  120 us
    all_gather x8, waiting for transfers between devices, gather_grads(): lax.all_gather(grad_rows, 'tensor', axis=0, tiled=True)  97.4 us
  transfers between devices with their start and end apart: 45, of which 40 were waited for; matrix products, arithmetic and copies ran while one was open for 20% of the time, Pallas kernels for 0%

commit v1 on v0

v1 whole, which is shorter than its diff:
```python
import jax
import jax.numpy as jnp
from jax import lax
from jax.sharding import PartitionSpec as P

HEAD_DIM = 64
BF = jnp.bfloat16
F32 = jnp.float32


def swap_tensor(x, bit):
    pairs = [(i, i ^ bit) for i in range(lax.axis_size("tensor"))]
    return lax.ppermute(x, "tensor", pairs)


def swap_dp(x, bit):
    pairs = [(i, i ^ bit) for i in range(lax.axis_size("dp"))]
    return lax.ppermute(x, "dp", pairs)


def in_order(flag, mine, theirs):
    return jnp.where(
        flag == 0, jnp.concatenate([mine, theirs], 0), jnp.concatenate([theirs, mine], 0)
    )


def normalize(states):
    average = jnp.mean(states, axis=-1, keepdims=True)
    centred = states - average
    variance = jnp.mean(centred * centred, axis=-1, keepdims=True)
    inverse = lax.rsqrt(variance + 1e-05)
    return (centred * inverse, inverse)


def norm_backward(normed, inverse, grad_normed):
    mean_grad = jnp.mean(grad_normed, axis=-1, keepdims=True)
    mean_proj = jnp.mean(grad_normed * normed, axis=-1, keepdims=True)
    return inverse * (grad_normed - mean_grad - normed * mean_proj)


def gelu_slope(hidden):
    normal_cdf = 0.5 * (1.0 + jax.scipy.special.erf(hidden * 0.7071067811865476))
    density = jnp.exp(-0.5 * hidden * hidden) * 0.3989422804014327
    return normal_cdf + hidden * density


def mm(left, right):
    return jnp.dot(left, right, preferred_element_type=F32)


def mm_rows(left, right):
    return lax.dot_general(left, right, (((0,), (0,)), ((), ())), preferred_element_type=F32)


def mm_cols(left, right):
    return lax.dot_general(left, right, (((1,), (1,)), ((), ())), preferred_element_type=F32)


def gather_core(mine):
    return jnp.concatenate([mine, swap_tensor(mine, 1)], axis=0)


def scatter_core(partial):
    half = partial.shape[0] // 2
    return partial[:half] + swap_tensor(partial[half:].astype(BF), 1).astype(F32)


def fetch_foreign(weight):
    dp = lax.axis_index("dp")
    rows = weight.shape[0]
    if lax.axis_size("dp") % 4 or rows % 64:
        return swap_tensor(weight, 2)
    quarter = rows // 4
    piece = lax.dynamic_slice_in_dim(weight, lax.rem(dp, 4) * quarter, quarter, 0)
    piece = swap_tensor(piece, 2)
    bit0 = lax.rem(dp, 2)
    bit1 = lax.rem(dp // 2, 2)
    pair = in_order(bit0, piece, swap_dp(piece, 1))
    return in_order(bit1, pair, swap_dp(pair, 2))


def reduce_dp(grad):
    dp = lax.axis_index("dp")
    bits = []
    size = lax.axis_size("dp")
    bit = 1
    while bit < size:
        bits.append(bit)
        bit *= 2
    value = grad.astype(BF)
    for bit in bits:
        half = value.shape[0] // 2
        flag = lax.rem(dp // bit, 2)
        send = lax.dynamic_slice_in_dim(value, (1 - flag) * half, half, 0)
        keep = lax.dynamic_slice_in_dim(value, flag * half, half, 0)
        value = (keep.astype(F32) + swap_dp(send, bit).astype(F32)).astype(BF)
    for bit in reversed(bits):
        flag = lax.rem(dp // bit, 2)
        value = in_order(flag, value, swap_dp(value, bit))
    return value.astype(F32)


def finish_grad(own, foreign):
    back = swap_tensor(foreign.astype(BF), 2)
    return reduce_dp(own + back.astype(F32))


def masked_scores(query_rows, keys, query_pos, key_pos, key_valid, causal, scaling):
    scores = (
        jnp.einsum("qhe,khe->hqk", query_rows, keys, preferred_element_type=F32) * scaling
    )
    allowed = key_valid[None, None, :]
    if causal:
        allowed = allowed & (key_pos[None, None, :] <= query_pos[None, :, None])
    return jnp.where(allowed, scores, -1e30)


def attention_forward(queries, keys, values, pos, key_valid, causal, scaling):
    length = queries.shape[0]
    block_rows = length // 2
    outputs = []
    logsums = []
    for first_row in range(0, length, block_rows):
        rows = slice(first_row, first_row + block_rows)
        scores = masked_scores(queries[rows], keys, pos[rows], pos, key_valid, causal, scaling)
        row_max = jnp.max(scores, axis=-1, keepdims=True)
        logsum = row_max + jnp.log(jnp.sum(jnp.exp(scores - row_max), axis=-1, keepdims=True))
        weights = jnp.exp(scores - logsum).astype(BF)
        mixed_rows = jnp.einsum("hqk,khe->qhe", weights, values, preferred_element_type=F32)
        outputs.append(mixed_rows.reshape(block_rows, -1).astype(BF))
        logsums.append(logsum[:, :, 0])
    return (jnp.concatenate(outputs, axis=0), jnp.concatenate(logsums, axis=1))


def attention_backward(queries, keys, values, logsums, grad_mixed, pos, key_valid, causal, scaling):
    length = queries.shape[0]
    block_rows = length // 2
    grad_heads = grad_mixed.reshape(queries.shape)
    grad_keys = jnp.zeros(keys.shape, F32)
    grad_values = jnp.zeros(values.shape, F32)
    query_grads = []
    for first_row in range(0, length, block_rows):
        rows = slice(first_row, first_row + block_rows)
        query_rows = queries[rows]
        grad_rows = grad_heads[rows]
        scores = masked_scores(query_rows, keys, pos[rows], pos, key_valid, causal, scaling)
        row_probs = jnp.exp(scores - logsums[:, rows, None])
        grad_probs = jnp.einsum("qhe,khe->hqk", grad_rows, values, preferred_element_type=F32)
        grad_values = grad_values + jnp.einsum(
            "hqk,qhe->khe", row_probs.astype(BF), grad_rows, preferred_element_type=F32
        )
        grad_scores = row_probs * (
            grad_probs - jnp.sum(row_probs * grad_probs, axis=-1, keepdims=True)
        )
        grad_scores = grad_scores.astype(BF)
        query_grads.append(
            jnp.einsum("hqk,khe->qhe", grad_scores, keys, preferred_element_type=F32) * scaling
        )
        grad_keys = (
            grad_keys
            + jnp.einsum("hqk,qhe->khe", grad_scores, query_rows, preferred_element_type=F32)
            * scaling
        )
    grad_queries = jnp.concatenate(query_grads, axis=0)
    stacked = jnp.stack([grad_queries, grad_keys, grad_values], axis=1).astype(BF)
    return stacked.reshape(length, -1)


def layer_forward(states, gains, shifts, weights, pos, key_valid, causal, scaling):
    normed_att, inverse_att = normalize(states)
    gathered_att = gather_core((normed_att * gains[0] + shifts[0]).astype(BF))
    length = gathered_att.shape[0]
    heads = []
    for part in range(2):
        projected = mm(gathered_att, weights["qkv"][part]).astype(BF)
        split = projected.reshape(length, 3, -1, HEAD_DIM)
        attended, logsums = attention_forward(
            split[:, 0], split[:, 1], split[:, 2], pos, key_valid, causal, scaling
        )
        heads.append((split, attended, logsums))
    middle = states + scatter_core(
        mm(heads[0][1], weights["out"][0]) + mm(heads[1][1], weights["out"][1])
    )
    normed_ffn, inverse_ffn = normalize(middle)
    gathered_ffn = gather_core((normed_ffn * gains[1] + shifts[1]).astype(BF))
    units = []
    for part in range(2):
        hidden = mm(gathered_ffn, weights["up"][part])
        active = jax.nn.gelu(hidden, approximate=False).astype(BF)
        units.append((hidden, active))
    result = middle + scatter_core(
        mm(units[0][1], weights["down"][0]) + mm(units[1][1], weights["down"][1])
    )
    kept = (normed_att, inverse_att, gathered_att, heads, normed_ffn, inverse_ffn, gathered_ffn, units)
    return result, kept


def layer_backward(grad_states, kept, gains, weights, pos, key_valid, causal, scaling):
    (normed_att, inverse_att, gathered_att, heads, normed_ffn, inverse_ffn, gathered_ffn, units) = kept
    grads = {"qkv": [], "out": [], "up": [], "down": []}
    gathered_grad = gather_core(grad_states.astype(BF))
    partial = 0.0
    for part in range(2):
        hidden, active = units[part]
        grad_active = mm_cols(gathered_grad, weights["down"][part])
        grad_hidden = (grad_active * gelu_slope(hidden)).astype(BF)
        grads["down"].append(mm_rows(active, gathered_grad))
        grads["up"].append(mm_rows(gathered_ffn, grad_hidden))
        partial = partial + mm_cols(grad_hidden, weights["up"][part])
    grad_entering = scatter_core(partial)
    gain_ffn = jnp.sum(grad_entering * normed_ffn, axis=0)
    shift_ffn = jnp.sum(grad_entering, axis=0)
    grad_middle = grad_states + norm_backward(normed_ffn, inverse_ffn, grad_entering * gains[1])
    gathered_grad = gather_core(grad_middle.astype(BF))
    partial = 0.0
    for part in range(2):
        split, attended, logsums = heads[part]
        grad_attended = mm_cols(gathered_grad, weights["out"][part]).astype(BF)
        grads["out"].append(mm_rows(attended, gathered_grad))
        grad_projected = attention_backward(
            split[:, 0], split[:, 1], split[:, 2], logsums, grad_attended, pos, key_valid, causal, scaling
        )
        grads["qkv"].append(mm_rows(gathered_att, grad_projected))
        partial = partial + mm_cols(grad_projected, weights["qkv"][part])
    grad_entering = scatter_core(partial)
    gain_att = jnp.sum(grad_entering * normed_att, axis=0)
    shift_att = jnp.sum(grad_entering, axis=0)
    grad_input = grad_middle + norm_backward(normed_att, inverse_att, grad_entering * gains[0])
    return (
        grad_input,
        {name: finish_grad(*pair) for name, pair in grads.items()},
        jnp.stack([gain_att, gain_ffn]),
        jnp.stack([shift_att, shift_ffn]),
    )


def per_device(
    frames, lengths, codebook, ln_gain, ln_bias, ada_scale, ada_shift, w_qkv, w_out, w_up, w_down, out_grad
):
    tensor = lax.axis_index("tensor")
    chip = tensor // 2
    core = lax.rem(tensor, 2)
    block = frames.shape[1]
    length = block * lax.axis_size("tensor")
    scaling = HEAD_DIM ** (-0.5)

    def pick(pair):
        return jnp.where(chip == 0, pair[0], pair[1])

    def other(pair):
        return jnp.where(chip == 0, pair[1], pair[0])

    def take_rows(array):
        return in_order(chip, pick(array), swap_tensor(other(array), 2)).astype(F32)

    blocks = [core, 2 + core, 1 - core, 3 - core]
    pos = jnp.concatenate([index * block + jnp.arange(block) for index in blocks])
    key_valid = pos < pick(lengths)
    section = pick(codebook)
    section_match = (jnp.arange(ada_scale.shape[0]) == section)[:, None, None]
    gains = (ln_gain, jnp.sum(jnp.where(section_match, ada_scale, 0.0), axis=0))
    shifts = (ln_bias, jnp.sum(jnp.where(section_match, ada_shift, 0.0), axis=0))
    weights = []
    for layer in range(2):
        own = {
            "qkv": w_qkv[layer].reshape(w_qkv.shape[1], -1),
            "out": w_out[layer],
            "up": w_up[layer],
            "down": w_down[layer],
        }
        weights.append({name: (own[name], fetch_foreign(own[name])) for name in own})
    states = take_rows(frames)
    kept = [None, None]
    for layer in range(2):
        states, kept[layer] = layer_forward(
            states, gains[layer], shifts[layer], weights[layer], pos, key_valid, layer == 0, scaling
        )

    def give_rows(array):
        first, second = array[:block], array[block:]
        mine = jnp.where(chip == 0, first, second)
        theirs = swap_tensor(jnp.where(chip == 0, second, first), 2)
        return in_order(chip, mine[None], theirs[None])

    hidden_out = give_rows(states.astype(BF))
    grad_states = take_rows(out_grad)
    sums = [None, None]
    gain_grads = [None, None]
    shift_grads = [None, None]
    for layer in (1, 0):
        grad_states, sums[layer], gain_grads[layer], shift_grads[layer] = layer_backward(
            grad_states, kept[layer], gains[layer], weights[layer], pos, key_valid, layer == 0, scaling
        )
    frames_grad = give_rows(grad_states.astype(BF)).astype(F32)
    sections = ada_scale.shape[0]
    small = jnp.concatenate(
        [
            gain_grads[0],
            shift_grads[0],
            jnp.where(section_match, gain_grads[1][None], 0.0).reshape(2 * sections, -1),
            jnp.where(section_match, shift_grads[1][None], 0.0).reshape(2 * sections, -1),
        ]
    )
    small = lax.psum(small, ("dp", "tensor"))

    def both(name, shape):
        return jnp.stack([sums[layer][name].reshape(shape[1:]) for layer in range(2)])

    return (
        hidden_out,
        frames_grad,
        small[0:2],
        small[2:4],
        small[4 : 4 + 2 * sections].reshape(ada_scale.shape),
        small[4 + 2 * sections :].reshape(ada_scale.shape),
        both("qkv", w_qkv.shape),
        both("out", w_out.shape),
        both("up", w_up.shape),
        both("down", w_down.shape),
    )


def solution(mesh):
    placed = (
        P("dp", "tensor", None),
        P("dp"),
        P("dp"),
        P(),
        P(),
        P(),
        P(),
        P(None, None, None, "tensor"),
        P(None, "tensor", None),
        P(None, None, "tensor"),
        P(None, "tensor", None),
        P("dp", "tensor", None),
    )
    return jax.shard_map(
        per_device,
        mesh=mesh,
        in_specs=placed,
        out_specs=(
            P("dp", "tensor", None),
            P("dp", "tensor", None),
            P(),
            P(),
            P(),
            P(),
            P(None, None, None, "tensor"),
            P(None, "tensor", None),
            P(None, None, "tensor"),
            P(None, "tensor", None),
        ),
        check_vma=False,
    )
```

time: 2140 us -> 1140 us (0.53)
  waiting for transfers between devices: 1460 us -> 443 us
  starting transfers between devices: 4.4 us -> 106 us
  blocking collectives: 74.7 us -> 0 us
  matrix products: 347 us -> 324 us
    reduce_scatter x20 -> x0, waiting for transfers between devices: 830 us -> none  [the longest x8 221 us: scatter_rows(): lax.psum_scatter(partial_sum(jnp.int32(0), row_count * lax.axis_size('ten...]
    all_gather x20 -> x0, waiting for transfers between devices: 439 us -> none  [the longest x8 125 us: gather_rows(): lax.all_gather(entering, 'tensor', axis=0, tiled=True)]
    ppermute x0 -> x100, waiting for transfers between devices: none -> 330 us  [the longest x64 259 us: swap_dp(): return lax.ppermute(x, 'dp', pairs)]
    unnamed x49 -> x1, waiting for transfers between devices: 193 us -> 0.02 us
    psum x1, waiting for transfers between devices: 0.02 us -> 113 us  [per_device(): small = lax.psum(small, ('dp', 'tensor'))]
    ppermute x0 -> x100, starting transfers between devices: none -> 106 us  [the longest x64 77.9 us: swap_dp(): return lax.ppermute(x, 'dp', pairs)]
    all_gather x4 -> x0, blocking collectives: 74.7 us -> none  [the longest x1 18.9 us: per_device(): lax.all_gather(shift_share.astype(jnp.bfloat16), 'dp', axis=2, tiled=True)]
    select_n x0 -> x39, other arithmetic: none -> 36.8 us  [the longest x36 34.7 us: in_order(): jnp.where(flag == 0, jnp.concatenate([mine, theirs], 0), jnp.concatenate(...]
  transfers between devices with their start and end apart: 45 -> 101, of which waited for: 40 -> 47; matrix products, arithmetic and copies ran while one was open for 20% -> 45% of each run, Pallas kernels for 0% -> 0%
where the time goes in v1:
time: 1140 us; the launch traced here: 1130 us
  waiting for transfers between devices  443 us (39%)
  matrix products  324 us (28%)
  other arithmetic  172 us (15%)
  starting transfers between devices  106 us (9%)
  local copies, waits for them, and re-layouts  65.9 us (6%)
  between operations  21.2 us (2%)
    ppermute x64, waiting for transfers between devices, swap_dp(): return lax.ppermute(x, 'dp', pairs)  259 us
    psum x1, waiting for transfers between devices, per_device(): small = lax.psum(small, ('dp', 'tensor'))  113 us
    ppermute x64, starting transfers between devices, swap_dp(): return lax.ppermute(x, 'dp', pairs)  77.9 us
    dot_general x16, matrix products, mm(): return jnp.dot(left, right, preferred_element_type=F32)  74.2 us
    ppermute x36, waiting for transfers between devices, swap_tensor(): return lax.ppermute(x, 'tensor', pairs)  70.8 us
    dot_general x8, matrix products, attention_backward(): jnp.einsum('qhe,khe->hqk', grad_rows, values, preferred_element_type=F32)  64.6 us
    dot_general x16, matrix products, mm_rows(): lax.dot_general(left, right, (((0,), (0,)), ((), ())), preferred_element_...  52.4 us
    convert_element_type x3, other arithmetic, attention_backward(): grad_scores = grad_scores.astype(BF)  45.6 us
  transfers between devices with their start and end apart: 101, of which 47 were waited for; matrix products, arithmetic and copies ran while one was open for 45% of the time, Pallas kernels for 0%

profile of v1, /device:TPU:0, one launch (start us, length us, event | category | flops | bytes accessed | tf_op | source)
XLA Modules:
  0.0 1131.8 jit_solution(17757385365313296700)
XLA Ops:
  53.2 9.9 collective-permute-done.4
  82.8 15.6 %exponential_reduce_fusion.4 = (f32[4,512]{1,0:T(4,128)S(1)}, f32[4,512]{1,0:T(4,128)S(1)}) fusion(f32[4,512,1024]{2,1,0:T(8,128)S(1)} %get-tuple-element.117, f32[4,512]{1,0:T(4,128)S(1)} %get-tuple-element.36, pred[512,1024]{1,0:T(8,128)(4,1)S(1)} %get-tuple-element.106, f32[4,512]{1,0:T(4,128)S(1)} %get-tuple-element.37, f32[4,512,1024]{2,1,0:T(8,128)S(1)} %fusion.156), kind=kLoop, calls=%fused_computation.29 | loop fusion | flops 16773120 | bytes 17334272 | tf_op jit(solution)/shard_map/reduce_sum | solution.py:127
  113.9 9.3 collective-permute-done.10
  124.3 9.6 collective-permute-done.13
  137.7 9.5 collective-permute-done.14
  149.0 13.5 %fusion.18 = (bf16[1024,1024]{1,0:T(8,128)(2,1)S(1)}, f32[1024,1024]{1,0:T(8,128)}) fusion(bf16[2,1024,1024]{2,1,0:T(8,128)(2,1)S(1)} %copy-done.54, bf16[512,1024]{1,0:T(8,128)(2,1)S(1)} %collective-permute-done.9, bf16[512,1024]{1,0:T(8,128)(2,1)S(1)} %add_convert_fusion.12), kind=kOutput, calls=%fused_computation.66 | convolution fusion | flops 2219835392 | bytes 10485760 | tf_op jit(solution)/shard_map/dot_general | solution.py:48
  162.7 12.6 %fusion.21 = (bf16[1024,1024]{1,0:T(8,128)(2,1)S(1)}, f32[1024,1024]{1,0:T(8,128)}) fusion(bf16[512,1024]{1,0:T(8,128)(2,1)S(1)} %collective-permute-done.12, bf16[512,1024]{1,0:T(8,128)(2,1)S(1)} %maximum_select_fusion.13, pred[]{:T(512)S(6)} %eq.17, bf16[512,1024]{1,0:T(8,128)(2,1)S(1)} %collective-permute-done.9, ...), kind=kOutput, calls=%fused_computation.69 | convolution fusion | flops 2229272576 | bytes 10485761 | tf_op jit(solution)/shard_map/dot_general | solution.py:48
  198.6 10.0 collective-permute-done.18
  227.7 18.4 %collective-permute-done.20 = bf16[512,768]{0,1:T(8,128)(2,1)S(1)} collective-permute-done((bf16[512,768]{0,1:T(8,128)(2,1)S(1)}, bf16[512,768]{0,1:T(8,128)(2,1)S(1)}, u32[]{:S(2)}, u32[]{:S(2)}) %collective-permute-start.20) | collective-permute-done | bytes 786464 | tf_op jit(solution)/shard_map/ppermute | solution.py:18
  254.4 10.7 exponential_reduce_fusion.1
  291.0 8.3 collective-permute-done.26
  300.2 10.3 collective-permute-done.29
  311.5 9.7 collective-permute-done.34
  325.5 10.8 fusion.24
  336.3 12.0 %collective-permute-done.28 = bf16[512,1024]{1,0:T(8,128)(2,1)S(1)} collective-permute-done((bf16[512,1024]{1,0:T(8,128)(2,1)S(1)}, bf16[512,1024]{1,0:T(8,128)(2,1)S(1)}, u32[]{:S(2)}, u32[]{:S(2)}) %collective-permute-start.28) | collective-permute-done | bytes 1048608 | tf_op jit(solution)/shard_map/ppermute | solution.py:18
  348.3 11.2 fusion.27
  433.6 18.8 %multiply_reduce_fusion.4 = (f32[4,512]{1,0:T(4,128)S(1)}, f32[4,512]{1,0:T(4,128)S(1)}, f32[4,512]{1,0:T(4,128)S(1)}, f32[4,512]{1,0:T(4,128)S(1)}, f32[4,512,1024]{2,1,0:T(8,128)}) fusion(f32[4,512,1024]{2,1,0:T(8,128)S(1)} %bitcast.373, f32[4,512]{1,0:T(4,128)S(1)} %copy-done.114, pred[1024]{0:T(1024)(128)(4,1)S(1)} %copy-done.134, ...), kind=kOutput, calls=%fused_computation.9 | convolution fusion | flops 310370304 | bytes 67961856 | tf_op jit(solution)/shard_map/qhe,khe->hqk/dot_general | solution.py:148
  452.4 26.8 %multiply_convert_fusion.4 = (bf16[4,512,1024]{2,1,0:T(8,128)(2,1)}, bf16[4,512,1024]{2,1,0:T(8,128)(2,1)}, bf16[4,512,1024]{2,1,0:T(8,128)(2,1)}, bf16[4,512,1024]{2,1,0:T(8,128)(2,1)}) fusion(f32[4,512,1024]{2,1,0:T(8,128)} %get-tuple-element.129, f32[4,512,1024]{2,1,0:T(8,128)S(1)} %bitcast.373, f32[4,512]{1,0:T(4,128)S(1)} %get-tuple-element.38, ...), kind=kLoop, calls=%fused_computation.8 | loop fusion | flops 50331648 | bytes 83952640 | tf_op jit(solution)/shard_map/convert_element_type | solution.py:155
  546.0 15.6 %collective-permute-done.80 = bf16[512,1024]{1,0:T(8,128)(2,1)} collective-permute-done((bf16[512,1024]{1,0:T(8,128)(2,1)}, bf16[512,1024]{1,0:T(8,128)(2,1)}, u32[]{:S(2)}, u32[]{:S(2)}) %collective-permute-start.80) | collective-permute-done | bytes 1048608 | tf_op jit(solution)/shard_map/ppermute | solution.py:18
  566.4 17.7 %collective-permute-done.94 = bf16[512,1024]{1,0:T(8,128)(2,1)} collective-permute-done((bf16[512,1024]{1,0:T(8,128)(2,1)S(1)}, bf16[512,1024]{1,0:T(8,128)(2,1)}, u32[]{:S(2)}, u32[]{:S(2)}) %collective-permute-start.94) | collective-permute-done | bytes 1048608 | tf_op jit(solution)/shard_map/ppermute | solution.py:18
  599.7 15.1 %collective-permute-done.82 = bf16[128,1024]{1,0:T(8,128)(2,1)S(1)} collective-permute-done((bf16[128,1024]{1,0:T(8,128)(2,1)S(1)}, bf16[128,1024]{1,0:T(8,128)(2,1)S(1)}, u32[]{:S(2)}, u32[]{:S(2)}) %collective-permute-start.82) | collective-permute-done | bytes 262176 | tf_op jit(solution)/shard_map/ppermute | solution.py:18
  614.9 11.1 collective-permute-done.96
  656.5 13.8 %collective-permute-done.54 = bf16[128,768]{0,1:T(8,128)(2,1)S(1)} collective-permute-done((bf16[128,768]{0,1:T(8,128)(2,1)S(1)}, bf16[128,768]{0,1:T(8,128)(2,1)S(1)}, u32[]{:S(2)}, u32[]{:S(2)}) %collective-permute-start.54) | collective-permute-done | bytes 196640 | tf_op jit(solution)/shard_map/ppermute | solution.py:18
  706.6 16.5 %collective-permute-done.99 = bf16[512,1024]{1,0:T(8,128)(2,1)} collective-permute-done((bf16[512,1024]{1,0:T(8,128)(2,1)}, bf16[512,1024]{1,0:T(8,128)(2,1)}, u32[]{:S(2)}, u32[]{:S(2)}) %collective-permute-start.99) | collective-permute-done | bytes 1048608 | tf_op jit(solution)/shard_map/ppermute | solution.py:18
  737.4 10.9 multiply_reduce_fusion.1
  748.3 10.2 multiply_convert_fusion.1
  801.2 10.8 multiply_reduce_fusion
  812.0 8.6 multiply_convert_fusion
  894.7 113.0 %all-reduce.2.cloned.1.call-done = f32[32,1024]{1,0:T(8,128)} async-done(((f32[32,1024]{1,0:T(8,128)}), f32[32,1024]{1,0:T(8,128)}) %all-reduce.2.cloned.1.call-update) | async-done | bytes 131088 | tf_op jit(solution)/shard_map/psum | solution.py:304
  1018.5 11.9 %collective-permute-done.76 = bf16[128,1024]{1,0:T(8,128)(2,1)S(1)} collective-permute-done((bf16[128,1024]{1,0:T(8,128)(2,1)S(1)}, bf16[128,1024]{1,0:T(8,128)(2,1)S(1)}, u32[]{:S(2)}, u32[]{:S(2)}) %collective-permute-start.76) | collective-permute-done | bytes 262176 | tf_op jit(solution)/shard_map/ppermute | solution.py:18
  1041.3 10.8 collective-permute-done.77
  1089.1 12.2 %collective-permute-done.92 = bf16[512,1024]{1,0:T(8,128)(2,1)} collective-permute-done((bf16[512,1024]{1,0:T(8,128)(2,1)S(1)}, bf16[512,1024]{1,0:T(8,128)(2,1)}, u32[]{:S(2)}, u32[]{:S(2)}) %collective-permute-start.92) | collective-permute-done | bytes 1048608 | tf_op jit(solution)/shard_map/ppermute | solution.py:18
  (958 shorter events, 605.0 us)
Async XLA Ops:
  7.2 1000.5 %all-reduce.2.cloned.1.call-start = ((), (), s32[]{:S(2)}) async-start(), calls=%async_computation | async-start | bytes 262144 | tf_op jit(solution)/shard_map/psum | solution.py:304
  38.6 65.6 %collective-permute-start.7 = (bf16[128,1024]{1,0:T(8,128)(2,1)S(1)}, bf16[128,1024]{1,0:T(8,128)(2,1)}, u32[]{:S(2)}, u32[]{:S(2)}) collective-permute-start(bf16[128,1024]{1,0:T(8,128)(2,1)S(1)} %maximum_select_fusion.54), channel_id=1, source_target_pairs={{0,8},{4,12},{8,0},{12,4},{16,24},{20,28},{24,16},{28,20},{1,9},{5... | collective-permute-start | bytes 786440 | tf_op jit(solution)/shard_map/ppermute | solution.py:18
  113.8 35.2 %collective-permute-start.9 = (bf16[512,1024]{1,0:T(8,128)(2,1)S(1)}, bf16[512,1024]{1,0:T(8,128)(2,1)S(1)}, u32[]{:S(2)}, u32[]{:S(2)}) collective-permute-start(bf16[512,1024]{1,0:T(8,128)(2,1)S(1)} %add_convert_fusion.12), channel_id=1, source_target_pairs={{0,1},{1,0},{2,3},{3,2},{4,5},{5,4},{6,7},{7,6},{8,9},{9,8},{10,11... | collective-permute-start | bytes 3145736 | tf_op jit(solution)/shard_map/ppermute | solution.py:13
  147.8 34.6 %collective-permute-start.15 = (bf16[512,1024]{1,0:T(8,128)(2,1)S(1)}, bf16[512,1024]{1,0:T(8,128)(2,1)S(1)}, u32[]{:S(2)}, u32[]{:S(2)}) collective-permute-start(bf16[512,1024]{1,0:T(8,128)(2,1)S(1)} %maximum_select_fusion.14), channel_id=1, source_target_pairs={{0,8},{4,12},{8,0},{12,4},{16,24},{20,28},{24,16},{28,20},{1,9},{5... | collective-permute-start | bytes 3145736 | tf_op jit(solution)/shard_map/ppermute | solution.py:18
  222.2 59.0 %collective-permute-start.23 = (bf16[128,1024]{1,0:T(8,128)(2,1)S(1)}, bf16[128,1024]{1,0:T(8,128)(2,1)}, u32[]{:S(2)}, u32[]{:S(2)}) collective-permute-start(bf16[128,1024]{1,0:T(8,128)(2,1)S(1)} %maximum_select_fusion.55), channel_id=1, source_target_pairs={{0,8},{4,12},{8,0},{12,4},{16,24},{20,28},{24,16},{28,20},{1,9},{5... | collective-permute-start | bytes 786440 | tf_op jit(solution)/shard_map/ppermute | solution.py:18
  288.9 36.6 %collective-permute-start.25 = (bf16[512,1024]{1,0:T(8,128)(2,1)S(1)}, bf16[512,1024]{1,0:T(8,128)(2,1)S(1)}, u32[]{:S(2)}, u32[]{:S(2)}) collective-permute-start(bf16[512,1024]{1,0:T(8,128)(2,1)S(1)} %add_convert_fusion.10), channel_id=1, source_target_pairs={{0,1},{1,0},{2,3},{3,2},{4,5},{5,4},{6,7},{7,6},{8,9},{9,8},{10,11... | collective-permute-start | bytes 3145736 | tf_op jit(solution)/shard_map/ppermute | solution.py:13
  321.7 37.8 %collective-permute-start.35 = (bf16[512,1024]{1,0:T(8,128)(2,1)S(1)}, bf16[512,1024]{1,0:T(8,128)(2,1)S(1)}, u32[]{:S(2)}, u32[]{:S(2)}) collective-permute-start(bf16[512,1024]{1,0:T(8,128)(2,1)S(1)} %maximum_select_fusion.18), channel_id=1, source_target_pairs={{0,1},{1,0},{2,3},{3,2},{4,5},{5,4},{6,7},{7,6},{8,9},{9,8},{10,11... | collective-permute-start | bytes 3145736 | tf_op jit(solution)/shard_map/ppermute | solution.py:13
  324.4 46.0 %collective-permute-start.31 = (bf16[512,1024]{1,0:T(8,128)(2,1)S(1)}, bf16[512,1024]{1,0:T(8,128)(2,1)S(1)}, u32[]{:S(2)}, u32[]{:S(2)}) collective-permute-start(bf16[512,1024]{1,0:T(8,128)(2,1)S(1)} %maximum_select_fusion.16), channel_id=1, source_target_pairs={{0,8},{4,12},{8,0},{12,4},{16,24},{20,28},{24,16},{28,20},{1,9},{5... | collective-permute-start | bytes 3145736 | tf_op jit(solution)/shard_map/ppermute | solution.py:18
  398.9 119.4 %collective-permute-start.93 = (bf16[1024,1024]{1,0:T(8,128)(2,1)}, bf16[1024,1024]{1,0:T(8,128)(2,1)}, u32[]{:S(2)}, u32[]{:S(2)}) collective-permute-start(bf16[1024,1024]{1,0:T(8,128)(2,1)} %convolution_convert_fusion), channel_id=1, source_target_pairs={{0,2},{1,3},{2,0},{3,1},{4,6},{5,7},{6,4},{7,5},{8,10},{9,11},{10,... | collective-permute-start | bytes 6291464 | tf_op jit(solution)/shard_map/ppermute | solution.py:13
  403.2 109.2 %collective-permute-start.79 = (bf16[1024,1024]{1,0:T(8,128)(2,1)}, bf16[1024,1024]{1,0:T(8,128)(2,1)}, u32[]{:S(2)}, u32[]{:S(2)}) collective-permute-start(bf16[1024,1024]{1,0:T(8,128)(2,1)} %convolution_convert_fusion.2), channel_id=1, source_target_pairs={{0,2},{1,3},{2,0},{3,1},{4,6},{5,7},{6,4},{7,5},{8,10},{9,11},{10,... | collective-permute-start | bytes 6291464 | tf_op jit(solution)/shard_map/ppermute | solution.py:13
  502.8 85.6 %collective-permute-start.51 = (bf16[1024,768]{0,1:T(8,128)(2,1)}, bf16[1024,768]{0,1:T(8,128)(2,1)}, u32[]{:S(2)}, u32[]{:S(2)}) collective-permute-start(bf16[1024,768]{0,1:T(8,128)(2,1)} %convolution_convert_fusion.4), channel_id=1, source_target_pairs={{0,2},{1,3},{2,0},{3,1},{4,6},{5,7},{6,4},{7,5},{8,10},{9,11},{10,... | collective-permute-start | bytes 4718600 | tf_op jit(solution)/shard_map/ppermute | solution.py:13
  536.2 48.0 %collective-permute-start.94 = (bf16[512,1024]{1,0:T(8,128)(2,1)S(1)}, bf16[512,1024]{1,0:T(8,128)(2,1)}, u32[]{:S(2)}, u32[]{:S(2)}) collective-permute-start(bf16[512,1024]{1,0:T(8,128)(2,1)S(1)} %constant_dynamic-slice_fusion.2), channel_id=1, source_target_pairs={{0,4},{4,0},{8,12},{12,8},{16,20},{20,16},{24,28},{28,24},{1,5},{5... | collective-permute-start | bytes 3145736 | tf_op jit(solution)/shard_map/ppermute | solution.py:18
  542.6 83.6 %collective-permute-start.39 = (bf16[512,1024]{1,0:T(8,128)(2,1)}, bf16[512,1024]{1,0:T(8,128)(2,1)S(1)}, u32[]{:S(2)}, u32[]{:S(2)}) collective-permute-start(bf16[512,1024]{1,0:T(8,128)(2,1)} %get-tuple-element.54), channel_id=1, source_target_pairs={{0,1},{1,0},{2,3},{3,2},{4,5},{5,4},{6,7},{7,6},{8,9},{9,8},{10,11... | collective-permute-start | bytes 3145736 | tf_op jit(solution)/shard_map/ppermute | solution.py:13
  598.6 39.2 %collective-permute-start.52 = (bf16[512,768]{0,1:T(8,128)(2,1)S(1)}, bf16[512,768]{0,1:T(8,128)(2,1)S(1)}, u32[]{:S(2)}, u32[]{:S(2)}) collective-permute-start(bf16[512,768]{0,1:T(8,128)(2,1)S(1)} %constant_dynamic-slice_fusion.20), channel_id=1, source_target_pairs={{0,4},{4,0},{8,12},{12,8},{16,20},{20,16},{24,28},{28,24},{1,5},{5... | collective-permute-start | bytes 2359304 | tf_op jit(solution)/shard_map/ppermute | solution.py:18
  640.8 43.7 %collective-permute-start.40 = (bf16[512,1024]{1,0:T(8,128)(2,1)S(1)}, bf16[512,1024]{1,0:T(8,128)(2,1)S(1)}, u32[]{:S(2)}, u32[]{:S(2)}) collective-permute-start(bf16[512,1024]{1,0:T(8,128)(2,1)S(1)} %slice.657), channel_id=1, source_target_pairs={{0,1},{1,0},{2,3},{3,2},{4,5},{5,4},{6,7},{7,6},{8,9},{9,8},{10,11... | collective-permute-start | bytes 3145736 | tf_op jit(solution)/shard_map/ppermute | solution.py:13
  655.0 106.9 %collective-permute-start.72 = (bf16[1024,1024]{1,0:T(8,128)(2,1)}, bf16[1024,1024]{1,0:T(8,128)(2,1)}, u32[]{:S(2)}, u32[]{:S(2)}) collective-permute-start(bf16[1024,1024]{1,0:T(8,128)(2,1)} %convolution_convert_fusion.3), channel_id=1, source_target_pairs={{0,2},{1,3},{2,0},{3,1},{4,6},{5,7},{6,4},{7,5},{8,10},{9,11},{10,... | collective-permute-start | bytes 6291464 | tf_op jit(solution)/shard_map/ppermute | solution.py:13
  676.8 46.3 %collective-permute-start.99 = (bf16[512,1024]{1,0:T(8,128)(2,1)}, bf16[512,1024]{1,0:T(8,128)(2,1)}, u32[]{:S(2)}, u32[]{:S(2)}) collective-permute-start(bf16[512,1024]{1,0:T(8,128)(2,1)} %maximum_select_fusion.23), channel_id=1, source_target_pairs={{0,4},{4,0},{8,12},{12,8},{16,20},{20,16},{24,28},{28,24},{1,5},{5... | collective-permute-start | bytes 3145736 | tf_op jit(solution)/shard_map/ppermute | solution.py:18
  688.7 39.1 %collective-permute-start.41 = (bf16[512,1024]{1,0:T(8,128)(2,1)}, bf16[512,1024]{1,0:T(8,128)(2,1)S(1)}, u32[]{:S(2)}, u32[]{:S(2)}) collective-permute-start(bf16[512,1024]{1,0:T(8,128)(2,1)} %get-tuple-element.52), channel_id=1, source_target_pairs={{0,1},{1,0},{2,3},{3,2},{4,5},{5,4},{6,7},{7,6},{8,9},{9,8},{10,11... | collective-permute-start | bytes 3145736 | tf_op jit(solution)/shard_map/ppermute | solution.py:13
  695.5 94.7 %collective-permute-start.86 = (bf16[1024,1024]{1,0:T(8,128)(2,1)}, bf16[1024,1024]{1,0:T(8,128)(2,1)}, u32[]{:S(2)}, u32[]{:S(2)}) collective-permute-start(bf16[1024,1024]{1,0:T(8,128)(2,1)} %convolution_convert_fusion.1), channel_id=1, source_target_pairs={{0,2},{1,3},{2,0},{3,1},{4,6},{5,7},{6,4},{7,5},{8,10},{9,11},{10,... | collective-permute-start | bytes 6291464 | tf_op jit(solution)/shard_map/ppermute | solution.py:13
  701.8 150.7 %collective-permute-start.57 = (bf16[512,768]{0,1:T(8,128)(2,1)}, bf16[512,768]{0,1:T(8,128)(2,1)}, u32[]{:S(2)}, u32[]{:S(2)}) collective-permute-start(bf16[512,768]{0,1:T(8,128)(2,1)} %maximum_select_fusion.29), channel_id=1, source_target_pairs={{0,4},{4,0},{8,12},{12,8},{16,20},{20,16},{24,28},{28,24},{1,5},{5... | collective-permute-start | bytes 2359304 | tf_op jit(solution)/shard_map/ppermute | solution.py:18
  767.8 93.9 %collective-permute-start.73 = (bf16[512,1024]{1,0:T(8,128)(2,1)}, bf16[512,1024]{1,0:T(8,128)(2,1)}, u32[]{:S(2)}, u32[]{:S(2)}) collective-permute-start(bf16[512,1024]{1,0:T(8,128)(2,1)} %constant_dynamic-slice_fusion.11), channel_id=1, source_target_pairs={{0,4},{4,0},{8,12},{12,8},{16,20},{20,16},{24,28},{28,24},{1,5},{5... | collective-permute-start | bytes 3145736 | tf_op jit(solution)/shard_map/ppermute | solution.py:18
  771.4 59.4 %collective-permute-start.58 = (bf16[256,1024]{1,0:T(8,128)(2,1)}, bf16[256,1024]{1,0:T(8,128)(2,1)}, u32[]{:S(2)}, u32[]{:S(2)}) collective-permute-start(bf16[256,1024]{1,0:T(8,128)(2,1)} %convolution_convert_fusion.11), channel_id=1, source_target_pairs={{0,2},{1,3},{2,0},{3,1},{4,6},{5,7},{6,4},{7,5},{8,10},{9,11},{10,... | collective-permute-start | bytes 1572872 | tf_op jit(solution)/shard_map/ppermute | solution.py:13
  796.8 67.7 %collective-permute-start.87 = (bf16[512,1024]{1,0:T(8,128)(2,1)}, bf16[512,1024]{1,0:T(8,128)(2,1)}, u32[]{:S(2)}, u32[]{:S(2)}) collective-permute-start(bf16[512,1024]{1,0:T(8,128)(2,1)} %constant_dynamic-slice_fusion.5), channel_id=1, source_target_pairs={{0,4},{4,0},{8,12},{12,8},{16,20},{20,16},{24,28},{28,24},{1,5},{5... | collective-permute-start | bytes 3145736 | tf_op jit(solution)/shard_map/ppermute | solution.py:18
  829.3 56.7 %collective-permute-start.44 = (bf16[1024,768]{0,1:T(8,128)(2,1)}, bf16[1024,768]{0,1:T(8,128)(2,1)}, u32[]{:S(2)}, u32[]{:S(2)}) collective-permute-start(bf16[1024,768]{0,1:T(8,128)(2,1)} %convolution_convert_fusion.5), channel_id=1, source_target_pairs={{0,2},{1,3},{2,0},{3,1},{4,6},{5,7},{6,4},{7,5},{8,10},{9,11},{10,... | collective-permute-start | bytes 4718600 | tf_op jit(solution)/shard_map/ppermute | solution.py:13
  859.6 179.1 %collective-permute-start.63 = (bf16[64,1024]{1,0:T(8,128)(2,1)S(1)}, bf16[64,1024]{1,0:T(8,128)(2,1)}, u32[]{:S(2)}, u32[]{:S(2)}) collective-permute-start(bf16[64,1024]{1,0:T(8,128)(2,1)S(1)} %maximum_select_fusion.58), channel_id=1, source_target_pairs={{0,8},{4,12},{8,0},{12,4},{16,24},{20,28},{24,16},{28,20},{1,9},{5... | collective-permute-start | bytes 393224 | tf_op jit(solution)/shard_map/ppermute | solution.py:18
  881.0 191.0 %collective-permute-start.43 = (bf16[256,1024]{1,0:T(8,128)(2,1)}, bf16[256,1024]{1,0:T(8,128)(2,1)}, u32[]{:S(2)}, u32[]{:S(2)}) collective-permute-start(bf16[256,1024]{1,0:T(8,128)(2,1)} %get-tuple-element.72), channel_id=1, source_target_pairs={{0,2},{1,3},{2,0},{3,1},{4,6},{5,7},{6,4},{7,5},{8,10},{9,11},{10,... | collective-permute-start | bytes 1572872 | tf_op jit(solution)/shard_map/ppermute | solution.py:13
  884.5 125.5 %collective-permute-start.75 = (bf16[128,1024]{1,0:T(8,128)(2,1)}, bf16[128,1024]{1,0:T(8,128)(2,1)}, u32[]{:S(2)}, u32[]{:S(2)}) collective-permute-start(bf16[128,1024]{1,0:T(8,128)(2,1)} %constant_dynamic-slice_fusion.9), channel_id=1, source_target_pairs={{0,16},{4,20},{8,24},{12,28},{16,0},{20,4},{24,8},{28,12},{1,17},{... | collective-permute-start | bytes 786440 | tf_op jit(solution)/shard_map/ppermute | solution.py:18
  890.9 123.2 %collective-permute-start.45 = (bf16[512,768]{0,1:T(8,128)(2,1)}, bf16[512,768]{0,1:T(8,128)(2,1)S(1)}, u32[]{:S(2)}, u32[]{:S(2)}) collective-permute-start(bf16[512,768]{0,1:T(8,128)(2,1)} %constant_dynamic-slice_fusion.23), channel_id=1, source_target_pairs={{0,4},{4,0},{8,12},{12,8},{16,20},{20,16},{24,28},{28,24},{1,5},{5... | collective-permute-start | bytes 2359304 | tf_op jit(solution)/shard_map/ppermute | solution.py:18
  894.5 118.0 %collective-permute-start.89 = (bf16[128,1024]{1,0:T(8,128)(2,1)S(1)}, bf16[128,1024]{1,0:T(8,128)(2,1)S(1)}, u32[]{:S(2)}, u32[]{:S(2)}) collective-permute-start(bf16[128,1024]{1,0:T(8,128)(2,1)S(1)} %constant_dynamic-slice_fusion.3), channel_id=1, source_target_pairs={{0,16},{4,20},{8,24},{12,28},{16,0},{20,4},{24,8},{28,12},{1,17},{... | collective-permute-start | bytes 786440 | tf_op jit(solution)/shard_map/ppermute | solution.py:18
  1052.6 33.8 %collective-permute-start.78 = (bf16[512,1024]{1,0:T(8,128)(2,1)S(1)}, bf16[512,1024]{1,0:T(8,128)(2,1)}, u32[]{:S(2)}, u32[]{:S(2)}) collective-permute-start(bf16[512,1024]{1,0:T(8,128)(2,1)S(1)} %maximum_select_fusion.20), channel_id=1, source_target_pairs={{0,4},{4,0},{8,12},{12,8},{16,20},{20,16},{24,28},{28,24},{1,5},{5... | collective-permute-start | bytes 3145736 | tf_op jit(solution)/shard_map/ppermute | solution.py:18
  1064.6 36.8 %collective-permute-start.92 = (bf16[512,1024]{1,0:T(8,128)(2,1)S(1)}, bf16[512,1024]{1,0:T(8,128)(2,1)}, u32[]{:S(2)}, u32[]{:S(2)}) collective-permute-start(bf16[512,1024]{1,0:T(8,128)(2,1)S(1)} %maximum_select_fusion.22), channel_id=1, source_target_pairs={{0,4},{4,0},{8,12},{12,8},{16,20},{20,16},{24,28},{28,24},{1,5},{5... | collective-permute-start | bytes 3145736 | tf_op jit(solution)/shard_map/ppermute | solution.py:18
  1083.1 33.4 %collective-permute-start.50 = (bf16[512,768]{0,1:T(8,128)(2,1)S(1)}, bf16[512,768]{0,1:T(8,128)(2,1)S(1)}, u32[]{:S(2)}, u32[]{:S(2)}) collective-permute-start(bf16[512,768]{0,1:T(8,128)(2,1)S(1)} %maximum_select_fusion.27), channel_id=1, source_target_pairs={{0,4},{4,0},{8,12},{12,8},{16,20},{20,16},{24,28},{28,24},{1,5},{5... | collective-permute-start | bytes 2359304 | tf_op jit(solution)/shard_map/ppermute | solution.py:18
  (302 other events, 4076.2 us)
Sparse Core Ops, SparseCore 0:
  877.0 130.6 all-reduce.1

commit v2 on v1

v2 whole, which is shorter than its diff:
```python
import functools
from typing import Any, NamedTuple

import jax
import jax.numpy as jnp
from jax import lax
from jax.experimental import pallas as pl
from jax.experimental.pallas import tpu as pltpu
from jax.sharding import PartitionSpec as P

HEAD_DIM = 64
BF = jnp.bfloat16
F32 = jnp.float32
HIGH = lax.Precision.HIGHEST
MESH = pl.DeviceIdType.MESH
VMEM_BYTES = 60 << 20
LANES = 128


def mm(left, right):
    return jnp.dot(left, right, preferred_element_type=F32)


def mm_rows(left, right):
    return lax.dot_general(left, right, (((0,), (0,)), ((), ())), preferred_element_type=F32)


def mm_cols(left, right, precision=None):
    return lax.dot_general(
        left, right, (((1,), (1,)), ((), ())), precision=precision, preferred_element_type=F32
    )


def head_of_lane(shape):
    return lax.broadcasted_iota(jnp.int32, shape, len(shape) - 1) // HEAD_DIM


def at(start, size, unit):
    return pl.ds(pl.multiple_of(start, unit), size)


def flip(index, bit):
    return index + bit - 2 * bit * lax.rem(index // bit, 2)


def dp_bits(size):
    bits = []
    while 2 ** len(bits) < size:
        bits.append(2 ** len(bits))
    return bits


def attend_part(causal, n_ref, w_ref, bias_ref, qkva_ref, lse_ref):
    length = n_ref.shape[0]
    part = qkva_ref.shape[1] // 4
    block = length // 4
    scaling = HEAD_DIM ** (-0.5)

    def project(index, _):
        rows = at(index * block, block, block)
        qkva_ref[rows, : 3 * part] = mm(n_ref[rows, :], w_ref[:, : 3 * part]).astype(BF)
        return 0

    lax.fori_loop(0, 4, project, 0)

    def pair_body(pair, _):
        q_cols, k_cols, v_cols, a_cols = [at(i * part + pair * LANES, LANES, LANES) for i in range(4)]
        for first in range(0, length, block):
            rows = pl.ds(first, block)
            reach = first + block if causal else length
            queries = qkva_ref[rows, q_cols] * jnp.asarray(scaling, BF)
            keys = qkva_ref[pl.ds(0, reach), k_cols]
            values = qkva_ref[pl.ds(0, reach), v_cols]
            bias = bias_ref[:, pl.ds(0, reach)]
            head = head_of_lane(queries.shape)
            lanes = lax.broadcasted_iota(jnp.int32, (block, LANES), 1)
            mixed = None
            stats = jnp.zeros((block, LANES), F32)
            for which in range(2):
                scores = mm_cols(jnp.where(head == which, queries, jnp.zeros_like(queries)), keys) + bias
                if causal:
                    query_at = first + lax.broadcasted_iota(jnp.int32, scores.shape, 0)
                    key_at = lax.broadcasted_iota(jnp.int32, scores.shape, 1)
                    scores = jnp.where(key_at <= query_at, scores, -1e30)
                row_max = jnp.max(scores, axis=-1, keepdims=True)
                raised = jnp.exp(scores - row_max)
                total = jnp.sum(raised, axis=-1, keepdims=True)
                one = mm(raised.astype(BF), values) * (1.0 / total)
                mixed = one if mixed is None else jnp.where(head == 0, mixed, one)
                stats = jnp.where(lanes == which, row_max + jnp.log(total), stats)
            qkva_ref[rows, a_cols] = mixed.astype(BF)
            square = lax.broadcasted_iota(jnp.int32, (8, LANES), 1)
            pick = (square == lax.broadcasted_iota(jnp.int32, (8, LANES), 0)).astype(F32)
            lse_ref[pair, :, rows] = mm_cols(pick, stats, HIGH)
        return 0

    lax.fori_loop(0, part // LANES, pair_body, 0)


def attend_part_back(causal, grad_att_ref, qkva_ref, lse_of, bias_ref, dqkv_ref, dk_ref, dv_ref):
    length = qkva_ref.shape[0]
    part = qkva_ref.shape[1] // 4
    block = length // 4
    scaling = HEAD_DIM ** (-0.5)

    def pair_body(pair, _):
        q_cols, k_cols, v_cols, a_cols = [at(i * part + pair * LANES, LANES, LANES) for i in range(4)]
        g_cols = at(pair * LANES, LANES, LANES)
        dk_ref[...] = jnp.zeros_like(dk_ref)
        dv_ref[...] = jnp.zeros_like(dv_ref)
        keys_turned = qkva_ref[:, k_cols].astype(F32).T.astype(BF)
        feature = lax.broadcasted_iota(jnp.int32, keys_turned.shape, 0) // HEAD_DIM
        turned = [
            jnp.where(feature == which, keys_turned, jnp.zeros_like(keys_turned)) for which in range(2)
        ]
        for first in range(0, length, block):
            rows = pl.ds(first, block)
            reach = first + block if causal else length
            queries = qkva_ref[rows, q_cols] * jnp.asarray(scaling, BF)
            grads = grad_att_ref[rows, g_cols]
            head = head_of_lane(queries.shape)
            pick = (head_of_lane((8, LANES)) == lax.broadcasted_iota(jnp.int32, (8, LANES), 0)).astype(F32)
            product = grads.astype(F32) * qkva_ref[rows, a_cols].astype(F32)
            delta = mm_cols(pick, product, HIGH)
            lse = lse_of(pair, rows)
            keys = qkva_ref[pl.ds(0, reach), k_cols]
            values = qkva_ref[pl.ds(0, reach), v_cols]
            bias = bias_ref[pl.ds(0, reach), :]
            dq_turned = None
            for which in range(2):
                queries_one = jnp.where(head == which, queries, jnp.zeros_like(queries))
                grads_one = jnp.where(head == which, grads, jnp.zeros_like(grads))
                scores = mm_cols(keys, queries_one) + bias
                if causal:
                    key_at = lax.broadcasted_iota(jnp.int32, scores.shape, 0)
                    query_at = first + lax.broadcasted_iota(jnp.int32, scores.shape, 1)
                    scores = jnp.where(key_at <= query_at, scores, -1e30)
                probs = jnp.exp(scores - lse[which : which + 1])
                grad_probs = mm_cols(values, grads_one)
                grad_scores = (probs * (grad_probs - delta[which : which + 1])).astype(BF)
                dv_ref[pl.ds(0, reach), :] += mm(probs.astype(BF), grads_one)
                dk_ref[pl.ds(0, reach), :] += mm(grad_scores, queries_one)
                one = mm(turned[which][:, :reach], grad_scores)
                dq_turned = one if dq_turned is None else dq_turned + one
            dqkv_ref[rows, q_cols] = (dq_turned.T * scaling).astype(BF)
        dqkv_ref[:, k_cols] = dk_ref[...].astype(BF)
        dqkv_ref[:, v_cols] = dv_ref[...].astype(BF)
        return 0

    lax.fori_loop(0, part // LANES, pair_body, 0)


def gelu_parts(hidden):
    bell = jnp.exp(-0.5 * hidden * hidden)
    t = 1.0 / (1.0 + 0.23164189 * jnp.abs(hidden))
    poly = 0.5307027145
    poly = poly * t - 0.7265760135
    poly = poly * t + 0.7107068705
    poly = poly * t - 0.142248368
    poly = poly * t + 0.127414796
    tail = poly * t * bell
    cdf = jnp.where(hidden >= 0, 1.0 - tail, tail)
    return hidden * cdf, cdf + hidden * bell * 0.3989422804014327


class Slots:
    def __init__(self, buffers, sems):
        self.buffers = buffers
        self.sems = sems
        self.free = list(range(buffers.shape[0]))
        self.held = {}

    def load(self, name, source):
        slot = self.free.pop(0)
        copy = pltpu.make_async_copy(source, self.buffers.at[slot], self.sems.at[slot])
        copy.start()
        self.held[name] = [slot, copy]

    def get(self, name):
        slot, copy = self.held[name]
        if copy is not None:
            copy.wait()
            self.held[name][1] = None
        return self.buffers.at[slot]

    def drop(self, *names):
        for name in names:
            self.free.append(self.held.pop(name)[0])


class Summing:
    AHEAD = 4

    def __init__(self, bits, own, foreign, landed, out, acc, seg, y_view, own_view, rbufs, send_sem, recv_sem, copy_sem, view_sem):
        self.bits, self.own, self.foreign, self.landed, self.out = bits, own, foreign, landed, out
        self.acc, self.seg, self.y_view, self.own_view, self.rbufs = acc, seg, y_view, own_view, rbufs
        self.send_sem, self.recv_sem, self.copy_sem, self.view_sem = send_sem, recv_sem, copy_sem, view_sem
        self.chunks, self.rows, self.columns = own.shape
        self.ring = acc.shape[0]
        self.stages = 2 * len(bits) + 1
        self.dp = lax.axis_index("dp")
        self.tensor = lax.axis_index("tensor")
        self.step = 0
        self.started = 0
        self.ready = 0
        row, column = 0, 0
        self.sizes, self.keep, self.send = [], [], []
        for half_rows, half_columns, bit, by_rows in halvings(bits, self.rows, self.columns):
            flag = lax.rem(self.dp // bit, 2)
            if by_rows:
                keep = (row + flag * half_rows, column)
                send = (row + (1 - flag) * half_rows, column)
            else:
                keep = (row, column + flag * half_columns)
                send = (row, column + (1 - flag) * half_columns)
            row, column = keep
            self.sizes.append((half_rows, half_columns))
            self.keep.append(keep)
            self.send.append(send)

    def region(self, where, size):
        return at(where[0], size[0], 16), at(where[1], size[1], LANES)

    def copy(self, s, c):
        count = len(self.bits)
        if s == 0:
            source, target = self.foreign.at[c], self.landed.at[c]
            device = {"tensor": flip(self.tensor, 2)}
        elif s <= count:
            i = s - 1
            rows, columns = self.region(self.send[i], self.sizes[i])
            source = self.acc.at[c % self.ring, rows, columns]
            target = self.rbufs[i].at[c % self.ring]
            device = {"dp": flip(self.dp, self.bits[i])}
        else:
            i = 2 * count - s
            rows, columns = self.region(self.keep[i], self.sizes[i])
            target = self.out.at[c, rows, columns]
            source = self.seg.at[c] if i == count - 1 else target
            device = {"dp": flip(self.dp, self.bits[i])}
        return pltpu.make_async_remote_copy(
            src_ref=source,
            dst_ref=target,
            send_sem=self.send_sem.at[s, c],
            recv_sem=self.recv_sem.at[s, c],
            device_id=device,
            device_id_type=MESH,
        )

    def seg_copy(self, c):
        rows, columns = self.region(self.keep[-1], self.sizes[-1])
        return pltpu.make_async_copy(self.seg.at[c], self.out.at[c, rows, columns], self.copy_sem.at[c])

    def views(self, c):
        return (
            pltpu.make_async_copy(self.landed.at[c], self.y_view, self.view_sem.at[0]),
            pltpu.make_async_copy(self.own.at[c], self.own_view, self.view_sem.at[1]),
        )

    def finish(self, s, c):
        count = len(self.bits)
        slot = c % self.ring
        if s == 0:
            for view in self.views(c):
                view.wait()
            if c >= self.ring:
                for stage in range(1, count + 1):
                    self.copy(stage, c - self.ring).wait_send()
            self.acc[slot] = (self.own_view[...].astype(F32) + self.y_view[...].astype(F32)).astype(BF)
            return
        self.copy(s, c).wait_recv()
        if s <= count:
            i = s - 1
            rows, columns = self.region(self.keep[i], self.sizes[i])
            total = self.acc[slot, rows, columns].astype(F32) + self.rbufs[i][slot].astype(F32)
            if s == count:
                self.seg[c] = total.astype(BF)
                self.seg_copy(c).start()
            else:
                self.acc[slot, rows, columns] = total.astype(BF)
        elif s == count + 1:
            self.seg_copy(c).wait()

    def advance(self):
        first = self.step
        if first < self.chunks:
            self.copy(0, first).wait_recv()
            for view in self.views(first):
                view.start()
        for s in range(self.stages, 0, -1):
            c = first + 1 - s
            if 0 <= c < self.chunks:
                self.finish(s - 1, c)
                if s < self.stages:
                    self.copy(s, c).start()
        self.step += 1
        self.feed()

    def feed(self):
        while self.started < min(self.ready, self.step + self.AHEAD):
            self.copy(0, self.started).start()
            self.started += 1

    def drain(self):
        while self.step < self.chunks + self.stages - 1:
            self.advance()
        count = len(self.bits)
        for c in range(self.chunks):
            for s in range(self.stages):
                if not (1 <= s <= count and c + self.ring < self.chunks):
                    self.copy(s, c).wait_send()


def halvings(bits, rows, columns):
    steps = []
    for bit in bits:
        by_rows = rows >= 32
        rows, columns = (rows // 2, columns) if by_rows else (rows, columns // 2)
        steps.append((rows, columns, bit, by_rows))
    return steps


def back_kernel(bits, *refs):
    r, refs = BackIn(*refs[: len(BackIn._fields)]), refs[len(BackIn._fields) :]
    o, refs = BackOut(*refs[: len(BackOut._fields)]), refs[len(BackOut._fields) :]
    b, rbufs = BackScratch(*refs[: len(BackScratch._fields)]), refs[len(BackScratch._fields) :]
    dp = lax.axis_index("dp")
    tensor = lax.axis_index("tensor")
    chip = tensor // 2
    core = lax.rem(tensor, 2)
    half, width = b.state.shape
    length = 2 * half
    block = length // 4
    core_partner = {"tensor": flip(tensor, 1)}
    partners = [core_partner, {"tensor": flip(tensor, 2)}] + [{"dp": flip(dp, bit)} for bit in bits]

    barrier = pltpu.get_barrier_semaphore()
    for partner in partners:
        pl.semaphore_signal(barrier, inc=1, device_id=partner, device_id_type=MESH)
    pl.semaphore_wait(barrier, len(partners))

    slots = Slots(b.slots, b.slot_sem)
    summing = Summing(
        bits, o.own, o.foreign, o.landed, o.total, b.acc, b.seg, b.y_view, b.own_view,
        rbufs, b.send_sem, b.recv_sem, b.copy_sem, b.view_sem,
    )
    per_matrix = length // summing.rows
    vec = b.vec
    vec[...] = jnp.zeros_like(vec)

    def remote(source, target, sem, device):
        return pltpu.make_async_remote_copy(
            src_ref=source,
            dst_ref=target,
            send_sem=b.ex_send.at[sem],
            recv_sem=b.ex_recv.at[sem],
            device_id=device,
            device_id_type=MESH,
        )

    def exchange_copies(turn):
        full = b.full.at[turn % 2]
        spans = [at((2 * j + core) * block, block, block) for j in range(2)]
        return [remote(full.at[s], full.at[s], 4 * turn + j, core_partner) for j, s in enumerate(spans)]

    def exchange_start(turn, j):
        exchange_copies(turn)[j].start()

    def exchange_wait(turn):
        for copy in exchange_copies(turn):
            copy.wait()

    def scatter_copies(turn):
        return [
            remote(
                b.rs_send.at[pl.ds(j * block, block)],
                b.rs_recv.at[turn % 2, pl.ds(j * block, block)],
                4 * turn + 2 + j,
                core_partner,
            )
            for j in range(2)
        ]

    def scatter(turn, partial):
        copies = scatter_copies(turn)
        for j in range(2):
            span = at((2 * j + 1 - core) * block, block, block)
            b.rs_send[pl.ds(j * block, block), :] = partial(span).astype(BF)
            copies[j].start()
        for j in range(2):
            span = at((2 * j + core) * block, block, block)
            b.keep[pl.ds(j * block, block), :] = partial(span)
        for copy in copies:
            copy.wait()

    def norm_back(turn, layer, which, normed_copy, inverse_copy, last):
        normed_copy.wait()
        inverse_copy.wait()
        index = 4 * layer + 2 * which
        gain = r.gains[2 * layer + which : 2 * layer + which + 1, :]
        step = 128

        def rows_body(i, _):
            span = at(i * step, step, step)
            grad = b.keep[span, :] + b.rs_recv[turn % 2, span, :].astype(F32)
            normed = b.normed[span, :]
            moved = grad * gain
            mean_grad = jnp.mean(moved, axis=-1, keepdims=True)
            mean_proj = jnp.mean(moved * normed, axis=-1, keepdims=True)
            state = b.state[span, :] + b.inverse[span, :1] * (moved - mean_grad - normed * mean_proj)
            b.state[span, :] = state
            vec[index : index + 1, :] += jnp.sum(grad * normed, axis=0, keepdims=True)
            vec[index + 1 : index + 2, :] += jnp.sum(grad, axis=0, keepdims=True)
            return 0

        lax.fori_loop(0, half // step, rows_body, 0)

    def gather(turn):
        for j in range(2):
            span = at((2 * j + core) * block, block, block)
            b.full[turn % 2, span, :] = b.state[pl.ds(j * block, block), :].astype(BF)
            exchange_start(turn, j)

    def store_chunks(where, matrix, chunk_of, previous):
        if previous is not None:
            previous.wait()
        stage = b.stage

        def body(i, _):
            chunk_of(i, at(i * summing.rows, summing.rows, summing.rows))
            return 0

        lax.fori_loop(0, per_matrix, body, 0)
        copy = pltpu.make_async_copy(
            stage, where.at[pl.ds(matrix * per_matrix, per_matrix)], b.stage_sem.at[0]
        )
        copy.start()
        return copy

    def into_stage(i, value, columns=slice(None)):
        b.stage[i, :, columns] = value.astype(BF)

    state_copy = pltpu.make_async_copy(r.grad_in, b.state, b.misc_sem.at[0])
    state_copy.start()
    slots.load((DOWN, 1), r.foreign_weights.at[1, 2])
    slots.load((SLOPE, 1), r.mats.at[1, 7])
    slots.load((ACT, 1), r.mats.at[1, 5])
    slots.load(ROWS, r.mats.at[1, 3])
    state_copy.wait()
    gather(0)
    pending = None

    for layer in (1, 0):
        base = 0 if layer == 1 else 3
        turn = 0 if layer == 1 else 2
        exchange_wait(turn)
        full = b.full.at[turn % 2]
        normed_copy = pltpu.make_async_copy(r.norms.at[layer, 1], b.normed, b.misc_sem.at[1])
        normed_copy.start()
        inverse_copy = pltpu.make_async_copy(r.inverses.at[layer, 1], b.inverse, b.misc_sem.at[2])
        inverse_copy.start()
        for part in (1, 0):
            down, slope = slots.get((DOWN, part)), slots.get((SLOPE, part))
            dpre = b.dpre.at[part]

            def slope_body(i, _, down=down, slope=slope, dpre=dpre):
                rows = at(i * 256, 256, 256)
                dpre[rows, :] = (mm_cols(full[rows, :], down[...]) * slope[rows, :].astype(F32)).astype(BF)
                return 0

            lax.fori_loop(0, length // 256, slope_body, 0)
            slots.drop((DOWN, part), (SLOPE, part))
            if part == 1:
                slots.load((DOWN, 0), r.w_down.at[layer])
                slots.load((SLOPE, 0), r.mats.at[layer, 6])
            else:
                slots.load((UP, 0), r.w_up.at[layer])
            act, n_full = slots.get((ACT, part)), slots.get(ROWS)
            where = o.foreign if part == 1 else o.own

            def down_chunk(i, rows, act=act):
                into_stage(i, mm_rows(act[:, rows], full[...]))

            def up_chunk(i, rows, n_full=n_full, dpre=dpre):
                into_stage(i, mm_rows(n_full[:, rows], dpre[...]))

            pending = store_chunks(where, base, down_chunk, pending)
            slots.drop((ACT, part))
            if part == 1:
                slots.load((ACT, 0), r.mats.at[layer, 4])
            else:
                slots.load((UP, 1), r.foreign_weights.at[layer, 1])
            pending = store_chunks(where, base + 1, up_chunk, pending)
            if part == 1:
                pending.wait()
                pending = None
                summing.ready = (base + 2) * per_matrix
                summing.feed()
            if layer == 0:
                summing.advance()
        slots.drop(ROWS)
        pending.wait()
        pending = None
        summing.advance()
        ups = [slots.get((UP, 0)), slots.get((UP, 1))]

        def up_partial(span, ups=ups):
            return mm_cols(b.dpre[0, span, :], ups[0][...]) + mm_cols(b.dpre[1, span, :], ups[1][...])

        scatter(turn, up_partial)
        slots.drop((UP, 0), (UP, 1))
        slots.load((QKVA, 1), r.mats.at[layer, 2])
        slots.load((WATTN, 1), r.foreign_weights.at[layer, 0])
        slots.load(ROWS, r.mats.at[layer, 0])
        slots.load((QKVA, 0), r.mats.at[layer, 1])
        slots.load((WATTN, 0), r.w_attn.at[layer])
        norm_back(turn, layer, 1, normed_copy, inverse_copy, False)
        gather(turn + 1)
        normed_copy = pltpu.make_async_copy(r.norms.at[layer, 0], b.normed, b.misc_sem.at[1])
        normed_copy.start()
        inverse_copy = pltpu.make_async_copy(r.inverses.at[layer, 0], b.inverse, b.misc_sem.at[2])
        inverse_copy.start()
        exchange_wait(turn + 1)
        full = b.full.at[(turn + 1) % 2]
        part_cols = width // 4
        for part in (1, 0):
            wattn, qkva = slots.get((WATTN, part)), slots.get((QKVA, part))
            dqkv = b.dpre.at[part]

            def att_body(i, _, wattn=wattn):
                rows = at(i * 256, 256, 256)
                b.grad_att[rows, :] = mm(full[rows, :], wattn[:, 3 * part_cols :]).astype(BF)
                return 0

            lax.fori_loop(0, length // 256, att_body, 0)
            lse_ref = r.lse.at[layer]
            attend_part_back(
                layer == 0,
                b.grad_att,
                qkva,
                lambda pair, rows, part=part, lse_ref=lse_ref: lse_ref[part, pair, :, rows],
                r.bias,
                dqkv,
                b.dk,
                b.dv,
            )
            summing.advance()
            n_full = slots.get(ROWS)

            def attn_chunk(i, rows, n_full=n_full, dqkv=dqkv, qkva=qkva):
                into_stage(i, mm_rows(n_full[:, rows], dqkv[:, : 3 * part_cols]), slice(0, 3 * part_cols))
                into_stage(i, mm_rows(full[:, rows], qkva[:, 3 * part_cols :]), slice(3 * part_cols, None))

            pending = store_chunks(o.foreign if part == 1 else o.own, base + 2, attn_chunk, pending)
        slots.drop((QKVA, 0), (QKVA, 1), ROWS)
        pending.wait()
        pending = None
        summing.ready = (base + 3) * per_matrix
        summing.feed()
        if layer == 1:
            slots.load((DOWN, 1), r.foreign_weights.at[0, 2])
            slots.load((SLOPE, 1), r.mats.at[0, 7])
            slots.load((ACT, 1), r.mats.at[0, 5])
        summing.advance()
        wattns = [slots.get((WATTN, 0)), slots.get((WATTN, 1))]

        def attn_partial(span, wattns=wattns):
            cols = slice(0, 3 * part_cols)
            return mm_cols(b.dpre[0, span, cols], wattns[0][:, cols]) + mm_cols(
                b.dpre[1, span, cols], wattns[1][:, cols]
            )

        scatter(turn + 1, attn_partial)
        slots.drop((WATTN, 0), (WATTN, 1))
        if layer == 1:
            slots.load(ROWS, r.mats.at[0, 3])
        norm_back(turn + 1, layer, 0, normed_copy, inverse_copy, layer == 0)
        if layer == 1:
            gather(turn + 2)

    other = at((1 - chip) * block, block, block)
    mine = at(chip * block, block, block)
    b.rows_send[...] = b.state[other, :].astype(BF)
    rows_copy = remote(b.rows_send, b.rows_recv, 16, {"tensor": flip(tensor, 2)})
    rows_copy.start()
    small = jnp.zeros(r.sel.shape[:1] + (width,), F32)
    for i in range(8):
        small = small + r.sel[:, i : i + 1] * vec[i : i + 1, :]
    b.small_buf[0, 0] = small

    def small_copy(i):
        return pltpu.make_async_remote_copy(
            src_ref=b.small_buf.at[0, i],
            dst_ref=b.small_buf.at[1, i],
            send_sem=b.small_send.at[i],
            recv_sem=b.small_recv.at[i],
            device_id=partners[i],
            device_id_type=MESH,
        )

    small_copy(0).start()
    for i in range(len(partners)):
        summing.advance()
        small_copy(i).wait()
        total = b.small_buf[0, i] + b.small_buf[1, i]
        if i + 1 < len(partners):
            b.small_buf[0, i + 1] = total
            small_copy(i + 1).start()
        else:
            o.small_out[...] = total
    rows_copy.wait()
    o.frames_grad[chip] = b.state[mine, :]
    o.frames_grad[1 - chip] = b.rows_recv[...].astype(F32)
    summing.drain()


ROWS, DOWN, SLOPE, ACT, UP, QKVA, WATTN = range(7)


class BackIn(NamedTuple):
    grad_in: Any
    mats: Any
    norms: Any
    inverses: Any
    foreign_weights: Any
    w_attn: Any
    w_up: Any
    w_down: Any
    gains: Any
    sel: Any
    bias: Any
    lse: Any


class BackOut(NamedTuple):
    total: Any
    own: Any
    foreign: Any
    landed: Any
    small_out: Any
    frames_grad: Any


class BackScratch(NamedTuple):
    slots: Any
    dpre: Any
    full: Any
    rs_send: Any
    rs_recv: Any
    state: Any
    keep: Any
    normed: Any
    inverse: Any
    stage: Any
    dk: Any
    dv: Any
    grad_att: Any
    vec: Any
    rows_send: Any
    rows_recv: Any
    small_buf: Any
    acc: Any
    seg: Any
    y_view: Any
    own_view: Any
    slot_sem: Any
    misc_sem: Any
    stage_sem: Any
    ex_send: Any
    ex_recv: Any
    small_send: Any
    small_recv: Any
    send_sem: Any
    recv_sem: Any
    copy_sem: Any
    view_sem: Any


def backward(inputs, size):
    half, width = inputs.grad_in.shape
    length = 2 * half
    block = length // 4
    bits = dp_bits(size)
    rows = 256
    matrices = 6
    chunks = matrices * length // rows
    stages = 2 * len(bits) + 1
    ring = min(chunks, 2 * len(bits) + 2)
    steps = halvings(bits, rows, width)
    small_rows = inputs.sel.shape[0]
    exchanges = len(bits) + 2
    whole = jax.ShapeDtypeStruct((chunks, rows, width), BF)
    dma = pltpu.SemaphoreType.DMA
    shapes = BackScratch(
        slots=pltpu.VMEM((5, length, width), BF),
        dpre=pltpu.VMEM((2, length, width), BF),
        full=pltpu.VMEM((2, length, width), BF),
        rs_send=pltpu.VMEM((half, width), BF),
        rs_recv=pltpu.VMEM((2, half, width), BF),
        state=pltpu.VMEM((half, width), F32),
        keep=pltpu.VMEM((half, width), F32),
        normed=pltpu.VMEM((half, width), F32),
        inverse=pltpu.VMEM((half, LANES), F32),
        stage=pltpu.VMEM((length // rows, rows, width), BF),
        dk=pltpu.VMEM((length, LANES), F32),
        dv=pltpu.VMEM((length, LANES), F32),
        grad_att=pltpu.VMEM((length, width // 4), BF),
        vec=pltpu.VMEM((8, width), F32),
        rows_send=pltpu.VMEM((block, width), BF),
        rows_recv=pltpu.VMEM((block, width), BF),
        small_buf=pltpu.VMEM((2, exchanges, small_rows, width), F32),
        acc=pltpu.VMEM((ring, rows, width), BF),
        seg=pltpu.VMEM((chunks,) + steps[-1][:2], BF),
        y_view=pltpu.VMEM((rows, width), BF),
        own_view=pltpu.VMEM((rows, width), BF),
        slot_sem=dma((5,)),
        misc_sem=dma((3,)),
        stage_sem=dma((1,)),
        ex_send=dma((17,)),
        ex_recv=dma((17,)),
        small_send=dma((exchanges,)),
        small_recv=dma((exchanges,)),
        send_sem=dma((stages, chunks)),
        recv_sem=dma((stages, chunks)),
        copy_sem=dma((chunks,)),
        view_sem=dma((2,)),
    )
    scratch = list(shapes)
    scratch += [pltpu.VMEM((ring,) + step[:2], BF) for step in steps]
    any_spec = pl.BlockSpec(memory_space=pl.ANY)
    vmem_spec = pl.BlockSpec(memory_space=pltpu.VMEM)
    outs = pl.pallas_call(
        functools.partial(back_kernel, bits),
        in_specs=[any_spec] * 8 + [vmem_spec] * 4,
        out_specs=[any_spec] * 4 + [vmem_spec] * 2,
        out_shape=[whole] * 4
        + [
            jax.ShapeDtypeStruct((small_rows, width), F32),
            jax.ShapeDtypeStruct((2, block, width), F32),
        ],
        scratch_shapes=scratch,
        compiler_params=pltpu.CompilerParams(
            vmem_limit_bytes=VMEM_BYTES, collective_id=1, has_side_effects=True
        ),
        name="backward",
    )(*inputs)
    total, small, frames_grad = outs[0], outs[4], outs[5]
    return total.reshape(matrices, length, width), small, frames_grad


class Fetching:
    SKEW = 2
    STAGES = 3

    def __init__(self, sources, targets, send_sem, recv_sem):
        self.sources, self.targets = sources, targets
        self.send_sem, self.recv_sem = send_sem, recv_sem
        self.dp = lax.axis_index("dp")
        self.tensor = lax.axis_index("tensor")
        self.half = sources[0].shape[0] // 2
        self.items = 2 * len(sources)
        self.step = 0

    def copies(self, stage, item):
        pieces = []
        for sub in range(2):
            first_bit = 1 + sub
            low = lax.rem(self.dp // first_bit, 2)
            high = lax.rem(self.dp // (3 - first_bit), 2)
            span = self.half // 2
            base = (item % 2) * self.half + sub * span
            quarter = span // 4
            if stage < 2:
                rows = at(base + (2 * high + low) * quarter, quarter, quarter)
            else:
                rows = at(base + high * 2 * quarter, 2 * quarter, 2 * quarter)
            target = self.targets[item // 2].at[rows]
            source = self.sources[item // 2].at[rows] if stage == 0 else target
            if stage == 0:
                device = {"tensor": flip(self.tensor, 2)}
            else:
                device = {"dp": flip(self.dp, first_bit if stage == 1 else 3 - first_bit)}
            pieces.append(
                pltpu.make_async_remote_copy(
                    src_ref=source,
                    dst_ref=target,
                    send_sem=self.send_sem.at[stage, item, sub],
                    recv_sem=self.recv_sem.at[stage, item, sub],
                    device_id=device,
                    device_id_type=MESH,
                )
            )
        return pieces

    def advance(self):
        step = self.step
        for stage in range(self.STAGES, 0, -1):
            item = step - self.SKEW * stage
            if 0 <= item < self.items:
                for copy in self.copies(stage - 1, item):
                    copy.wait_recv()
                if stage < self.STAGES:
                    for copy in self.copies(stage, item):
                        copy.start()
        if step < self.items:
            for copy in self.copies(0, step):
                copy.start()
        self.step += 1

    def need(self, matrix):
        while self.step <= 2 * matrix + 1 + self.SKEW * self.STAGES:
            self.advance()

    def drain(self):
        self.need(len(self.sources) - 1)
        for item in range(self.items):
            for stage in range(self.STAGES):
                for copy in self.copies(stage, item):
                    copy.wait_send()


def forward_kernel(bits, *refs):
    r, refs = ForwardIn(*refs[: len(ForwardIn._fields)]), refs[len(ForwardIn._fields) :]
    o, refs = ForwardOut(*refs[: len(ForwardOut._fields)]), refs[len(ForwardOut._fields) :]
    b = ForwardScratch(*refs)
    dp = lax.axis_index("dp")
    tensor = lax.axis_index("tensor")
    chip = tensor // 2
    core = lax.rem(tensor, 2)
    half, width = b.state.shape
    length = 2 * half
    block = length // 4
    part_cols = width // 4
    core_partner = {"tensor": flip(tensor, 1)}
    chip_partner = {"tensor": flip(tensor, 2)}
    partners = [core_partner, chip_partner] + [{"dp": flip(dp, bit)} for bit in bits[:2]]

    barrier = pltpu.get_barrier_semaphore()
    for partner in partners:
        pl.semaphore_signal(barrier, inc=1, device_id=partner, device_id_type=MESH)
    pl.semaphore_wait(barrier, len(partners))

    def remote(source, target, sem, device):
        return pltpu.make_async_remote_copy(
            src_ref=source,
            dst_ref=target,
            send_sem=b.ex_send.at[sem],
            recv_sem=b.ex_recv.at[sem],
            device_id=device,
            device_id_type=MESH,
        )

    def local(source, target, sem):
        return pltpu.make_async_copy(source, target, b.local_sem.at[sem])

    frames_copy = remote(r.frames.at[1 - chip], b.frames_got, 16, chip_partner)
    frames_copy.start()
    own_copy = local(r.frames.at[chip], b.frames_own, 0)
    own_copy.start()
    slots = Slots(b.slots, b.slot_sem)
    slots.load((WATTN, 0), r.w_attn.at[0])
    sources, targets = [], []
    for layer in range(2):
        sources += [r.w_attn.at[layer], r.w_up.at[layer], r.w_down.at[layer]]
        targets += [o.foreign_weights.at[layer, i] for i in range(3)]
    fetching = Fetching(sources, targets, b.send_sem, b.recv_sem)
    fetching.advance()
    fetching.advance()
    own_copy.wait()
    frames_copy.wait()
    b.state[at(chip * block, block, block), :] = b.frames_own[...].astype(F32)
    b.state[at((1 - chip) * block, block, block), :] = b.frames_got[...].astype(F32)
    grad_copy = remote(r.out_grad.at[1 - chip], b.grad_got, 17, chip_partner)
    grad_copy.start()
    grad_own_copy = local(r.out_grad.at[chip], b.grad_own, 0)
    grad_own_copy.start()

    def exchange_copies(turn):
        full = b.full.at[turn % 2]
        spans = [at((2 * j + core) * block, block, block) for j in range(2)]
        return [remote(full.at[s], full.at[s], 4 * turn + j, core_partner) for j, s in enumerate(spans)]

    def scatter(turn, partial):
        copies = [
            remote(
                b.rs_send.at[pl.ds(j * block, block)],
                b.rs_recv.at[turn % 2, pl.ds(j * block, block)],
                4 * turn + 2 + j,
                core_partner,
            )
            for j in range(2)
        ]
        for j in range(2):
            span = at((2 * j + 1 - core) * block, block, block)
            b.rs_send[pl.ds(j * block, block), :] = partial(span).astype(BF)
            copies[j].start()
        for j in range(2):
            span = at((2 * j + core) * block, block, block)
            b.keep[pl.ds(j * block, block), :] = partial(span)
        for copy in copies:
            copy.wait()

    norm_copies = []

    def norm(turn, layer, which, add):
        for copy in norm_copies:
            copy.wait()
        norm_copies.clear()
        gain = r.gains[2 * layer + which : 2 * layer + which + 1, :]
        shift = r.shifts[2 * layer + which : 2 * layer + which + 1, :]
        step = 128
        copies = exchange_copies(turn)
        for j in range(2):

            def rows_body(i, _, j=j):
                span = at(j * block + i * step, step, step)
                state = b.state[span, :]
                if add:
                    state = state + (b.keep[span, :] + b.rs_recv[(turn - 1) % 2, span, :].astype(F32))
                    b.state[span, :] = state
                centred = state - jnp.mean(state, axis=-1, keepdims=True)
                variance = jnp.mean(centred * centred, axis=-1, keepdims=True)
                inverse = lax.rsqrt(variance + 1e-05)
                normed = centred * inverse
                b.normed[span, :] = normed
                b.inverse[span, :] = jnp.broadcast_to(inverse, (step, LANES))
                b.full[turn % 2, at((2 * j + core) * block + i * step, step, step), :] = (
                    normed * gain + shift
                ).astype(BF)
                return 0

            lax.fori_loop(0, block // step, rows_body, 0)
            copies[j].start()
        norm_copies.append(local(b.normed, o.norms.at[layer, which], 1))
        norm_copies.append(local(b.inverse, o.inverses.at[layer, which], 2))
        for copy in norm_copies:
            copy.start()
        for copy in copies:
            copy.wait()

    saves = []

    def save(source, target, sem):
        copy = local(source, target, sem)
        copy.start()
        saves.append(copy)

    def settle():
        for copy in saves:
            copy.wait()
        saves.clear()

    for layer in range(2):
        turn = 2 * layer
        norm(turn, layer, 0, layer == 1)
        full = b.full.at[turn % 2]
        settle()
        save(full, o.mats.at[layer, 0], 3)
        fetching.advance()
        for part in range(2):
            if part == 1:
                fetching.need(3 * layer)
                slots.load((WATTN, 1), o.foreign_weights.at[layer, 0])
            attend_part(
                layer == 0, full, slots.get((WATTN, part)), r.bias, b.acts.at[part], o.lse.at[layer, part]
            )
            save(b.acts.at[part], o.mats.at[layer, 1 + part], 4 + part)
            if part == 0:
                slots.load((UP, 0), r.w_up.at[layer])
                slots.load((DOWN, 0), r.w_down.at[layer])
            fetching.advance()
        weights = [slots.get((WATTN, part)) for part in range(2)]

        def out_partial(span, weights=weights):
            cols = slice(3 * part_cols, None)
            return mm_cols(b.acts[0, span, cols], weights[0][:, cols]) + mm_cols(
                b.acts[1, span, cols], weights[1][:, cols]
            )

        scatter(turn, out_partial)
        slots.drop((WATTN, 0), (WATTN, 1))
        fetching.advance()
        turn += 1
        norm(turn, layer, 1, True)
        full = b.full.at[turn % 2]
        settle()
        save(full, o.mats.at[layer, 3], 3)
        fetching.advance()
        for part in range(2):
            if part == 1:
                fetching.need(3 * layer + 1)
                slots.load((UP, 1), o.foreign_weights.at[layer, 1])
            up = slots.get((UP, part))

            def up_body(i, _, part=part, up=up, full=full):
                rows = at(i * 256, 256, 256)
                for first in range(0, width, 256):
                    cols = pl.ds(first, 256)
                    active, slope = gelu_parts(mm(full[rows, :], up[:, cols]))
                    b.acts[part, rows, cols] = active.astype(BF)
                    b.slope[part, rows, cols] = slope.astype(BF)
                return 0

            lax.fori_loop(0, length // 256, up_body, 0)
            save(b.acts.at[part], o.mats.at[layer, 4 + part], 4 + part)
            save(b.slope.at[part], o.mats.at[layer, 6 + part], 6 + part)
            slots.drop((UP, part))
            if part == 0 and layer == 0:
                slots.load((WATTN, 0), r.w_attn.at[1])
            fetching.advance()
        fetching.need(3 * layer + 2)
        slots.load((DOWN, 1), o.foreign_weights.at[layer, 2])
        downs = [slots.get((DOWN, part)) for part in range(2)]

        def down_partial(span, downs=downs):
            return mm(b.acts[0, span, :], downs[0][...]) + mm(b.acts[1, span, :], downs[1][...])

        scatter(turn, down_partial)
        slots.drop((DOWN, 0), (DOWN, 1))
        if layer == 0:
            fetching.advance()

    for j in range(2):
        span = pl.ds(j * block, block)
        total = b.state[span, :] + (b.keep[span, :] + b.rs_recv[1, span, :].astype(F32))
        b.hidden[j] = total.astype(BF)
    hidden_copy = remote(b.hidden.at[1 - chip], b.hidden_got, 18, chip_partner)
    hidden_copy.start()
    grad_own_copy.wait()
    grad_copy.wait()
    o.grad_in[at(chip * block, block, block), :] = b.grad_own[...].astype(F32)
    o.grad_in[at((1 - chip) * block, block, block), :] = b.grad_got[...].astype(F32)
    fetching.drain()
    settle()
    for copy in norm_copies:
        copy.wait()
    hidden_copy.wait()
    o.hidden_out[chip] = b.hidden[chip]
    o.hidden_out[1 - chip] = b.hidden_got[...]


class ForwardIn(NamedTuple):
    frames: Any
    out_grad: Any
    w_attn: Any
    w_up: Any
    w_down: Any
    gains: Any
    shifts: Any
    bias: Any


class ForwardOut(NamedTuple):
    mats: Any
    norms: Any
    inverses: Any
    foreign_weights: Any
    lse: Any
    grad_in: Any
    hidden_out: Any


class ForwardScratch(NamedTuple):
    slots: Any
    acts: Any
    slope: Any
    full: Any
    rs_send: Any
    rs_recv: Any
    state: Any
    keep: Any
    normed: Any
    inverse: Any
    frames_own: Any
    frames_got: Any
    grad_own: Any
    grad_got: Any
    hidden: Any
    hidden_got: Any
    slot_sem: Any
    local_sem: Any
    ex_send: Any
    ex_recv: Any
    send_sem: Any
    recv_sem: Any


def forward(inputs, size):
    block, width = inputs.frames.shape[1:]
    half, length = 2 * block, 4 * block
    bits = dp_bits(size)
    dma = pltpu.SemaphoreType.DMA
    rows = pltpu.VMEM((block, width), BF)
    scratch = ForwardScratch(
        slots=pltpu.VMEM((5, length, width), BF),
        acts=pltpu.VMEM((2, length, width), BF),
        slope=pltpu.VMEM((2, length, width), BF),
        full=pltpu.VMEM((2, length, width), BF),
        rs_send=pltpu.VMEM((half, width), BF),
        rs_recv=pltpu.VMEM((2, half, width), BF),
        state=pltpu.VMEM((half, width), F32),
        keep=pltpu.VMEM((half, width), F32),
        normed=pltpu.VMEM((half, width), F32),
        inverse=pltpu.VMEM((half, LANES), F32),
        frames_own=rows,
        frames_got=rows,
        grad_own=rows,
        grad_got=rows,
        hidden=pltpu.VMEM((2, block, width), BF),
        hidden_got=rows,
        slot_sem=dma((5,)),
        local_sem=dma((8,)),
        ex_send=dma((19,)),
        ex_recv=dma((19,)),
        send_sem=dma((3, 12, 2)),
        recv_sem=dma((3, 12, 2)),
    )
    out_shape = ForwardOut(
        mats=jax.ShapeDtypeStruct((2, 8, length, width), BF),
        norms=jax.ShapeDtypeStruct((2, 2, half, width), F32),
        inverses=jax.ShapeDtypeStruct((2, 2, half, LANES), F32),
        foreign_weights=jax.ShapeDtypeStruct((2, 3, length, width), BF),
        lse=jax.ShapeDtypeStruct((2, 2, width // (4 * LANES), 8, length), F32),
        grad_in=jax.ShapeDtypeStruct((half, width), F32),
        hidden_out=jax.ShapeDtypeStruct((2, block, width), BF),
    )
    any_spec = pl.BlockSpec(memory_space=pl.ANY)
    vmem_spec = pl.BlockSpec(memory_space=pltpu.VMEM)
    outs = pl.pallas_call(
        functools.partial(forward_kernel, bits),
        in_specs=[any_spec] * 5 + [vmem_spec] * 3,
        out_specs=[any_spec] * 4 + [vmem_spec] * 3,
        out_shape=list(out_shape),
        scratch_shapes=list(scratch),
        compiler_params=pltpu.CompilerParams(
            vmem_limit_bytes=VMEM_BYTES, collective_id=2, has_side_effects=True
        ),
        name="forward",
    )(*inputs)
    return ForwardOut(*outs)


def per_device(
    frames, lengths, codebook, ln_gain, ln_bias, ada_scale, ada_shift, w_qkv, w_out, w_up, w_down, out_grad
):
    chip = lax.axis_index("tensor") // 2
    length = frames.shape[1] * lax.axis_size("tensor")
    size = lax.axis_size("dp")

    def pick(pair):
        return jnp.where(chip == 0, pair[0], pair[1])

    bias = jnp.where(jnp.arange(length) < pick(lengths), 0.0, -1e30).astype(F32)
    sections = ada_scale.shape[0]
    chosen = (jnp.arange(sections) == pick(codebook))[:, None, None]
    gains = jnp.concatenate([ln_gain, jnp.sum(jnp.where(chosen, ada_scale, 0.0), axis=0)])
    shifts = jnp.concatenate([ln_bias, jnp.sum(jnp.where(chosen, ada_shift, 0.0), axis=0)])
    w_attn = jnp.concatenate(
        [w_qkv.reshape(w_qkv.shape[0], w_qkv.shape[1], -1), w_out.transpose(0, 2, 1)], axis=2
    )
    ahead = forward(
        ForwardIn(frames, out_grad, w_attn, w_up, w_down, gains, shifts, bias[None, :]), size
    )
    unit = jnp.eye(8, dtype=F32)
    sel = jnp.concatenate(
        [unit[0:3:2], unit[1:4:2]]
        + [jnp.where(chosen, rows[None], 0.0).reshape(2 * sections, 8) for rows in (unit[4:7:2], unit[5:8:2])]
    )
    total, small, frames_grad = backward(
        BackIn(
            ahead.grad_in,
            ahead.mats,
            ahead.norms,
            ahead.inverses,
            ahead.foreign_weights,
            w_attn,
            w_up,
            w_down,
            gains,
            sel,
            bias[:, None],
            ahead.lse,
        ),
        size,
    )
    total = total.reshape((2, 3) + total.shape[1:])
    wide = w_qkv.shape[2] * w_qkv.shape[3]
    return (
        ahead.hidden_out,
        frames_grad,
        small[0:2],
        small[2:4],
        small[4 : 4 + 2 * sections].reshape(ada_scale.shape),
        small[4 + 2 * sections :].reshape(ada_scale.shape),
        total[::-1, 2, :, :wide].reshape(w_qkv.shape).astype(F32),
        total[::-1, 2, :, wide:].transpose(0, 2, 1).astype(F32),
        total[::-1, 1].astype(F32),
        total[::-1, 0].astype(F32),
    )


def solution(mesh):
    placed = (
        P("dp", "tensor", None),
        P("dp"),
        P("dp"),
        P(),
        P(),
        P(),
        P(),
        P(None, None, None, "tensor"),
        P(None, "tensor", None),
        P(None, None, "tensor"),
        P(None, "tensor", None),
        P("dp", "tensor", None),
    )
    return jax.shard_map(
        per_device,
        mesh=mesh,
        in_specs=placed,
        out_specs=(
            P("dp", "tensor", None),
            P("dp", "tensor", None),
            P(),
            P(),
            P(),
            P(),
            P(None, None, None, "tensor"),
            P(None, "tensor", None),
            P(None, None, "tensor"),
            P(None, "tensor", None),
        ),
        check_vma=False,
    )
```

time: 1140 us -> 657 us (0.58)
  Pallas kernels: 0 us -> 585 us
  waiting for transfers between devices: 443 us -> 0 us
  matrix products: 324 us -> 0 us
  other arithmetic: 172 us -> 22.1 us
  starting transfers between devices: 106 us -> 0 us
  local copies, waits for them, and re-layouts: 65.9 us -> 35.7 us
  between operations: 21.2 us -> 3.78 us
    pallas_call x0 -> x2, Pallas kernels: none -> 585 us  [the longest x1 396 us: backward(): pl.pallas_call(functools.partial(back_kernel, bits), in_specs=[any_spec]...]
    ppermute x100 -> x0, waiting for transfers between devices: 330 us -> none  [the longest x64 259 us: swap_dp(): return lax.ppermute(x, 'dp', pairs)]
    dot_general x96 -> x0, matrix products: 324 us -> none  [the longest x16 74.2 us: mm(): return jnp.dot(left, right, preferred_element_type=F32)]
    psum x1 -> x0, waiting for transfers between devices: 113 us -> none  [per_device(): small = lax.psum(small, ('dp', 'tensor'))]
    ppermute x100 -> x0, starting transfers between devices: 106 us -> none  [the longest x64 77.9 us: swap_dp(): return lax.ppermute(x, 'dp', pairs)]
    convert_element_type x38 -> x4, other arithmetic: 76.3 us -> 12.8 us  [the longest x1 6.79 us: per_device(): total[::-1, 0].astype(F32)]
    reduce_sum x16 -> x1, other arithmetic: 40.9 us -> 0.97 us  [per_device(): jnp.sum(jnp.where(chosen, ada_shift, 0.0), axis=0)]
    select_n x39 -> x3, other arithmetic: 36.8 us -> 1.52 us  [the longest x2 1.45 us: per_device(): jnp.where(jnp.arange(length) < pick(lengths), 0.0, -1e+30).astype(F32)]
  transfers between devices with their start and end apart: 101 -> 0, of which waited for: 47 -> 0; matrix products, arithmetic and copies ran while one was open for 45% -> 0% of each run, Pallas kernels for 0% -> 0%
where the time goes in v2:
time: 657 us; the launch traced here: 647 us
  Pallas kernels  585 us (89%)
  local copies, waits for them, and re-layouts  35.7 us (5%)
  other arithmetic  22.1 us (3%)
    pallas_call x1, Pallas kernels, backward(): pl.pallas_call(functools.partial(back_kernel, bits), in_specs=[any_spec]...  396 us
    pallas_call x1, Pallas kernels, forward(): pl.pallas_call(functools.partial(forward_kernel, bits), in_specs=[any_spe...  190 us
    unnamed x14, local copies, waits for them, and re-layouts  20.7 us

profile of v2, /device:TPU:0, one launch (start us, length us, event | category | flops | bytes accessed | tf_op | source)
XLA Modules:
  0.0 646.7 jit_solution(3207596806067571798)
XLA Ops:
  0.7 1.3 fusion.4
  3.3 1.3 fusion.5
  5.9 0.1 broadcast_in_dim.74
  6.0 0.1 broadcast_in_dim.75
  6.1 0.6 compare_select_fusion.refs_7_
  6.8 0.1 broadcast_select_fusion.1
  6.9 0.6 pad_maximum_fusion.3.refs_9_
  7.5 1.0 select_reduce_fusion
  8.5 1.3 pad_maximum_fusion.1
  9.8 0.8 fusion.refs_10_
  10.7 2.3 copy.49
  12.9 3.2 copy.48
  16.1 2.8 copy.50
  18.9 4.8 pad_maximum_fusion.refs_2_.refs_5_
  23.7 189.5 %forward.1 = (bf16[2,8,1024,1024]{3,2,1,0:T(8,128)(2,1)}, f32[2,2,512,1024]{3,2,1,0:T(8,128)}, f32[2,2,512,128]{3,2,1,0:T(8,128)}, bf16[2,3,1024,1024]{3,2,1,0:T...) custom-call(bf16[2,256,1024]{2,1,0:T(8,128)(2,1)} %refs_0_.1, ...), custom_call_target="tpu_custom_call" | custom-call | tf_op jit(solution)/shard_map/forward/pallas_call | solution.py:1129
  213.2 395.6 %backward.1 = (bf16[24,256,1024]{2,1,0:T(8,128)(2,1)}, bf16[24,256,1024]{2,1,0:T(8,128)(2,1)}, bf16[24,256,1024]{2,1,0:T(8,128)(2,1)}, bf16[24,256,1024]{2,1,0:T...) custom-call(f32[512,1024]{1,0:T(8,128)} %get-tuple-element.21.refs_0_, ...), custom_call_target="tpu_custom_call" | custom-call | tf_op jit(solution)/shard_map/backward/pallas_call | solution.py:732
  608.8 1.4 fusion.3
  610.3 1.0 fusion.2
  611.2 0.7 reshape.71
  611.9 0.7 reshape.70
  612.6 1.3 slice.65
  613.9 0.5 copy.57
  614.4 1.6 convert_bitcast_fusion
  616.0 2.1 slice.64
  618.1 6.0 slice_bitcast_fusion
  624.1 2.9 copy.56
  627.0 2.2 rev.12
  629.2 3.5 copy.55
  632.7 6.8 %bitcast_convert_fusion = f32[2,1024,1024]{2,1,0:T(8,128)} fusion(bf16[2,1,1024,1024]{3,2,0,1:T(8,128)(2,1)} %get-tuple-element.62), kind=kLoop, calls=%fused_computation.3 | loop fusion | flops 2097152 | bytes 12582912 | tf_op jit(solution)/shard_map/convert_element_type | solution.py:1198
  639.5 4.4 bitcast_convert_fusion.1
  644.0 1.0 copy.62
  644.9 1.3 copy.63
  (16 shorter events, 0.1 us)
Async XLA Ops:
  632.7 6.8 %copy-start = (bf16[2,1,1024,1024]{3,2,0,1:T(8,128)(2,1)S(1)}, bf16[2,1,1024,1024]{3,2,0,1:T(8,128)(2,1)}, u32[]{:S(2)}) copy-start(bf16[2,1,1024,1024]{3,2,0,1:T(8,128)(2,1)} %get-tuple-element.63) | copy-start | bytes 12582916
  639.5 4.4 copy-start.2
  639.5 5.4 copy-start.1

commit v3 on v2

--- a/solution.py
+++ b/solution.py
@@ -50,7 +50,7 @@
     return bits
 
 
-def attend_part(causal, n_ref, w_ref, bias_ref, qkva_ref, lse_ref):
+def attend_part(causal, n_ref, w_ref, bias_ref, qkva_ref, lse_ref, between):
     length = n_ref.shape[0]
     part = qkva_ref.shape[1] // 4
     block = length // 4
@@ -63,8 +63,8 @@
 
     lax.fori_loop(0, 4, project, 0)
 
-    def pair_body(pair, _):
-        q_cols, k_cols, v_cols, a_cols = [at(i * part + pair * LANES, LANES, LANES) for i in range(4)]
+    for pair in range(part // LANES):
+        q_cols, k_cols, v_cols, a_cols = [pl.ds(i * part + pair * LANES, LANES) for i in range(4)]
         for first in range(0, length, block):
             rows = pl.ds(first, block)
             reach = first + block if causal else length
@@ -79,9 +79,10 @@
             for which in range(2):
                 scores = mm_cols(jnp.where(head == which, queries, jnp.zeros_like(queries)), keys) + bias
                 if causal:
-                    query_at = first + lax.broadcasted_iota(jnp.int32, scores.shape, 0)
-                    key_at = lax.broadcasted_iota(jnp.int32, scores.shape, 1)
-                    scores = jnp.where(key_at <= query_at, scores, -1e30)
+                    query_at = lax.broadcasted_iota(jnp.int32, (block, block), 0)
+                    key_at = lax.broadcasted_iota(jnp.int32, (block, block), 1)
+                    last = jnp.where(key_at <= query_at, scores[:, first:], -1e30)
+                    scores = jnp.concatenate([scores[:, :first], last], axis=1) if first else last
                 row_max = jnp.max(scores, axis=-1, keepdims=True)
                 raised = jnp.exp(scores - row_max)
                 total = jnp.sum(raised, axis=-1, keepdims=True)
@@ -92,20 +93,18 @@
             square = lax.broadcasted_iota(jnp.int32, (8, LANES), 1)
             pick = (square == lax.broadcasted_iota(jnp.int32, (8, LANES), 0)).astype(F32)
             lse_ref[pair, :, rows] = mm_cols(pick, stats, HIGH)
-        return 0
-
-    lax.fori_loop(0, part // LANES, pair_body, 0)
-
-
-def attend_part_back(causal, grad_att_ref, qkva_ref, lse_of, bias_ref, dqkv_ref, dk_ref, dv_ref):
+        between()
+
+
+def attend_part_back(causal, grad_att_ref, qkva_ref, lse_of, bias_ref, dqkv_ref, dk_ref, dv_ref, between):
     length = qkva_ref.shape[0]
     part = qkva_ref.shape[1] // 4
     block = length // 4
     scaling = HEAD_DIM ** (-0.5)
 
-    def pair_body(pair, _):
-        q_cols, k_cols, v_cols, a_cols = [at(i * part + pair * LANES, LANES, LANES) for i in range(4)]
-        g_cols = at(pair * LANES, LANES, LANES)
+    for pair in range(part // LANES):
+        q_cols, k_cols, v_cols, a_cols = [pl.ds(i * part + pair * LANES, LANES) for i in range(4)]
+        g_cols = pl.ds(pair * LANES, LANES)
         dk_ref[...] = jnp.zeros_like(dk_ref)
         dv_ref[...] = jnp.zeros_like(dv_ref)
         keys_turned = qkva_ref[:, k_cols].astype(F32).T.astype(BF)
@@ -132,9 +131,10 @@
                 grads_one = jnp.where(head == which, grads, jnp.zeros_like(grads))
                 scores = mm_cols(keys, queries_one) + bias
                 if causal:
-                    key_at = lax.broadcasted_iota(jnp.int32, scores.shape, 0)
-                    query_at = first + lax.broadcasted_iota(jnp.int32, scores.shape, 1)
-                    scores = jnp.where(key_at <= query_at, scores, -1e30)
+                    key_at = lax.broadcasted_iota(jnp.int32, (block, block), 0)
+                    query_at = lax.broadcasted_iota(jnp.int32, (block, block), 1)
+                    last = jnp.where(key_at <= query_at, scores[first:], -1e30)
+                    scores = jnp.concatenate([scores[:first], last], axis=0) if first else last
                 probs = jnp.exp(scores - lse[which : which + 1])
                 grad_probs = mm_cols(values, grads_one)
                 grad_scores = (probs * (grad_probs - delta[which : which + 1])).astype(BF)
@@ -145,14 +145,14 @@
             dqkv_ref[rows, q_cols] = (dq_turned.T * scaling).astype(BF)
         dqkv_ref[:, k_cols] = dk_ref[...].astype(BF)
         dqkv_ref[:, v_cols] = dv_ref[...].astype(BF)
-        return 0
-
-    lax.fori_loop(0, part // LANES, pair_body, 0)
+        between()
 
 
 def gelu_parts(hidden):
     bell = jnp.exp(-0.5 * hidden * hidden)
-    t = 1.0 / (1.0 + 0.23164189 * jnp.abs(hidden))
+    base = 1.0 + 0.23164189 * jnp.abs(hidden)
+    t = pl.reciprocal(base, approx=True)
+    t = t * (2.0 - base * t)
     poly = 0.5307027145
     poly = poly * t - 0.7265760135
     poly = poly * t + 0.7107068705
@@ -183,6 +183,14 @@
             self.held[name][1] = None
         return self.buffers.at[slot]
 
+    def reserve(self, name):
+        slot = self.free.pop(0)
+        self.held[name] = [slot, None]
+        return self.buffers.at[slot]
+
+    def rename(self, old, new):
+        self.held[new] = self.held.pop(old)
+
     def drop(self, *names):
         for name in names:
             self.free.append(self.held.pop(name)[0])
@@ -191,9 +199,9 @@
 class Summing:
     AHEAD = 4
 
-    def __init__(self, bits, own, foreign, landed, out, acc, seg, y_view, own_view, rbufs, send_sem, recv_sem, copy_sem, view_sem):
-        self.bits, self.own, self.foreign, self.landed, self.out = bits, own, foreign, landed, out
-        self.acc, self.seg, self.y_view, self.own_view, self.rbufs = acc, seg, y_view, own_view, rbufs
+    def __init__(self, bits, own, foreign, outs, acc, seg, own_view, rbufs, send_sem, recv_sem, copy_sem, view_sem):
+        self.bits, self.own, self.foreign, self.outs = bits, own, foreign, outs
+        self.acc, self.seg, self.own_view, self.rbufs = acc, seg, own_view, rbufs
         self.send_sem, self.recv_sem, self.copy_sem, self.view_sem = send_sem, recv_sem, copy_sem, view_sem
         self.chunks, self.rows, self.columns = own.shape
         self.ring = acc.shape[0]
@@ -203,8 +211,9 @@
         self.step = 0
         self.started = 0
         self.ready = 0
+        self.sizes = [step[:2] for step in halvings(bits, self.rows, self.columns)]
         row, column = 0, 0
-        self.sizes, self.keep, self.send = [], [], []
+        self.plan = []
         for half_rows, half_columns, bit, by_rows in halvings(bits, self.rows, self.columns):
             flag = lax.rem(self.dp // bit, 2)
             if by_rows:
@@ -214,30 +223,35 @@
                 keep = (row, column + flag * half_columns)
                 send = (row, column + (1 - flag) * half_columns)
             row, column = keep
-            self.sizes.append((half_rows, half_columns))
-            self.keep.append(keep)
-            self.send.append(send)
+            self.plan.append((keep, send, bit))
 
     def region(self, where, size):
         return at(where[0], size[0], 16), at(where[1], size[1], LANES)
 
+    def place(self, c):
+        per_matrix = self.outs[0].shape[1]
+        matrix = c // per_matrix
+        return self.outs[matrix % 3].at[1 - matrix // 3, c % per_matrix]
+
     def copy(self, s, c):
         count = len(self.bits)
+        slot = c % self.ring
         if s == 0:
-            source, target = self.foreign.at[c], self.landed.at[c]
+            source, target = self.foreign.at[c], self.acc.at[slot]
             device = {"tensor": flip(self.tensor, 2)}
         elif s <= count:
             i = s - 1
-            rows, columns = self.region(self.send[i], self.sizes[i])
-            source = self.acc.at[c % self.ring, rows, columns]
-            target = self.rbufs[i].at[c % self.ring]
-            device = {"dp": flip(self.dp, self.bits[i])}
+            _, send, bit = self.plan[i]
+            rows, columns = self.region(send, self.sizes[i])
+            source = self.acc.at[slot, rows, columns]
+            target, device = self.rbufs[i].at[slot], {"dp": flip(self.dp, bit)}
         else:
             i = 2 * count - s
-            rows, columns = self.region(self.keep[i], self.sizes[i])
-            target = self.out.at[c, rows, columns]
+            keep, _, bit = self.plan[i]
+            rows, columns = self.region(keep, self.sizes[i])
+            target = self.place(c).at[rows, columns]
             source = self.seg.at[c] if i == count - 1 else target
-            device = {"dp": flip(self.dp, self.bits[i])}
+            device = {"dp": flip(self.dp, bit)}
         return pltpu.make_async_remote_copy(
             src_ref=source,
             dst_ref=target,
@@ -248,56 +262,49 @@
         )
 
     def seg_copy(self, c):
-        rows, columns = self.region(self.keep[-1], self.sizes[-1])
-        return pltpu.make_async_copy(self.seg.at[c], self.out.at[c, rows, columns], self.copy_sem.at[c])
-
-    def views(self, c):
-        return (
-            pltpu.make_async_copy(self.landed.at[c], self.y_view, self.view_sem.at[0]),
-            pltpu.make_async_copy(self.own.at[c], self.own_view, self.view_sem.at[1]),
-        )
+        rows, columns = self.region(self.plan[-1][0], self.sizes[-1])
+        return pltpu.make_async_copy(self.seg.at[c], self.place(c).at[rows, columns], self.copy_sem.at[c])
+
+    def view(self, c):
+        return pltpu.make_async_copy(self.own.at[c], self.own_view.at[c % 2], self.view_sem.at[c % 2])
 
     def finish(self, s, c):
         count = len(self.bits)
         slot = c % self.ring
+        self.copy(s, c).wait_recv()
         if s == 0:
-            for view in self.views(c):
-                view.wait()
-            if c >= self.ring:
-                for stage in range(1, count + 1):
-                    self.copy(stage, c - self.ring).wait_send()
-            self.acc[slot] = (self.own_view[...].astype(F32) + self.y_view[...].astype(F32)).astype(BF)
-            return
-        self.copy(s, c).wait_recv()
-        if s <= count:
+            self.view(c).wait()
+            self.acc[slot] = (self.own_view[c % 2].astype(F32) + self.acc[slot].astype(F32)).astype(BF)
+        elif s <= count:
             i = s - 1
-            rows, columns = self.region(self.keep[i], self.sizes[i])
+            rows, columns = self.region(self.plan[i][0], self.sizes[i])
             total = self.acc[slot, rows, columns].astype(F32) + self.rbufs[i][slot].astype(F32)
             if s == count:
                 self.seg[c] = total.astype(BF)
                 self.seg_copy(c).start()
+                for stage in range(1, count + 1):
+                    self.copy(stage, c).wait_send()
             else:
                 self.acc[slot, rows, columns] = total.astype(BF)
         elif s == count + 1:
             self.seg_copy(c).wait()
 
     def advance(self):
-        first = self.step
-        if first < self.chunks:
-            self.copy(0, first).wait_recv()
-            for view in self.views(first):
-                view.start()
-        for s in range(self.stages, 0, -1):
-            c = first + 1 - s
+        step = self.step
+        if step < self.chunks:
+            self.view(step).start()
+        for s in range(self.stages - 1, -1, -1):
+            c = step - s
             if 0 <= c < self.chunks:
-                self.finish(s - 1, c)
-                if s < self.stages:
-                    self.copy(s, c).start()
+                self.finish(s, c)
+                if s + 1 < self.stages:
+                    self.copy(s + 1, c).start()
         self.step += 1
         self.feed()
 
     def feed(self):
-        while self.started < min(self.ready, self.step + self.AHEAD):
+        ahead = self.AHEAD if self.step < self.chunks // 2 else 2
+        while self.started < min(self.ready, self.step + ahead):
             self.copy(0, self.started).start()
             self.started += 1
 
@@ -307,7 +314,7 @@
         count = len(self.bits)
         for c in range(self.chunks):
             for s in range(self.stages):
-                if not (1 <= s <= count and c + self.ring < self.chunks):
+                if not 1 <= s <= count:
                     self.copy(s, c).wait_send()
 
 
@@ -341,7 +348,7 @@
 
     slots = Slots(b.slots, b.slot_sem)
     summing = Summing(
-        bits, o.own, o.foreign, o.landed, o.total, b.acc, b.seg, b.y_view, b.own_view,
+        bits, o.own, o.foreign, (o.down, o.up, o.attn), b.acc, b.seg, b.own_view,
         rbufs, b.send_sem, b.recv_sem, b.copy_sem, b.view_sem,
     )
     per_matrix = length // summing.rows
@@ -440,6 +447,10 @@
     def into_stage(i, value, columns=slice(None)):
         b.stage[i, :, columns] = value.astype(BF)
 
+    hidden_copy = remote(r.hidden.at[1 - chip], o.hidden_out.at[chip], 17, {"tensor": flip(tensor, 2)})
+    hidden_copy.start()
+    hidden_own_copy = pltpu.make_async_copy(r.hidden.at[chip], o.hidden_out.at[chip], b.misc_sem.at[3])
+    hidden_own_copy.start()
     state_copy = pltpu.make_async_copy(r.grad_in, b.state, b.misc_sem.at[0])
     state_copy.start()
     slots.load((DOWN, 1), r.foreign_weights.at[1, 2])
@@ -460,14 +471,34 @@
         inverse_copy = pltpu.make_async_copy(r.inverses.at[layer, 1], b.inverse, b.misc_sem.at[2])
         inverse_copy.start()
         for part in (1, 0):
+            where = o.foreign if part == 1 else o.own
+            act, n_full = slots.get((ACT, part)), slots.get(ROWS)
+            dpre = b.dpre.at[part]
+
+            def down_chunk(i, rows, act=act):
+                into_stage(i, mm_rows(act[:, rows], full[...]))
+
+            def up_chunk(i, rows, n_full=n_full, dpre=dpre):
+                into_stage(i, mm_rows(n_full[:, rows], dpre[...]))
+
+            pending = store_chunks(where, base, down_chunk, pending)
+            slots.drop((ACT, part))
+            if part == 1:
+                slots.load((ACT, 0), r.mats.at[layer, 4])
+            else:
+                slots.load((UP, 1), r.foreign_weights.at[layer, 1])
             down, slope = slots.get((DOWN, part)), slots.get((SLOPE, part))
-            dpre = b.dpre.at[part]
 
             def slope_body(i, _, down=down, slope=slope, dpre=dpre):
                 rows = at(i * 256, 256, 256)
                 dpre[rows, :] = (mm_cols(full[rows, :], down[...]) * slope[rows, :].astype(F32)).astype(BF)
                 return 0
 
+            if part == 1:
+                pending.wait()
+                pending = None
+                summing.ready = (base + 1) * per_matrix
+                summing.feed()
             lax.fori_loop(0, length // 256, slope_body, 0)
             slots.drop((DOWN, part), (SLOPE, part))
             if part == 1:
@@ -475,21 +506,6 @@
                 slots.load((SLOPE, 0), r.mats.at[layer, 6])
             else:
                 slots.load((UP, 0), r.w_up.at[layer])
-            act, n_full = slots.get((ACT, part)), slots.get(ROWS)
-            where = o.foreign if part == 1 else o.own
-
-            def down_chunk(i, rows, act=act):
-                into_stage(i, mm_rows(act[:, rows], full[...]))
-
-            def up_chunk(i, rows, n_full=n_full, dpre=dpre):
-                into_stage(i, mm_rows(n_full[:, rows], dpre[...]))
-
-            pending = store_chunks(where, base, down_chunk, pending)
-            slots.drop((ACT, part))
-            if part == 1:
-                slots.load((ACT, 0), r.mats.at[layer, 4])
-            else:
-                slots.load((UP, 1), r.foreign_weights.at[layer, 1])
             pending = store_chunks(where, base + 1, up_chunk, pending)
             if part == 1:
                 pending.wait()
@@ -516,6 +532,7 @@
         slots.load((WATTN, 0), r.w_attn.at[layer])
         norm_back(turn, layer, 1, normed_copy, inverse_copy, False)
         gather(turn + 1)
+        summing.advance()
         normed_copy = pltpu.make_async_copy(r.norms.at[layer, 0], b.normed, b.misc_sem.at[1])
         normed_copy.start()
         inverse_copy = pltpu.make_async_copy(r.inverses.at[layer, 0], b.inverse, b.misc_sem.at[2])
@@ -529,7 +546,9 @@
 
             def att_body(i, _, wattn=wattn):
                 rows = at(i * 256, 256, 256)
-                b.grad_att[rows, :] = mm(full[rows, :], wattn[:, 3 * part_cols :]).astype(BF)
+                cols = slice(3 * part_cols, None)
+                spans = [pl.ds(k * part_cols, part_cols) for k in range(4)]
+                b.grad_att[rows, :] = sum(mm_cols(full[rows, s], wattn[s, cols]) for s in spans).astype(BF)
                 return 0
 
             lax.fori_loop(0, length // 256, att_body, 0)
@@ -543,13 +562,13 @@
                 dqkv,
                 b.dk,
                 b.dv,
+                summing.advance,
             )
-            summing.advance()
             n_full = slots.get(ROWS)
 
             def attn_chunk(i, rows, n_full=n_full, dqkv=dqkv, qkva=qkva):
                 into_stage(i, mm_rows(n_full[:, rows], dqkv[:, : 3 * part_cols]), slice(0, 3 * part_cols))
-                into_stage(i, mm_rows(full[:, rows], qkva[:, 3 * part_cols :]), slice(3 * part_cols, None))
+                into_stage(i, mm_rows(qkva[:, 3 * part_cols :], full[:, rows]), slice(3 * part_cols, None))
 
             pending = store_chunks(o.foreign if part == 1 else o.own, base + 2, attn_chunk, pending)
         slots.drop((QKVA, 0), (QKVA, 1), ROWS)
@@ -577,6 +596,7 @@
         norm_back(turn + 1, layer, 0, normed_copy, inverse_copy, layer == 0)
         if layer == 1:
             gather(turn + 2)
+            summing.advance()
 
     other = at((1 - chip) * block, block, block)
     mine = at(chip * block, block, block)
@@ -609,15 +629,18 @@
         else:
             o.small_out[...] = total
     rows_copy.wait()
+    hidden_copy.wait()
+    hidden_own_copy.wait()
     o.frames_grad[chip] = b.state[mine, :]
     o.frames_grad[1 - chip] = b.rows_recv[...].astype(F32)
     summing.drain()
 
 
-ROWS, DOWN, SLOPE, ACT, UP, QKVA, WATTN = range(7)
+ROWS, DOWN, SLOPE, ACT, UP, QKVA, WATTN, PACK = range(8)
 
 
 class BackIn(NamedTuple):
+    hidden: Any
     grad_in: Any
     mats: Any
     norms: Any
@@ -633,10 +656,12 @@
 
 
 class BackOut(NamedTuple):
-    total: Any
+    down: Any
+    up: Any
+    attn: Any
     own: Any
     foreign: Any
-    landed: Any
+    hidden_out: Any
     small_out: Any
     frames_grad: Any
 
@@ -661,7 +686,6 @@
     small_buf: Any
     acc: Any
     seg: Any
-    y_view: Any
     own_view: Any
     slot_sem: Any
     misc_sem: Any
@@ -685,7 +709,7 @@
     matrices = 6
     chunks = matrices * length // rows
     stages = 2 * len(bits) + 1
-    ring = min(chunks, 2 * len(bits) + 2)
+    ring = min(chunks, max(2 * Summing.AHEAD + len(bits), 2 * len(bits)) + 1)
     steps = halvings(bits, rows, width)
     small_rows = inputs.sel.shape[0]
     exchanges = len(bits) + 2
@@ -711,13 +735,12 @@
         small_buf=pltpu.VMEM((2, exchanges, small_rows, width), F32),
         acc=pltpu.VMEM((ring, rows, width), BF),
         seg=pltpu.VMEM((chunks,) + steps[-1][:2], BF),
-        y_view=pltpu.VMEM((rows, width), BF),
-        own_view=pltpu.VMEM((rows, width), BF),
+        own_view=pltpu.VMEM((2, rows, width), BF),
         slot_sem=dma((5,)),
-        misc_sem=dma((3,)),
+        misc_sem=dma((4,)),
         stage_sem=dma((1,)),
-        ex_send=dma((17,)),
-        ex_recv=dma((17,)),
+        ex_send=dma((18,)),
+        ex_recv=dma((18,)),
         small_send=dma((exchanges,)),
         small_recv=dma((exchanges,)),
         send_sem=dma((stages, chunks)),
@@ -731,10 +754,12 @@
     vmem_spec = pl.BlockSpec(memory_space=pltpu.VMEM)
     outs = pl.pallas_call(
         functools.partial(back_kernel, bits),
-        in_specs=[any_spec] * 8 + [vmem_spec] * 4,
-        out_specs=[any_spec] * 4 + [vmem_spec] * 2,
-        out_shape=[whole] * 4
+        in_specs=[any_spec] * 9 + [vmem_spec] * 4,
+        out_specs=[any_spec] * 6 + [vmem_spec] * 2,
+        out_shape=[jax.ShapeDtypeStruct((2, length // rows, rows, width), BF)] * 3
+        + [whole] * 2
         + [
+            jax.ShapeDtypeStruct((2, block, width), BF),
             jax.ShapeDtypeStruct((small_rows, width), F32),
             jax.ShapeDtypeStruct((2, block, width), F32),
         ],
@@ -744,8 +769,7 @@
         ),
         name="backward",
     )(*inputs)
-    total, small, frames_grad = outs[0], outs[4], outs[5]
-    return total.reshape(matrices, length, width), small, frames_grad
+    return BackOut(*outs)
 
 
 class Fetching:
@@ -853,27 +877,54 @@
     def local(source, target, sem):
         return pltpu.make_async_copy(source, target, b.local_sem.at[sem])
 
-    frames_copy = remote(r.frames.at[1 - chip], b.frames_got, 16, chip_partner)
+    frames_copy = local(r.frames_got, b.frames_got, 3)
     frames_copy.start()
     own_copy = local(r.frames.at[chip], b.frames_own, 0)
     own_copy.start()
+
     slots = Slots(b.slots, b.slot_sem)
-    slots.load((WATTN, 0), r.w_attn.at[0])
+
+    def pack_copies(layer, slot):
+        pairs = []
+        for i in range(3):
+            pairs.append((r.w_qkv.at[layer, i], slot.at[:, pl.ds(i * part_cols, part_cols)]))
+        for k in range(4):
+            span = pl.ds(k * part_cols, part_cols)
+            pairs.append((r.w_out.at[layer, :, span], slot.at[span, pl.ds(3 * part_cols, part_cols)]))
+        return [
+            pltpu.make_async_copy(source, target, b.pack_sem.at[layer, i])
+            for i, (source, target) in enumerate(pairs)
+        ]
+
+    pack_slots = [slots.reserve((WATTN, 0)), slots.reserve(PACK)]
+    packs = [pack_copies(layer, slot) for layer, slot in enumerate(pack_slots)]
+    stores = [
+        pltpu.make_async_copy(slot, o.w_attn.at[layer], b.pack_sem.at[layer, 7])
+        for layer, slot in enumerate(pack_slots)
+    ]
+    for pack in packs:
+        for copy in pack:
+            copy.start()
+    for copy in packs[0]:
+        copy.wait()
+    stores[0].start()
+    stores[0].wait()
     sources, targets = [], []
     for layer in range(2):
-        sources += [r.w_attn.at[layer], r.w_up.at[layer], r.w_down.at[layer]]
+        sources += [o.w_attn.at[layer], r.w_up.at[layer], r.w_down.at[layer]]
         targets += [o.foreign_weights.at[layer, i] for i in range(3)]
     fetching = Fetching(sources, targets, b.send_sem, b.recv_sem)
     fetching.advance()
     fetching.advance()
+    for copy in packs[1]:
+        copy.wait()
+    stores[1].start()
     own_copy.wait()
     frames_copy.wait()
     b.state[at(chip * block, block, block), :] = b.frames_own[...].astype(F32)
     b.state[at((1 - chip) * block, block, block), :] = b.frames_got[...].astype(F32)
-    grad_copy = remote(r.out_grad.at[1 - chip], b.grad_got, 17, chip_partner)
-    grad_copy.start()
+    grad_copy = remote(r.out_grad.at[1 - chip], b.grad_got, 16, chip_partner)
     grad_own_copy = local(r.out_grad.at[chip], b.grad_own, 0)
-    grad_own_copy.start()
 
     def exchange_copies(turn):
         full = b.full.at[turn % 2]
@@ -953,6 +1004,10 @@
     for layer in range(2):
         turn = 2 * layer
         norm(turn, layer, 0, layer == 1)
+        if layer == 0:
+            stores[1].wait()
+            fetching.advance()
+            fetching.advance()
         full = b.full.at[turn % 2]
         settle()
         save(full, o.mats.at[layer, 0], 3)
@@ -961,20 +1016,30 @@
             if part == 1:
                 fetching.need(3 * layer)
                 slots.load((WATTN, 1), o.foreign_weights.at[layer, 0])
+            calls = [layer == 0 and part == 1]
+
+            def steps(calls=calls):
+                if calls:
+                    skip = calls.pop()
+                    if skip:
+                        return
+                fetching.advance()
+
             attend_part(
-                layer == 0, full, slots.get((WATTN, part)), r.bias, b.acts.at[part], o.lse.at[layer, part]
+                layer == 0, full, slots.get((WATTN, part)), r.bias, b.acts.at[part], o.lse.at[layer, part], steps
             )
             save(b.acts.at[part], o.mats.at[layer, 1 + part], 4 + part)
             if part == 0:
                 slots.load((UP, 0), r.w_up.at[layer])
                 slots.load((DOWN, 0), r.w_down.at[layer])
-            fetching.advance()
         weights = [slots.get((WATTN, part)) for part in range(2)]
 
         def out_partial(span, weights=weights):
             cols = slice(3 * part_cols, None)
-            return mm_cols(b.acts[0, span, cols], weights[0][:, cols]) + mm_cols(
-                b.acts[1, span, cols], weights[1][:, cols]
+            first, second = b.acts[0, span, cols], b.acts[1, span, cols]
+            spans = [pl.ds(k * part_cols, part_cols) for k in range(4)]
+            return jnp.concatenate(
+                [mm(first, weights[0][s, cols]) + mm(second, weights[1][s, cols]) for s in spans], axis=1
             )
 
         scatter(turn, out_partial)
@@ -985,7 +1050,6 @@
         full = b.full.at[turn % 2]
         settle()
         save(full, o.mats.at[layer, 3], 3)
-        fetching.advance()
         for part in range(2):
             if part == 1:
                 fetching.need(3 * layer + 1)
@@ -1005,9 +1069,6 @@
             save(b.acts.at[part], o.mats.at[layer, 4 + part], 4 + part)
             save(b.slope.at[part], o.mats.at[layer, 6 + part], 6 + part)
             slots.drop((UP, part))
-            if part == 0 and layer == 0:
-                slots.load((WATTN, 0), r.w_attn.at[1])
-            fetching.advance()
         fetching.need(3 * layer + 2)
         slots.load((DOWN, 1), o.foreign_weights.at[layer, 2])
         downs = [slots.get((DOWN, part)) for part in range(2)]
@@ -1018,14 +1079,14 @@
         scatter(turn, down_partial)
         slots.drop((DOWN, 0), (DOWN, 1))
         if layer == 0:
-            fetching.advance()
+            slots.rename(PACK, (WATTN, 0))
+            grad_copy.start()
+            grad_own_copy.start()
 
     for j in range(2):
         span = pl.ds(j * block, block)
         total = b.state[span, :] + (b.keep[span, :] + b.rs_recv[1, span, :].astype(F32))
-        b.hidden[j] = total.astype(BF)
-    hidden_copy = remote(b.hidden.at[1 - chip], b.hidden_got, 18, chip_partner)
-    hidden_copy.start()
+        o.hidden[j] = total.astype(BF)
     grad_own_copy.wait()
     grad_copy.wait()
     o.grad_in[at(chip * block, block, block), :] = b.grad_own[...].astype(F32)
@@ -1034,15 +1095,14 @@
     settle()
     for copy in norm_copies:
         copy.wait()
-    hidden_copy.wait()
-    o.hidden_out[chip] = b.hidden[chip]
-    o.hidden_out[1 - chip] = b.hidden_got[...]
 
 
 class ForwardIn(NamedTuple):
     frames: Any
+    frames_got: Any
     out_grad: Any
-    w_attn: Any
+    w_qkv: Any
+    w_out: Any
     w_up: Any
     w_down: Any
     gains: Any
@@ -1055,9 +1115,10 @@
     norms: Any
     inverses: Any
     foreign_weights: Any
+    w_attn: Any
     lse: Any
     grad_in: Any
-    hidden_out: Any
+    hidden: Any
 
 
 class ForwardScratch(NamedTuple):
@@ -1075,10 +1136,9 @@
     frames_got: Any
     grad_own: Any
     grad_got: Any
-    hidden: Any
-    hidden_got: Any
     slot_sem: Any
     local_sem: Any
+    pack_sem: Any
     ex_send: Any
     ex_recv: Any
     send_sem: Any
@@ -1106,12 +1166,11 @@
         frames_got=rows,
         grad_own=rows,
         grad_got=rows,
-        hidden=pltpu.VMEM((2, block, width), BF),
-        hidden_got=rows,
         slot_sem=dma((5,)),
         local_sem=dma((8,)),
-        ex_send=dma((19,)),
-        ex_recv=dma((19,)),
+        pack_sem=dma((2, 8)),
+        ex_send=dma((17,)),
+        ex_recv=dma((17,)),
         send_sem=dma((3, 12, 2)),
         recv_sem=dma((3, 12, 2)),
     )
@@ -1120,16 +1179,17 @@
         norms=jax.ShapeDtypeStruct((2, 2, half, width), F32),
         inverses=jax.ShapeDtypeStruct((2, 2, half, LANES), F32),
         foreign_weights=jax.ShapeDtypeStruct((2, 3, length, width), BF),
+        w_attn=jax.ShapeDtypeStruct((2, length, width), BF),
         lse=jax.ShapeDtypeStruct((2, 2, width // (4 * LANES), 8, length), F32),
         grad_in=jax.ShapeDtypeStruct((half, width), F32),
-        hidden_out=jax.ShapeDtypeStruct((2, block, width), BF),
+        hidden=jax.ShapeDtypeStruct((2, block, width), BF),
     )
     any_spec = pl.BlockSpec(memory_space=pl.ANY)
     vmem_spec = pl.BlockSpec(memory_space=pltpu.VMEM)
     outs = pl.pallas_call(
         functools.partial(forward_kernel, bits),
-        in_specs=[any_spec] * 5 + [vmem_spec] * 3,
-        out_specs=[any_spec] * 4 + [vmem_spec] * 3,
+        in_specs=[any_spec] * 7 + [vmem_spec] * 3,
+        out_specs=[any_spec] * 5 + [vmem_spec] * 3,
         out_shape=list(out_shape),
         scratch_shapes=list(scratch),
         compiler_params=pltpu.CompilerParams(
@@ -1155,25 +1215,29 @@
     chosen = (jnp.arange(sections) == pick(codebook))[:, None, None]
     gains = jnp.concatenate([ln_gain, jnp.sum(jnp.where(chosen, ada_scale, 0.0), axis=0)])
     shifts = jnp.concatenate([ln_bias, jnp.sum(jnp.where(chosen, ada_shift, 0.0), axis=0)])
-    w_attn = jnp.concatenate(
-        [w_qkv.reshape(w_qkv.shape[0], w_qkv.shape[1], -1), w_out.transpose(0, 2, 1)], axis=2
-    )
+    pairs = [(i, i ^ 2) for i in range(lax.axis_size("tensor"))]
+    frames_got = lax.ppermute(jnp.where(chip == 0, frames[1], frames[0]), "tensor", pairs)
+    w_by_kind = w_qkv.transpose(0, 2, 1, 3)
     ahead = forward(
-        ForwardIn(frames, out_grad, w_attn, w_up, w_down, gains, shifts, bias[None, :]), size
+        ForwardIn(
+            frames, frames_got, out_grad, w_by_kind, w_out, w_up, w_down, gains, shifts, bias[None, :]
+        ),
+        size,
     )
     unit = jnp.eye(8, dtype=F32)
     sel = jnp.concatenate(
         [unit[0:3:2], unit[1:4:2]]
         + [jnp.where(chosen, rows[None], 0.0).reshape(2 * sections, 8) for rows in (unit[4:7:2], unit[5:8:2])]
     )
-    total, small, frames_grad = backward(
+    back = backward(
         BackIn(
+            ahead.hidden,
             ahead.grad_in,
             ahead.mats,
             ahead.norms,
             ahead.inverses,
             ahead.foreign_weights,
-            w_attn,
+            ahead.w_attn,
             w_up,
             w_down,
             gains,
@@ -1183,19 +1247,23 @@
         ),
         size,
     )
-    total = total.reshape((2, 3) + total.shape[1:])
-    wide = w_qkv.shape[2] * w_qkv.shape[3]
+    small = back.small_out
+    layers, part, width = w_out.shape
+    attn = back.attn.reshape(layers, width, width)
+    grad_qkv = jnp.stack([attn[:, :, i * part : (i + 1) * part].astype(F32) for i in range(3)], axis=1)
+    quarters = [back.attn[:, k, :, 3 * part :].astype(F32) for k in range(width // part)]
+    grad_out = jnp.concatenate(quarters, axis=2)
     return (
-        ahead.hidden_out,
-        frames_grad,
+        back.hidden_out,
+        back.frames_grad,
         small[0:2],
         small[2:4],
         small[4 : 4 + 2 * sections].reshape(ada_scale.shape),
         small[4 + 2 * sections :].reshape(ada_scale.shape),
-        total[::-1, 2, :, :wide].reshape(w_qkv.shape).astype(F32),
-        total[::-1, 2, :, wide:].transpose(0, 2, 1).astype(F32),
-        total[::-1, 1].astype(F32),
-        total[::-1, 0].astype(F32),
+        grad_qkv.transpose(0, 2, 1, 3),
+        grad_out.reshape(w_out.shape),
+        back.up.astype(F32).reshape(w_up.shape),
+        back.down.astype(F32).reshape(w_down.shape),
     )
 
 

time: 657 us -> 558 us (0.85)
  Pallas kernels: 585 us -> 507 us
  local copies, waits for them, and re-layouts: 35.7 us -> 15.1 us
    pallas_call x1, Pallas kernels: 396 us -> 354 us  [backward(): pl.pallas_call(functools.partial(back_kernel, bits), in_specs=[any_spec]...]
    pallas_call x1, Pallas kernels: 190 us -> 153 us  [forward(): pl.pallas_call(functools.partial(forward_kernel, bits), in_specs=[any_spe...]
    unnamed x14 -> x12, local copies, waits for them, and re-layouts: 20.7 us -> 4.03 us
    convert_element_type x3 -> x0, other arithmetic: 12.8 us -> none  [the longest x1 6.79 us: per_device(): total[::-1, 0].astype(F32)]
    reshape x0 -> x2, other arithmetic: none -> 9.45 us  [the longest x1 4.73 us: per_device(): back.up.astype(F32).reshape(w_up.shape)]
  transfers between devices with their start and end apart: 0 -> 1, of which waited for: 0 -> 1; matrix products, arithmetic and copies ran while one was open for 0% -> 1% of each run, Pallas kernels for 0% -> 0%
where the time goes in v3:
time: 558 us; the launch traced here: 551 us
  Pallas kernels  507 us (91%)
  other arithmetic  19.9 us (4%)
  local copies, waits for them, and re-layouts  15.1 us (3%)
    pallas_call x1, Pallas kernels, backward(): pl.pallas_call(functools.partial(back_kernel, bits), in_specs=[any_spec]...  354 us
    pallas_call x1, Pallas kernels, forward(): pl.pallas_call(functools.partial(forward_kernel, bits), in_specs=[any_spe...  153 us
  transfers between devices with their start and end apart: 1, of which 1 were waited for; matrix products, arithmetic and copies ran while one was open for 1% of the time, Pallas kernels for 0%

profile of v3, /device:TPU:0, one launch (start us, length us, event | category | flops | bytes accessed | tf_op | source)
XLA Modules:
  0.0 550.9 jit_solution(6464983931891038804)
XLA Ops:
  0.7 1.3 select_bitcast_fusion
  1.9 3.0 collective-permute-start
  5.0 1.3 fusion.4
  6.3 1.3 fusion.5
  8.9 0.1 broadcast_in_dim.74
  9.0 0.1 broadcast_in_dim.75
  10.4 0.1 broadcast_select_fusion.1
  10.5 0.6 compare_select_fusion.refs_9_
  11.2 0.6 pad_maximum_fusion.2.refs_10_
  11.8 1.0 select_reduce_fusion
  12.8 1.3 pad_maximum_fusion
  14.1 0.8 fusion.refs_11_
  14.9 1.9 collective-permute-done.refs_1_
  16.9 0.8 copy-done.4
  17.7 152.9 %forward.1 = (bf16[2,8,1024,1024]{3,2,1,0:T(8,128)(2,1)}, f32[2,2,512,1024]{3,2,1,0:T(8,128)}, f32[2,2,512,128]{3,2,1,0:T(8,128)}, bf16[2,3,1024,1024]{3,2,1,0:T...) custom-call(bf16[2,256,1024]{2,1,0:T(8,128)(2,1)} %refs_0_.1, ...), custom_call_target="tpu_custom_call" | custom-call | tf_op jit(solution)/shard_map/forward/pallas_call | solution.py:1189
  170.6 354.5 %backward.1 = (bf16[2,4,256,1024]{3,2,1,0:T(8,128)(2,1)}, bf16[2,4,256,1024]{3,2,1,0:T(8,128)(2,1)}, bf16[2,4,256,1024]{3,2,1,0:T(8,128)(2,1)}, bf16[24,256,1024...) custom-call(bf16[2,256,1024]{2,1,0:T(8,128)(2,1)} %get-tuple-element, ...), custom_call_target="tpu_custom_call" | custom-call | tf_op jit(solution)/shard_map/backward/pallas_call | solution.py:755
  525.0 1.4 fusion.3
  526.5 1.0 fusion.2
  527.5 1.0 slice_bitcast_fusion.6
  528.5 1.2 slice_bitcast_fusion.5
  529.6 0.7 reshape.84
  530.3 0.7 reshape.83
  531.0 2.2 slice_bitcast_fusion.2
  533.2 0.9 copy-done.1
  534.2 4.7 bitcast_convert_fusion.1
  538.9 0.0 copy-done
  538.9 4.7 bitcast_convert_fusion
  543.6 3.2 convert_bitcast_fusion
  546.8 1.6 maximum_convert_fusion
  548.4 0.0 copy-done.3
  548.4 1.0 copy.51
  549.3 1.3 copy.52
  (16 shorter events, 0.1 us)
Async XLA Ops:
  1.9 15.0 %collective-permute-start = (bf16[256,1024]{1,0:T(8,128)(2,1)S(1)}, bf16[256,1024]{1,0:T(8,128)(2,1)S(1)}, u32[]{:S(2)}, u32[]{:S(2)}) collective-permute-start(bf16[256,1024]{1,0:T(8,128)(2,1)S(1)} %select_bitcast_fusion), channel_id=1, source_target_pairs={{0,2},{1,3},{2,0},{3,1},{4,6},{5,7},{6,4},{7,5},{8,10},{9,11},{10,... | collective-permute-start | bytes 1572872 | tf_op jit(solution)/shard_map/ppermute | solution.py:1219
  16.9 0.8 copy-start.4
  531.0 3.2 copy-start.1
  534.1 4.7 copy-start
  543.6 4.8 copy-start.3
  546.8 2.6 copy-start.2

commit v4 on v3

--- a/solution.py
+++ b/solution.py
@@ -50,18 +50,33 @@
     return bits
 
 
-def attend_part(causal, n_ref, w_ref, bias_ref, qkva_ref, lse_ref, between):
+def own_rows_first(body, arrive):
+    core = lax.rem(lax.axis_index("tensor"), 2)
+
+    def own_body(j, _):
+        body(2 * j + core)
+        return 0
+
+    def other_body(j, _):
+        body(2 * j + 1 - core)
+        return 0
+
+    lax.fori_loop(0, 2, own_body, 0)
+    arrive()
+    lax.fori_loop(0, 2, other_body, 0)
+
+
+def attend_part(causal, n_ref, w_ref, bias_ref, qkva_ref, lse_ref, arrive, between):
     length = n_ref.shape[0]
     part = qkva_ref.shape[1] // 4
     block = length // 4
     scaling = HEAD_DIM ** (-0.5)
 
-    def project(index, _):
+    def project(index):
         rows = at(index * block, block, block)
         qkva_ref[rows, : 3 * part] = mm(n_ref[rows, :], w_ref[:, : 3 * part]).astype(BF)
-        return 0
-
-    lax.fori_loop(0, 4, project, 0)
+
+    own_rows_first(project, arrive)
 
     for pair in range(part // LANES):
         q_cols, k_cols, v_cols, a_cols = [pl.ds(i * part + pair * LANES, LANES) for i in range(4)]
@@ -354,6 +369,10 @@
     per_matrix = length // summing.rows
     vec = b.vec
     vec[...] = jnp.zeros_like(vec)
+    section = r.codebook[chip]
+    choose_maps(b.gains, r.ln_gain, r.ada_scale, section)
+    key_at = lax.broadcasted_iota(jnp.int32, (length, 1), 0)
+    b.bias[...] = jnp.where(key_at < r.lengths[chip], 0.0, -1e30).astype(F32)
 
     def remote(source, target, sem, device):
         return pltpu.make_async_remote_copy(
@@ -404,7 +423,7 @@
         normed_copy.wait()
         inverse_copy.wait()
         index = 4 * layer + 2 * which
-        gain = r.gains[2 * layer + which : 2 * layer + which + 1, :]
+        gain = b.gains[2 * layer + which : 2 * layer + which + 1, :]
         step = 128
 
         def rows_body(i, _):
@@ -558,7 +577,7 @@
                 b.grad_att,
                 qkva,
                 lambda pair, rows, part=part, lse_ref=lse_ref: lse_ref[part, pair, :, rows],
-                r.bias,
+                b.bias,
                 dqkv,
                 b.dk,
                 b.dv,
@@ -603,10 +622,16 @@
     b.rows_send[...] = b.state[other, :].astype(BF)
     rows_copy = remote(b.rows_send, b.rows_recv, 16, {"tensor": flip(tensor, 2)})
     rows_copy.start()
-    small = jnp.zeros(r.sel.shape[:1] + (width,), F32)
-    for i in range(8):
-        small = small + r.sel[:, i : i + 1] * vec[i : i + 1, :]
-    b.small_buf[0, 0] = small
+    sections = r.ada_scale.shape[0]
+    for k in range(2):
+        b.small_buf[0, 0, k : k + 1, :] = vec[2 * k : 2 * k + 1, :]
+        b.small_buf[0, 0, 2 + k : 3 + k, :] = vec[2 * k + 1 : 2 * k + 2, :]
+        for index in range(sections):
+            chosen = jnp.where(section == index, 1.0, 0.0).astype(F32)
+            for which in range(2):
+                row = 4 + 2 * sections * which + 2 * index + k
+                source = 4 + 2 * k + which
+                b.small_buf[0, 0, row : row + 1, :] = vec[source : source + 1, :] * chosen
 
     def small_copy(i):
         return pltpu.make_async_remote_copy(
@@ -627,7 +652,13 @@
             b.small_buf[0, i + 1] = total
             small_copy(i + 1).start()
         else:
-            o.small_out[...] = total
+            o.gain_out[...] = total[0:2]
+            o.bias_out[...] = total[2:4]
+            for index in range(sections):
+                row = 4 + 2 * index
+                o.scale_out[index] = total[row : row + 2]
+                row += 2 * sections
+                o.shift_out[index] = total[row : row + 2]
     rows_copy.wait()
     hidden_copy.wait()
     hidden_own_copy.wait()
@@ -649,9 +680,10 @@
     w_attn: Any
     w_up: Any
     w_down: Any
-    gains: Any
-    sel: Any
-    bias: Any
+    lengths: Any
+    codebook: Any
+    ln_gain: Any
+    ada_scale: Any
     lse: Any
 
 
@@ -662,11 +694,16 @@
     own: Any
     foreign: Any
     hidden_out: Any
-    small_out: Any
     frames_grad: Any
+    gain_out: Any
+    bias_out: Any
+    scale_out: Any
+    shift_out: Any
 
 
 class BackScratch(NamedTuple):
+    gains: Any
+    bias: Any
     slots: Any
     dpre: Any
     full: Any
@@ -711,11 +748,14 @@
     stages = 2 * len(bits) + 1
     ring = min(chunks, max(2 * Summing.AHEAD + len(bits), 2 * len(bits)) + 1)
     steps = halvings(bits, rows, width)
-    small_rows = inputs.sel.shape[0]
+    sections = inputs.ada_scale.shape[0]
+    small_rows = 4 + 4 * sections
     exchanges = len(bits) + 2
     whole = jax.ShapeDtypeStruct((chunks, rows, width), BF)
     dma = pltpu.SemaphoreType.DMA
     shapes = BackScratch(
+        gains=pltpu.VMEM((4, width), F32),
+        bias=pltpu.VMEM((length, 1), F32),
         slots=pltpu.VMEM((5, length, width), BF),
         dpre=pltpu.VMEM((2, length, width), BF),
         full=pltpu.VMEM((2, length, width), BF),
@@ -752,16 +792,20 @@
     scratch += [pltpu.VMEM((ring,) + step[:2], BF) for step in steps]
     any_spec = pl.BlockSpec(memory_space=pl.ANY)
     vmem_spec = pl.BlockSpec(memory_space=pltpu.VMEM)
+    smem_spec = pl.BlockSpec(memory_space=pltpu.SMEM)
     outs = pl.pallas_call(
         functools.partial(back_kernel, bits),
-        in_specs=[any_spec] * 9 + [vmem_spec] * 4,
-        out_specs=[any_spec] * 6 + [vmem_spec] * 2,
+        in_specs=[any_spec] * 9 + [smem_spec] * 2 + [vmem_spec] * 3,
+        out_specs=[any_spec] * 6 + [vmem_spec] * 5,
         out_shape=[jax.ShapeDtypeStruct((2, length // rows, rows, width), BF)] * 3
         + [whole] * 2
         + [
             jax.ShapeDtypeStruct((2, block, width), BF),
-            jax.ShapeDtypeStruct((small_rows, width), F32),
             jax.ShapeDtypeStruct((2, block, width), F32),
+            jax.ShapeDtypeStruct((2, width), F32),
+            jax.ShapeDtypeStruct((2, width), F32),
+            jax.ShapeDtypeStruct((sections, 2, width), F32),
+            jax.ShapeDtypeStruct((sections, 2, width), F32),
         ],
         scratch_shapes=scratch,
         compiler_params=pltpu.CompilerParams(
@@ -772,6 +816,14 @@
     return BackOut(*outs)
 
 
+def choose_maps(target, shared, adaptive, section):
+    target[0:2, :] = shared[...]
+    chosen = jnp.zeros_like(shared[...])
+    for index in range(adaptive.shape[0]):
+        chosen = jnp.where(section == index, adaptive[index], chosen)
+    target[2:4, :] = chosen
+
+
 class Fetching:
     SKEW = 2
     STAGES = 3
@@ -781,9 +833,20 @@
         self.send_sem, self.recv_sem = send_sem, recv_sem
         self.dp = lax.axis_index("dp")
         self.tensor = lax.axis_index("tensor")
-        self.half = sources[0].shape[0] // 2
+        self.unit = sources[0].shape[0] // 16
         self.items = 2 * len(sources)
         self.step = 0
+
+    def remote(self, stage, item, sub, rows, device):
+        target = self.targets[item // 2].at[rows]
+        return pltpu.make_async_remote_copy(
+            src_ref=self.sources[item // 2].at[rows] if stage == 0 else target,
+            dst_ref=target,
+            send_sem=self.send_sem.at[stage, item, sub],
+            recv_sem=self.recv_sem.at[stage, item, sub],
+            device_id=device,
+            device_id_type=MESH,
+        )
 
     def copies(self, stage, item):
         pieces = []
@@ -791,29 +854,17 @@
             first_bit = 1 + sub
             low = lax.rem(self.dp // first_bit, 2)
             high = lax.rem(self.dp // (3 - first_bit), 2)
-            span = self.half // 2
-            base = (item % 2) * self.half + sub * span
-            quarter = span // 4
+            base = (8 * (item % 2) + 4 * sub) * self.unit
+            quarter = self.unit
             if stage < 2:
-                rows = at(base + (2 * high + low) * quarter, quarter, quarter)
+                rows = at(base + (2 * high + low) * quarter, quarter, 16)
             else:
-                rows = at(base + high * 2 * quarter, 2 * quarter, 2 * quarter)
-            target = self.targets[item // 2].at[rows]
-            source = self.sources[item // 2].at[rows] if stage == 0 else target
+                rows = at(base + high * 2 * quarter, 2 * quarter, 16)
             if stage == 0:
                 device = {"tensor": flip(self.tensor, 2)}
             else:
                 device = {"dp": flip(self.dp, first_bit if stage == 1 else 3 - first_bit)}
-            pieces.append(
-                pltpu.make_async_remote_copy(
-                    src_ref=source,
-                    dst_ref=target,
-                    send_sem=self.send_sem.at[stage, item, sub],
-                    recv_sem=self.recv_sem.at[stage, item, sub],
-                    device_id=device,
-                    device_id_type=MESH,
-                )
-            )
+            pieces.append(self.remote(stage, item, sub, rows, device))
         return pieces
 
     def advance(self):
@@ -877,7 +928,7 @@
     def local(source, target, sem):
         return pltpu.make_async_copy(source, target, b.local_sem.at[sem])
 
-    frames_copy = local(r.frames_got, b.frames_got, 3)
+    frames_copy = remote(r.frames.at[1 - chip], b.frames_got, 17, chip_partner)
     frames_copy.start()
     own_copy = local(r.frames.at[chip], b.frames_own, 0)
     own_copy.start()
@@ -896,6 +947,10 @@
             for i, (source, target) in enumerate(pairs)
         ]
 
+    choose_maps(b.gains, r.ln_gain, r.ada_scale, r.codebook[chip])
+    choose_maps(b.shifts, r.ln_bias, r.ada_shift, r.codebook[chip])
+    key_at = lax.broadcasted_iota(jnp.int32, (1, length), 1)
+    b.bias[...] = jnp.where(key_at < r.lengths[chip], 0.0, -1e30).astype(F32)
     pack_slots = [slots.reserve((WATTN, 0)), slots.reserve(PACK)]
     packs = [pack_copies(layer, slot) for layer, slot in enumerate(pack_slots)]
     stores = [
@@ -915,12 +970,13 @@
         targets += [o.foreign_weights.at[layer, i] for i in range(3)]
     fetching = Fetching(sources, targets, b.send_sem, b.recv_sem)
     fetching.advance()
-    fetching.advance()
     for copy in packs[1]:
         copy.wait()
     stores[1].start()
     own_copy.wait()
     frames_copy.wait()
+    fetching.advance()
+    fetching.advance()
     b.state[at(chip * block, block, block), :] = b.frames_own[...].astype(F32)
     b.state[at((1 - chip) * block, block, block), :] = b.frames_got[...].astype(F32)
     grad_copy = remote(r.out_grad.at[1 - chip], b.grad_got, 16, chip_partner)
@@ -951,14 +1007,26 @@
         for copy in copies:
             copy.wait()
 
+    saves = []
+
+    def save(source, target, sem):
+        copy = local(source, target, sem)
+        copy.start()
+        saves.append(copy)
+
+    def settle():
+        for copy in saves:
+            copy.wait()
+        saves.clear()
+
     norm_copies = []
 
     def norm(turn, layer, which, add):
         for copy in norm_copies:
             copy.wait()
         norm_copies.clear()
-        gain = r.gains[2 * layer + which : 2 * layer + which + 1, :]
-        shift = r.shifts[2 * layer + which : 2 * layer + which + 1, :]
+        gain = b.gains[2 * layer + which : 2 * layer + which + 1, :]
+        shift = b.shifts[2 * layer + which : 2 * layer + which + 1, :]
         step = 128
         copies = exchange_copies(turn)
         for j in range(2):
@@ -986,47 +1054,38 @@
         norm_copies.append(local(b.inverse, o.inverses.at[layer, which], 2))
         for copy in norm_copies:
             copy.start()
-        for copy in copies:
-            copy.wait()
-
-    saves = []
-
-    def save(source, target, sem):
-        copy = local(source, target, sem)
-        copy.start()
-        saves.append(copy)
-
-    def settle():
-        for copy in saves:
-            copy.wait()
-        saves.clear()
+
+        def arrive(copies=copies):
+            for copy in copies:
+                copy.wait()
+            save(b.full.at[turn % 2], o.mats.at[layer, 3 * which], 3)
+
+        return arrive
 
     for layer in range(2):
         turn = 2 * layer
-        norm(turn, layer, 0, layer == 1)
+        arrive = norm(turn, layer, 0, layer == 1)
         if layer == 0:
             stores[1].wait()
             fetching.advance()
-            fetching.advance()
         full = b.full.at[turn % 2]
         settle()
-        save(full, o.mats.at[layer, 0], 3)
         fetching.advance()
         for part in range(2):
             if part == 1:
                 fetching.need(3 * layer)
                 slots.load((WATTN, 1), o.foreign_weights.at[layer, 0])
-            calls = [layer == 0 and part == 1]
-
-            def steps(calls=calls):
-                if calls:
-                    skip = calls.pop()
-                    if skip:
-                        return
-                fetching.advance()
+            quiet = [] if layer == 0 and part == 0 else [None]
+
+            def steps(quiet=quiet):
+                if quiet:
+                    quiet.pop()
+                else:
+                    fetching.advance()
 
             attend_part(
-                layer == 0, full, slots.get((WATTN, part)), r.bias, b.acts.at[part], o.lse.at[layer, part], steps
+                layer == 0, full, slots.get((WATTN, part)), b.bias, b.acts.at[part], o.lse.at[layer, part],
+                arrive if part == 0 else lambda: None, steps,
             )
             save(b.acts.at[part], o.mats.at[layer, 1 + part], 4 + part)
             if part == 0:
@@ -1046,29 +1105,33 @@
         slots.drop((WATTN, 0), (WATTN, 1))
         fetching.advance()
         turn += 1
-        norm(turn, layer, 1, True)
+        if layer == 1:
+            grad_copy.start()
+            grad_own_copy.start()
+        arrive = norm(turn, layer, 1, True)
         full = b.full.at[turn % 2]
         settle()
-        save(full, o.mats.at[layer, 3], 3)
+        fetching.advance()
         for part in range(2):
             if part == 1:
                 fetching.need(3 * layer + 1)
                 slots.load((UP, 1), o.foreign_weights.at[layer, 1])
             up = slots.get((UP, part))
 
-            def up_body(i, _, part=part, up=up, full=full):
-                rows = at(i * 256, 256, 256)
+            def up_body(i, part=part, up=up, full=full):
+                rows = at(i * block, block, block)
                 for first in range(0, width, 256):
                     cols = pl.ds(first, 256)
                     active, slope = gelu_parts(mm(full[rows, :], up[:, cols]))
                     b.acts[part, rows, cols] = active.astype(BF)
                     b.slope[part, rows, cols] = slope.astype(BF)
-                return 0
-
-            lax.fori_loop(0, length // 256, up_body, 0)
+
+            own_rows_first(up_body, arrive if part == 0 else lambda: None)
             save(b.acts.at[part], o.mats.at[layer, 4 + part], 4 + part)
             save(b.slope.at[part], o.mats.at[layer, 6 + part], 6 + part)
             slots.drop((UP, part))
+            if layer == 1 and part == 0:
+                fetching.advance()
         fetching.need(3 * layer + 2)
         slots.load((DOWN, 1), o.foreign_weights.at[layer, 2])
         downs = [slots.get((DOWN, part)) for part in range(2)]
@@ -1080,8 +1143,6 @@
         slots.drop((DOWN, 0), (DOWN, 1))
         if layer == 0:
             slots.rename(PACK, (WATTN, 0))
-            grad_copy.start()
-            grad_own_copy.start()
 
     for j in range(2):
         span = pl.ds(j * block, block)
@@ -1099,15 +1160,17 @@
 
 class ForwardIn(NamedTuple):
     frames: Any
-    frames_got: Any
     out_grad: Any
     w_qkv: Any
     w_out: Any
     w_up: Any
     w_down: Any
-    gains: Any
-    shifts: Any
-    bias: Any
+    lengths: Any
+    codebook: Any
+    ln_gain: Any
+    ln_bias: Any
+    ada_scale: Any
+    ada_shift: Any
 
 
 class ForwardOut(NamedTuple):
@@ -1122,6 +1185,9 @@
 
 
 class ForwardScratch(NamedTuple):
+    gains: Any
+    shifts: Any
+    bias: Any
     slots: Any
     acts: Any
     slope: Any
@@ -1152,6 +1218,9 @@
     dma = pltpu.SemaphoreType.DMA
     rows = pltpu.VMEM((block, width), BF)
     scratch = ForwardScratch(
+        gains=pltpu.VMEM((4, width), F32),
+        shifts=pltpu.VMEM((4, width), F32),
+        bias=pltpu.VMEM((1, length), F32),
         slots=pltpu.VMEM((5, length, width), BF),
         acts=pltpu.VMEM((2, length, width), BF),
         slope=pltpu.VMEM((2, length, width), BF),
@@ -1169,8 +1238,8 @@
         slot_sem=dma((5,)),
         local_sem=dma((8,)),
         pack_sem=dma((2, 8)),
-        ex_send=dma((17,)),
-        ex_recv=dma((17,)),
+        ex_send=dma((18,)),
+        ex_recv=dma((18,)),
         send_sem=dma((3, 12, 2)),
         recv_sem=dma((3, 12, 2)),
     )
@@ -1186,9 +1255,10 @@
     )
     any_spec = pl.BlockSpec(memory_space=pl.ANY)
     vmem_spec = pl.BlockSpec(memory_space=pltpu.VMEM)
+    smem_spec = pl.BlockSpec(memory_space=pltpu.SMEM)
     outs = pl.pallas_call(
         functools.partial(forward_kernel, bits),
-        in_specs=[any_spec] * 7 + [vmem_spec] * 3,
+        in_specs=[any_spec] * 6 + [smem_spec] * 2 + [vmem_spec] * 4,
         out_specs=[any_spec] * 5 + [vmem_spec] * 3,
         out_shape=list(out_shape),
         scratch_shapes=list(scratch),
@@ -1203,31 +1273,23 @@
 def per_device(
     frames, lengths, codebook, ln_gain, ln_bias, ada_scale, ada_shift, w_qkv, w_out, w_up, w_down, out_grad
 ):
-    chip = lax.axis_index("tensor") // 2
-    length = frames.shape[1] * lax.axis_size("tensor")
     size = lax.axis_size("dp")
-
-    def pick(pair):
-        return jnp.where(chip == 0, pair[0], pair[1])
-
-    bias = jnp.where(jnp.arange(length) < pick(lengths), 0.0, -1e30).astype(F32)
-    sections = ada_scale.shape[0]
-    chosen = (jnp.arange(sections) == pick(codebook))[:, None, None]
-    gains = jnp.concatenate([ln_gain, jnp.sum(jnp.where(chosen, ada_scale, 0.0), axis=0)])
-    shifts = jnp.concatenate([ln_bias, jnp.sum(jnp.where(chosen, ada_shift, 0.0), axis=0)])
-    pairs = [(i, i ^ 2) for i in range(lax.axis_size("tensor"))]
-    frames_got = lax.ppermute(jnp.where(chip == 0, frames[1], frames[0]), "tensor", pairs)
-    w_by_kind = w_qkv.transpose(0, 2, 1, 3)
     ahead = forward(
         ForwardIn(
-            frames, frames_got, out_grad, w_by_kind, w_out, w_up, w_down, gains, shifts, bias[None, :]
+            frames,
+            out_grad,
+            w_qkv.transpose(0, 2, 1, 3),
+            w_out,
+            w_up,
+            w_down,
+            lengths,
+            codebook,
+            ln_gain,
+            ln_bias,
+            ada_scale,
+            ada_shift,
         ),
         size,
-    )
-    unit = jnp.eye(8, dtype=F32)
-    sel = jnp.concatenate(
-        [unit[0:3:2], unit[1:4:2]]
-        + [jnp.where(chosen, rows[None], 0.0).reshape(2 * sections, 8) for rows in (unit[4:7:2], unit[5:8:2])]
     )
     back = backward(
         BackIn(
@@ -1240,14 +1302,14 @@
             ahead.w_attn,
             w_up,
             w_down,
-            gains,
-            sel,
-            bias[:, None],
+            lengths,
+            codebook,
+            ln_gain,
+            ada_scale,
             ahead.lse,
         ),
         size,
     )
-    small = back.small_out
     layers, part, width = w_out.shape
     attn = back.attn.reshape(layers, width, width)
     grad_qkv = jnp.stack([attn[:, :, i * part : (i + 1) * part].astype(F32) for i in range(3)], axis=1)
@@ -1256,10 +1318,10 @@
     return (
         back.hidden_out,
         back.frames_grad,
-        small[0:2],
-        small[2:4],
-        small[4 : 4 + 2 * sections].reshape(ada_scale.shape),
-        small[4 + 2 * sections :].reshape(ada_scale.shape),
+        back.gain_out,
+        back.bias_out,
+        back.scale_out,
+        back.shift_out,
         grad_qkv.transpose(0, 2, 1, 3),
         grad_out.reshape(w_out.shape),
         back.up.astype(F32).reshape(w_up.shape),

time: 558 us -> 553 us (level)
  Pallas kernels: 507 us -> 520 us
  local copies, waits for them, and re-layouts: 15.1 us -> 9.38 us
    pallas_call x1, Pallas kernels: 153 us -> 165 us  [forward(): pl.pallas_call(functools.partial(forward_kernel, bits), in_specs=[any_spe...]
    reshape x1, other arithmetic: 4.72 us -> 10.9 us  [per_device(): back.down.astype(F32).reshape(w_down.shape)]
  transfers between devices with their start and end apart: 1 -> 0, of which waited for: 1 -> 0; matrix products, arithmetic and copies ran while one was open for 1% -> 0% of each run, Pallas kernels for 0% -> 0%
where the time goes in v4:
time: 553 us; the launch traced here: 546 us
  Pallas kernels  520 us (94%)
  other arithmetic  16 us (3%)
  local copies, waits for them, and re-layouts  9.38 us (2%)
    pallas_call x1, Pallas kernels, backward(): pl.pallas_call(functools.partial(back_kernel, bits), in_specs=[any_spec]...  354 us
    pallas_call x1, Pallas kernels, forward(): pl.pallas_call(functools.partial(forward_kernel, bits), in_specs=[any_spe...  165 us

profile of v4, /device:TPU:0, one launch (start us, length us, event | category | flops | bytes accessed | tf_op | source)
XLA Modules:
  0.0 546.0 jit_solution(4887539043636660138)
XLA Ops:
  0.6 165.2 %forward.1 = (bf16[2,8,1024,1024]{3,2,1,0:T(8,128)(2,1)}, f32[2,2,512,1024]{3,2,1,0:T(8,128)}, f32[2,2,512,128]{3,2,1,0:T(8,128)}, bf16[2,3,1024,1024]{3,2,1,0:T...) custom-call(bf16[2,256,1024]{2,1,0:T(8,128)(2,1)} %refs_0_.1, ...), custom_call_target="tpu_custom_call" | custom-call | tf_op jit(solution)/shard_map/forward/pallas_call | solution.py:1259
  165.9 354.5 %backward.1 = (bf16[2,4,256,1024]{3,2,1,0:T(8,128)(2,1)}, bf16[2,4,256,1024]{3,2,1,0:T(8,128)(2,1)}, bf16[2,4,256,1024]{3,2,1,0:T(8,128)(2,1)}, bf16[24,256,1024...) custom-call(bf16[2,256,1024]{2,1,0:T(8,128)(2,1)} %get-tuple-element, ...), custom_call_target="tpu_custom_call" | custom-call | tf_op jit(solution)/shard_map/backward/pallas_call | solution.py:796
  520.4 0.0 copy-start
  520.4 1.1 slice_bitcast_fusion.6
  521.5 1.4 slice_bitcast_fusion.5
  522.9 1.6 maximum_convert_fusion
  524.5 0.0 copy-done
  524.5 0.2 slice_bitcast_fusion.2
  524.7 0.0 copy-start.1
  524.7 3.5 convert_bitcast_fusion
  528.2 0.6 copy-done.1
  528.8 0.0 copy-start.2
  528.8 10.9 %bitcast_convert_fusion = (f32[2,1024,1024]{2,1,0:T(8,128)}, f32[2,1024,1024]{2,1,0:T(8,128)}) fusion(bf16[2,4,256,1024]{3,2,1,0:T(8,128)(2,1)S(1)} %copy-done.1, bf16[2,4,256,1024]{3,2,1,0:T(8,128)(2,1)} %get-tuple-element.42), kind=kLoop, calls=%fused_computation.1 | loop fusion | flops 4194304 | bytes 25165824 | tf_op jit(solution)/shard_map/reshape | solution.py:1328
  539.7 0.0 copy-start.6
  539.7 0.0 copy-start.5
  539.7 0.0 copy-start.4
  539.7 0.0 copy-start.3
  539.7 2.3 copy.35
  542.0 0.0 copy-done.2
  542.0 1.3 copy.36
  543.3 0.0 copy-done.6
  543.3 0.6 copy.37
  543.9 0.0 copy-done.5
  543.9 0.6 copy.38
  544.5 0.0 copy-done.4
  544.5 0.6 copy.39
  545.1 0.0 copy-done.3
  545.1 0.6 copy.40
Async XLA Ops:
  520.4 4.1 copy-start
  524.7 4.1 copy-start.1
  528.8 13.2 %copy-start.2 = (f32[2,256,1024]{2,1,0:T(8,128)S(1)}, f32[2,256,1024]{2,1,0:T(8,128)}, u32[]{:S(2)}) copy-start(f32[2,256,1024]{2,1,0:T(8,128)} %get-tuple-element.63) | copy-start | bytes 6291460
  539.7 3.6 copy-start.6
  539.7 4.2 copy-start.5
  539.7 4.8 copy-start.4
  539.7 5.5 %copy-start.3 = (f32[7,2,1024]{2,1,0:T(2,128)S(1)}, f32[7,2,1024]{2,1,0:T(2,128)}, u32[]{:S(2)}) copy-start(f32[7,2,1024]{2,1,0:T(2,128)} %get-tuple-element.67) | copy-start | bytes 172036
